TPU v7x, 768 devices: a whole 4x8x12 slice. The times are simulated.
768 devices in a mesh: rep: 12 (over z), shard: 64 (over x, y, core).
Axes of the slice: x: 4, y: 8, z: 12, core: 2. Of those that a mesh axis runs over, the one named last changes fastest.
Arguments:
- grad_parts: bfloat16 [12, 96, 256, 3584], P('rep', None, 'shard'), may hold values from -6 to 6
- momentum: float32 [96, 256, 3584], P('rep', 'shard'), may hold values from -131 to 131
- mask_codes: int32 [96, 256, 896], P('rep', 'shard'), may hold values from 0 to 5
Outputs:
- momentum_next: float32 [96, 256, 3584], P('rep', 'shard')
- update: bfloat16 [96, 256, 3584], P('rep', 'shard')
All inputs are finite; a program needn't handle non-finite values.
Results may differ from a plain program's by a relative error of at most 0.02.
Values may be sent and summed in bfloat16 or wider, within the bound.
No kernel may reach another device: no remote copies, remote signals or barrier semaphores. Data moves between devices by JAX's collectives and lax.ppermute only.
A program may use at most 64 MiB of HBM per device.

v0:
```python
import jax
import jax.numpy as jnp
from jax import lax
from jax.sharding import PartitionSpec as P

ITERS = 5


DECAY_RATE = 0.95
EPSILON = 1e-07
QUINTIC_FIRST = 3.4445
QUINTIC_SECOND = -4.775
QUINTIC_THIRD = 2.0315
UPDATE_SCALE = 64.0


def keep_columns(code_array):
    holders = ((0, 1, 2), (0, 3, 4), (1, 3, 5), (2, 4, 5))
    parts = []
    for codes_here in holders:
        hit = (
            (code_array == codes_here[0])
            | (code_array == codes_here[1])
            | (code_array == codes_here[2])
        )
        parts.append(hit.astype(jnp.float32))
    stacked = jnp.stack(parts, axis=-1)
    return stacked.reshape(code_array.shape[:-1] + (code_array.shape[-1] * 4,))


def coefficients(gram_matrix):
    row_total = gram_matrix.shape[0]
    trace_sum = jnp.trace(gram_matrix)
    inverse = lax.rsqrt(trace_sum + EPSILON)
    scaled = gram_matrix * (inverse * inverse)
    identity = jnp.eye(row_total, dtype=jnp.float32)
    factor_now = identity
    for iteration in range(ITERS):
        product = jnp.dot(factor_now, scaled, precision=lax.Precision.HIGHEST)
        square_form = jnp.dot(product, factor_now.T, precision=lax.Precision.HIGHEST)
        polynomial = (
            QUINTIC_FIRST * identity
            + QUINTIC_SECOND * square_form
            + QUINTIC_THIRD * jnp.dot(square_form, square_form, precision=lax.Precision.HIGHEST)
        )
        factor_now = jnp.dot(polynomial, factor_now, precision=lax.Precision.HIGHEST)
    return (factor_now * inverse).astype(jnp.bfloat16)


def local(grad_parts, momentum, mask_codes):
    shards = lax.axis_size("shard")
    group_size = momentum.shape[0]
    piece_rows = momentum.shape[1]
    col_total = momentum.shape[2]
    spacing = shards // group_size
    summed = lax.psum_scatter(
        grad_parts[0].astype(jnp.float32).astype(jnp.bfloat16),
        "rep",
        scatter_dimension=0,
        tiled=True,
    ).astype(jnp.float32)
    momentum_next = DECAY_RATE * momentum + summed
    inputs_bf = momentum_next.astype(jnp.bfloat16)
    kept_mask = keep_columns(mask_codes)
    slot_buffer = jnp.zeros((group_size, spacing, piece_rows, col_total), jnp.bfloat16)
    slot_buffer = slot_buffer.at[:, 0].set(inputs_bf)
    outgoing = slot_buffer.reshape(shards * piece_rows, col_total)
    gathered = lax.all_to_all(outgoing, "shard", split_axis=0, concat_axis=0, tiled=True)
    gram_matrix = lax.dot_general(
        gathered, gathered, (((1,), (1,)), ((), ())), preferred_element_type=jnp.float32
    )
    coef = coefficients(gram_matrix)
    orthogonal = jnp.dot(coef, gathered, preferred_element_type=jnp.float32).astype(jnp.bfloat16)
    returned = lax.all_to_all(orthogonal, "shard", split_axis=0, concat_axis=0, tiled=True)
    returned = returned.reshape(group_size, spacing, piece_rows, col_total)[:, 0]
    update = (UPDATE_SCALE * kept_mask * returned.astype(jnp.float32)).astype(jnp.bfloat16)
    return (momentum_next, update)


def solution(mesh):
    in_specs = (P("rep", None, "shard", None), P("rep", "shard", None), P("rep", "shard", None))
    out_specs = (P("rep", "shard", None), P("rep", "shard", None))
    return jax.shard_map(local, mesh=mesh, in_specs=in_specs, out_specs=out_specs, check_vma=False)
```

profile of v0, /device:TPU:1, one launch (start us, length us, event | category | flops | bytes accessed | tf_op | source)
XLA Modules:
  0.0 229.4 jit_solution(4292325005993765336)
XLA Ops:
  7.2 0.0 reduce-scatter.4.cloned.1.call-start
  7.2 2.2 copy.43
  9.4 1.8 copy.37
  11.3 0.0 copy-start.2
  11.3 0.0 reduce-scatter.4.cloned.1.call-update
  11.3 64.7 %reduce-scatter.4.cloned.1.call-done = bf16[8,14336]{1,0:T(8,128)(2,1)} async-done(((bf16[96,14336]{1,0:T(8,128)(2,1)}), bf16[8,14336]{1,0:T(8,128)(2,1)}) %reduce-scatter.4.cloned.1.call-update) | async-done | bytes 229392
  76.0 0.0 copy-done.2
  76.0 1.1 convert_bitcast_fusion
  77.1 0.4 copy.36
  77.5 0.4 pad_bitcast_fusion
  77.9 1.4 copy.26
  79.3 62.4 %all_to_all.21 = bf16[64,4,3584]{2,1,0:T(4,128)(2,1)S(1)} all-to-all(bf16[64,4,3584]{2,1,0:T(4,128)(2,1)S(1)} %copy.26), channel_id=1, replica_groups=mesh['rep'=12,'shard'=64] {'shard'}, dimensions={0} | all-to-all | bytes 3670016 | tf_op jit(solution)/shard_map/all_to_all | solution.py:68
  141.7 1.5 all_to_all.16
  143.1 3.3 %select_reduce_fusion = (f32[]{:T(128)}, f32[256,256]{1,0:T(8,128)S(1)}) fusion(bf16[256,3584]{1,0:T(8,128)(2,1)} %all_to_all.16), kind=kOutput, calls=%fused_computation.25 | convolution fusion | flops 469958656 | bytes 2097156 | tf_op jit(solution)/shard_map/dot_general | solution.py:69
  147.1 0.3 fusion.10
  147.5 0.3 fusion.9
  147.8 0.4 fusion.5
  148.2 0.3 fusion.8
  148.5 0.4 fusion.17
  148.9 0.4 fusion.26
  149.3 0.4 fusion.4
  149.7 0.4 fusion.27
  150.1 0.4 fusion.15
  150.5 0.4 fusion.28
  150.9 0.4 fusion.3
  151.3 0.4 fusion.29
  151.7 0.4 fusion.13
  152.1 0.4 fusion.30
  152.5 0.4 fusion.2
  152.9 0.0 copy-start
  152.9 0.4 fusion.31
  153.3 0.4 fusion.11
  153.7 0.4 fusion.32
  154.1 0.4 fusion.1
  154.5 0.4 fusion.6
  154.9 0.0 copy-done
  154.9 0.6 convolution_convert_fusion
  155.5 1.5 all_to_all.17
  157.1 0.0 copy-start.1
  157.1 6.2 %all-to-all-start.1 = ((bf16[64,4,3584]{2,1,0:T(4,128)(2,1)}), bf16[64,4,3584]{2,1,0:T(4,128)(2,1)S(1)}, u32[]{:S(2)}, u32[]{:S(2)}) async-start(bf16[64,4,3584]{2,1,0:T(4,128)(2,1)} %all_to_all.17), calls=%async_computation.1 | async-start | bytes 3670016 | tf_op jit(solution)/shard_map/all_to_all | solution.py:74
  163.3 0.0 copy-done.1
  163.3 0.1 or_bitcast_fusion.3
  163.4 0.1 or_bitcast_fusion.2
  163.5 0.1 or_bitcast_fusion.1
  163.6 0.1 or_bitcast_fusion
  163.7 0.2 add_select_fusion
  163.9 5.3 %copy.24 = f32[8,4,896,4]{0,3,2,1:T(4,128)} copy(f32[8,4,896,4]{2,1,0,3:T(4,128)S(1)} %add_select_fusion) | data formatting | bytes 917504 | tf_op jit(solution)/shard_map/mul | solution.py:76
  169.2 1.1 copy.29
  170.3 38.4 %all-to-all-done.1 = bf16[64,4,3584]{2,1,0:T(4,128)(2,1)S(1)} async-done(((bf16[64,4,3584]{2,1,0:T(4,128)(2,1)}), bf16[64,4,3584]{2,1,0:T(4,128)(2,1)S(1)}, u32[]{:S(2)}, u32[]{:S(2)}) %all-to-all-start.1) | async-done | bytes 1835040 | tf_op jit(solution)/shard_map/all_to_all | solution.py:74
  208.7 0.1 slice.28
  208.8 3.0 %copy.35 = bf16[8,1,4,3584]{0,3,2,1:T(8,128)(2,1)} copy(bf16[8,1,4,3584]{3,2,1,0:T(4,128)(2,1)S(1)} %slice.28) | data formatting | bytes 458752
  211.8 6.8 %fusion = bf16[8,4,3584]{0,2,1:T(8,128)(2,1)} fusion(f32[8,4,3584]{0,2,1:T(8,128)} %bitcast.60, bf16[8,1,4,3584]{0,3,2,1:T(8,128)(2,1)} %copy.35), kind=kLoop, calls=%fused_computation.1 | loop fusion | flops 344064 | bytes 917504 | tf_op jit(solution)/shard_map/convert_element_type | solution.py:76
  218.5 4.0 %copy.30 = bf16[8,4,3584]{2,1,0:T(4,128)(2,1)} copy(bf16[8,4,3584]{0,2,1:T(8,128)(2,1)} %fusion) | data formatting | bytes 458752
Async XLA Ops:
  7.2 68.9 %reduce-scatter.4.cloned.1.call-start = ((), (), s32[]{:S(2)}) async-start(), calls=%async_computation.3 | async-start | bytes 2981888
  11.3 64.8 %copy-start.2 = (f32[8,4,3584]{2,1,0:T(4,128)S(1)}, f32[8,4,3584]{2,1,0:T(4,128)}, u32[]{:S(2)}) copy-start(f32[8,4,3584]{2,1,0:T(4,128)} %param.6) | copy-start | bytes 1376260
  152.9 2.0 copy-start
  157.1 6.2 %copy-start.1 = (s32[8,4,896]{2,1,0:T(4,128)S(1)}, s32[8,4,896]{2,1,0:T(4,128)}, u32[]{:S(2)}) copy-start(s32[8,4,896]{2,1,0:T(4,128)} %param.7) | copy-start | bytes 344068
  157.1 51.6 %all-to-all-start.1 = ((bf16[64,4,3584]{2,1,0:T(4,128)(2,1)}), bf16[64,4,3584]{2,1,0:T(4,128)(2,1)S(1)}, u32[]{:S(2)}, u32[]{:S(2)}) async-start(bf16[64,4,3584]{2,1,0:T(4,128)(2,1)} %all_to_all.17), calls=%async_computation.1 | async-start | bytes 3670016 | tf_op jit(solution)/shard_map/all_to_all | solution.py:74
Sparse Core Ops, SparseCore 0:
  11.4 64.5 reduce-scatter.3
where the time goes:
time: 230 us; the launch traced here: 229 us
  waiting for transfers between devices  103 us (45%)
  blocking collectives  62.4 us (27%)
  local copies, waits for them, and re-layouts  22.7 us (10%)
  between operations  15 us (7%)
  matrix products  11.5 us (5%)
  other arithmetic  8.41 us (4%)
  starting transfers between devices  6.25 us (3%)
    unnamed x2, waiting for transfers between devices  64.8 us
    all_to_all x1, blocking collectives, local(): lax.all_to_all(outgoing, 'shard', split_axis=0, concat_axis=0, tiled=True)  62.4 us
    all_to_all x1, waiting for transfers between devices, local(): lax.all_to_all(orthogonal, 'shard', split_axis=0, concat_axis=0, tiled=True)  38.4 us
    unnamed x12, local copies, waits for them, and re-layouts  12.5 us
    convert_element_type x1, other arithmetic, local(): (UPDATE_SCALE * kept_mask * returned.astype(jnp.float32)).astype(jnp.bflo...  6.76 us
    all_to_all x1, starting transfers between devices, local(): lax.all_to_all(orthogonal, 'shard', split_axis=0, concat_axis=0, tiled=True)  6.21 us
    mul x1, local copies, waits for them, and re-layouts, local(): UPDATE_SCALE * kept_mask * returned.astype(jnp.float32)  5.34 us
  transfers between devices with their start and end apart: 2, of which 2 were waited for; matrix products, arithmetic and copies ran while one was open for 3% of the time, Pallas kernels for 0%

commit v1 on v0

v1 whole, which is shorter than its diff:
```python
import jax
import jax.numpy as jnp
from jax import lax
from jax.experimental import pallas as pl
from jax.experimental.pallas import tpu as pltpu
from jax.sharding import PartitionSpec as P

ITERS = 5
DECAY_RATE = 0.95
EPSILON = 1e-07
QUINTIC_FIRST = 3.4445
QUINTIC_SECOND = -4.775
QUINTIC_THIRD = 2.0315
UPDATE_SCALE = 64.0

REPS = 12
MATS_HERE = 8
PIECE_ROWS = 4
COLS = 3584
SHARDS = 64
ROWS = 256
SLICE = 512
SLICES_USED = COLS // SLICE
HALF = ROWS // 2
BF = jnp.bfloat16
F32 = jnp.float32
PARAMS = pltpu.CompilerParams(vmem_limit_bytes=40 * 1024 * 1024)
GROUP_BITS = (1, 2, 16)


def device_of(matrix, column_slice):
    return (
        (matrix >> 2) * 32
        + (column_slice >> 2) * 16
        + (matrix & 3) * 4
        + (column_slice & 3)
    )


def vmem():
    return pl.BlockSpec(memory_space=pltpu.VMEM)


def mask_kernel(codes_ref, mask_ref):
    group = lax.broadcasted_iota(jnp.int32, (128, 512), 0)
    column = lax.broadcasted_iota(jnp.int32, (128, 512), 1)
    spread = jnp.where((column >> 2) == group, 1.0, 0.0).astype(BF)
    place = lax.broadcasted_iota(jnp.int32, (32, 512), 1) & 3
    for block in range(7):
        code = codes_ref[:, block * 128 : (block + 1) * 128]
        pair = jnp.where(code == 0, 3, jnp.where(code == 1, 5, jnp.where(code == 2, 9, 0)))
        pair = jnp.where(code == 3, 6, jnp.where(code == 4, 10, jnp.where(code == 5, 12, pair)))
        wide = jnp.dot(pair.astype(F32).astype(BF), spread, preferred_element_type=F32).astype(jnp.int32)
        kept = ((wide >> place) & 1).astype(F32) * UPDATE_SCALE
        mask_ref[:, block * 512 : (block + 1) * 512] = kept.astype(BF)


def momentum_kernel(sum_ref, momentum_ref, next_ref, out_ref):
    for matrix in range(MATS_HERE):
        for column_slice in range(8):
            target = device_of(matrix, column_slice)
            if column_slice < SLICES_USED:
                here = slice(column_slice * SLICE, (column_slice + 1) * SLICE)
                value = DECAY_RATE * momentum_ref[matrix, :, here] + sum_ref[matrix, :, here].astype(F32)
                next_ref[matrix, :, here] = value
                out_ref[target] = value.astype(BF)
            else:
                out_ref[target] = jnp.zeros((PIECE_ROWS, SLICE), BF)


def gram_kernel(x_ref, packed_ref):
    def product(a, b):
        return lax.dot_general(a, b, (((1,), (1,)), ((), ())), preferred_element_type=F32)

    low = x_ref[:HALF, :]
    high = x_ref[HALF:, :]
    packed_ref[0] = product(low, low)
    packed_ref[1] = product(low, high)
    packed_ref[2] = product(high, high)


def orthogonal_kernel(packed_ref, x_ref, out_ref):
    def product(a, b):
        return jnp.dot(a, b, precision=lax.Precision.HIGHEST, preferred_element_type=F32)

    cross = packed_ref[1]
    gram = jnp.concatenate(
        [
            jnp.concatenate([packed_ref[0], cross], axis=1),
            jnp.concatenate([cross.T, packed_ref[2]], axis=1),
        ],
        axis=0,
    )
    diagonal = lax.broadcasted_iota(jnp.int32, (ROWS, ROWS), 0) == lax.broadcasted_iota(jnp.int32, (ROWS, ROWS), 1)
    trace_sum = jnp.sum(jnp.where(diagonal, gram, 0.0))
    inverse = lax.rsqrt(jnp.full((1, 1), trace_sum + EPSILON, F32))
    scaled = gram * (inverse * inverse)
    square_form = scaled
    factor = None
    for iteration in range(ITERS):
        polynomial = (
            jnp.where(diagonal, QUINTIC_FIRST, 0.0)
            + QUINTIC_SECOND * square_form
            + QUINTIC_THIRD * product(square_form, square_form)
        )
        factor = polynomial if factor is None else product(polynomial, factor)
        if iteration + 1 < ITERS:
            square_form = product(product(factor, scaled), factor.T)
    coef = (factor * inverse).astype(BF)
    out_ref[...] = jnp.dot(coef, x_ref[...], preferred_element_type=F32).astype(BF)


def update_kernel(returned_ref, mask_ref, update_ref):
    for matrix in range(MATS_HERE):
        for column_slice in range(SLICES_USED):
            here = slice(column_slice * SLICE, (column_slice + 1) * SLICE)
            value = returned_ref[device_of(matrix, column_slice)].astype(F32)
            update_ref[matrix, :, here] = (value * mask_ref[matrix, :, here].astype(F32)).astype(BF)


def call(kernel, outs, *args):
    return pl.pallas_call(
        kernel,
        out_shape=outs,
        in_specs=[vmem() for _ in args],
        out_specs=jax.tree.map(lambda _: vmem(), outs),
        compiler_params=PARAMS,
    )(*args)


def shaped(shape, dtype):
    return jax.ShapeDtypeStruct(shape, dtype)


def local(grad_parts, momentum, mask_codes):
    summed = lax.psum_scatter(
        grad_parts[0].reshape(REPS * MATS_HERE, PIECE_ROWS * COLS), "rep", scatter_dimension=0, tiled=True
    ).reshape(MATS_HERE, PIECE_ROWS, COLS)
    mask = call(mask_kernel, shaped((32, COLS), BF), mask_codes.reshape(32, COLS // 4))
    mask = mask.reshape(MATS_HERE, PIECE_ROWS, COLS)
    summed, mask = lax.optimization_barrier((summed, mask))
    momentum_next, outgoing = call(
        momentum_kernel,
        (shaped((MATS_HERE, PIECE_ROWS, COLS), F32), shaped((SHARDS, PIECE_ROWS, SLICE), BF)),
        summed,
        momentum,
    )
    gathered = lax.all_to_all(outgoing, "shard", split_axis=0, concat_axis=0, tiled=True)
    xmat = gathered.reshape(ROWS, SLICE)
    packed = call(gram_kernel, shaped((3, HALF, HALF), F32), xmat)
    for bit in GROUP_BITS:
        packed = packed + lax.ppermute(packed, "shard", [(i, i ^ bit) for i in range(SHARDS)])
    orthogonal = call(orthogonal_kernel, shaped((ROWS, SLICE), BF), packed, xmat)
    returned = lax.all_to_all(
        orthogonal.reshape(SHARDS, PIECE_ROWS, SLICE), "shard", split_axis=0, concat_axis=0, tiled=True
    )
    update = call(update_kernel, shaped((MATS_HERE, PIECE_ROWS, COLS), BF), returned, mask)
    return (momentum_next, update)


def solution(mesh):
    in_specs = (P("rep", None, "shard", None), P("rep", "shard", None), P("rep", "shard", None))
    out_specs = (P("rep", "shard", None), P("rep", "shard", None))
    return jax.shard_map(local, mesh=mesh, in_specs=in_specs, out_specs=out_specs, check_vma=False)
```

time: 230 us -> 162 us (0.70)
  waiting for transfers between devices: 103 us -> 73.8 us
  local copies, waits for them, and re-layouts: 22.7 us -> 6.03 us
  blocking collectives: 62.4 us -> 48.5 us
  matrix products: 11.5 us -> 0 us
  Pallas kernels: 0 us -> 10.6 us
  other arithmetic: 8.41 us -> 0.07 us
    unnamed x2 -> x1, waiting for transfers between devices: 64.8 us -> 0.02 us
    reduce_scatter x0 -> x1, waiting for transfers between devices: none -> 63.4 us  [local(): lax.psum_scatter(grad_parts[0].reshape(REPS * MATS_HERE, PIECE_ROWS * COL...]
    all_to_all x1 -> x0, waiting for transfers between devices: 38.4 us -> none  [local(): lax.all_to_all(orthogonal, 'shard', split_axis=0, concat_axis=0, tiled=True)]
    all_to_all x1, blocking collectives: 62.4 us -> 29 us  [local(): lax.all_to_all(outgoing, 'shard', split_axis=0, concat_axis=0, tiled=True)]
    all_to_all x0 -> x1, blocking collectives: none -> 19.5 us  [local(): lax.all_to_all(orthogonal.reshape(SHARDS, PIECE_ROWS, SLICE), 'shard', sp...]
    dot_general x22 -> x0, matrix products: 11.5 us -> none  [the longest x1 3.33 us: local(): lax.dot_general(gathered, gathered, (((1,), (1,)), ((), ())), preferred_e...]
    pallas_call x0 -> x5, Pallas kernels: none -> 10.6 us  [call(): pl.pallas_call(kernel, out_shape=outs, in_specs=[vmem() for _ in args], o...]
    ppermute x0 -> x3, waiting for transfers between devices: none -> 10.3 us  [local(): lax.ppermute(packed, 'shard', [(i, i ^ bit) for i in range(SHARDS)])]
  transfers between devices with their start and end apart: 2 -> 4, of which waited for: 2 -> 4; matrix products, arithmetic and copies ran while one was open for 3% -> 0% of each run, Pallas kernels for 0% -> 0%
where the time goes in v1:
time: 162 us; the launch traced here: 161 us
  waiting for transfers between devices  73.8 us (46%)
  blocking collectives  48.5 us (30%)
  between operations  14.1 us (9%)
  Pallas kernels  10.6 us (7%)
  starting transfers between devices  8.18 us (5%)
  local copies, waits for them, and re-layouts  6.03 us (4%)
    reduce_scatter x1, waiting for transfers between devices, local(): lax.psum_scatter(grad_parts[0].reshape(REPS * MATS_HERE, PIECE_ROWS * COL...  63.4 us
    all_to_all x1, blocking collectives, local(): lax.all_to_all(outgoing, 'shard', split_axis=0, concat_axis=0, tiled=True)  29 us
    all_to_all x1, blocking collectives, local(): lax.all_to_all(orthogonal.reshape(SHARDS, PIECE_ROWS, SLICE), 'shard', sp...  19.5 us
    pallas_call x5, Pallas kernels, call(): pl.pallas_call(kernel, out_shape=outs, in_specs=[vmem() for _ in args], o...  10.6 us
    ppermute x3, waiting for transfers between devices, local(): lax.ppermute(packed, 'shard', [(i, i ^ bit) for i in range(SHARDS)])  10.3 us
    ppermute x3, starting transfers between devices, local(): lax.ppermute(packed, 'shard', [(i, i ^ bit) for i in range(SHARDS)])  8.15 us
    unnamed x5, local copies, waits for them, and re-layouts  4.7 us
  transfers between devices with their start and end apart: 4, of which 4 were waited for; matrix products, arithmetic and copies ran while one was open for 0% of the time, Pallas kernels for 0%

profile of v1, /device:TPU:1, one launch (start us, length us, event | category | flops | bytes accessed | tf_op | source)
XLA Modules:
  0.0 161.2 jit_solution(2396484559867584757)
XLA Ops:
  7.2 0.0 reduce-scatter.2.cloned.1.call-start
  7.2 3.8 %copy.5 = bf16[12,8,4,3584]{3,1,2,0:T(8,128)(2,1)} copy(bf16[12,8,4,3584]{3,2,1,0:T(4,128)(2,1)} %bitcast.4) | data formatting | bytes 5505024
  11.0 0.0 copy-start.1
  11.0 0.0 copy-start
  11.0 0.0 reduce-scatter.2.cloned.1.call-update
  11.1 0.9 copy-done.1
  12.0 0.3 shard_map.50
  12.3 0.1 reshape.21.mask_ref
  12.3 63.4 %reduce-scatter.2.cloned.1.call-done = bf16[8,14336]{1,0:T(8,128)(2,1)} async-done(((bf16[96,14336]{1,0:T(8,128)(2,1)}), bf16[8,14336]{1,0:T(8,128)(2,1)}) %reduce-scatter.2.cloned.1.call-update) | async-done | bytes 229392 | tf_op jit(solution)/shard_map/reduce_scatter | solution.py:136
  75.7 1.1 reshape.19.sum_ref
  76.8 0.0 copy-done
  76.9 0.8 shard_map.51
  77.7 29.0 %all_to_all.10 = bf16[64,4,512]{2,1,0:T(4,128)(2,1)S(1)} all-to-all(bf16[64,4,512]{2,1,0:T(4,128)(2,1)S(1)} %get-tuple-element.8), channel_id=1, replica_groups=mesh['rep'=12,'shard'=64] {'shard'}, dimensions={0} | all-to-all | bytes 524288 | tf_op jit(solution)/shard_map/all_to_all | solution.py:148
  106.7 0.1 reshape.22.x_ref
  106.7 0.3 shard_map.52
  107.0 2.4 %collective-permute-start = (f32[3,128,128]{2,1,0:T(8,128)S(1)}, f32[3,128,128]{2,1,0:T(8,128)S(1)}, u32[]{:S(2)}, u32[]{:S(2)}) collective-permute-start(f32[3,128,128]{2,1,0:T(8,128)S(1)} %shard_map.52), channel_id=1, source_target_pairs={{0,1},{1,0},{2,3},{3,2},{4,5},{5,4},{6,7},{7,6},{8,9},{9,8},{10,11... | collective-permute-start | bytes 589832 | tf_op jit(solution)/shard_map/ppermute | solution.py:152
  109.4 1.0 collective-permute-done
  110.4 3.0 %collective-permute-start.1 = (f32[3,128,128]{2,1,0:T(8,128)S(1)}, f32[3,128,128]{2,1,0:T(8,128)S(1)}, u32[]{:S(2)}, u32[]{:S(2)}) collective-permute-start(f32[3,128,128]{2,1,0:T(8,128)S(1)} %add.11), channel_id=1, source_target_pairs={{0,2},{1,3},{2,0},{3,1},{4,6},{5,7},{6,4},{7,5},{8,10},{9,11},{10,... | collective-permute-start | bytes 589832 | tf_op jit(solution)/shard_map/ppermute | solution.py:152
  113.5 5.0 %collective-permute-done.1 = f32[3,128,128]{2,1,0:T(8,128)S(1)} collective-permute-done((f32[3,128,128]{2,1,0:T(8,128)S(1)}, f32[3,128,128]{2,1,0:T(8,128)S(1)}, u32[]{:S(2)}, u32[]{:S(2)}) %collective-permute-start.1) | collective-permute-done | bytes 196640 | tf_op jit(solution)/shard_map/ppermute | solution.py:152
  118.5 2.8 %collective-permute-start.2 = (f32[3,128,128]{2,1,0:T(8,128)S(1)}, f32[3,128,128]{2,1,0:T(8,128)S(1)}, u32[]{:S(2)}, u32[]{:S(2)}) collective-permute-start(f32[3,128,128]{2,1,0:T(8,128)S(1)} %add.12), channel_id=1, source_target_pairs={{0,16},{1,17},{2,18},{3,19},{4,20},{5,21},{6,22},{7,23},{8,24},{9,... | collective-permute-start | bytes 589832 | tf_op jit(solution)/shard_map/ppermute | solution.py:152
  121.2 4.3 %collective-permute-done.2 = f32[3,128,128]{2,1,0:T(8,128)S(1)} collective-permute-done((f32[3,128,128]{2,1,0:T(8,128)S(1)}, f32[3,128,128]{2,1,0:T(8,128)S(1)}, u32[]{:S(2)}, u32[]{:S(2)}) %collective-permute-start.2) | collective-permute-done | bytes 196640 | tf_op jit(solution)/shard_map/ppermute | solution.py:152
  125.6 8.4 %shard_map.53 = bf16[256,512]{1,0:T(8,128)(2,1)S(1)} custom-call(f32[3,128,128]{2,1,0:T(8,128)S(1)} %add.13.packed_ref, bf16[256,512]{1,0:T(8,128)(2,1)S(1)} %reshape.22.x_ref), custom_call_target="tpu_custom_call" | custom-call | tf_op jit(solution)/shard_map/pallas_call | solution.py:122
  134.0 0.1 reshape.23
  134.1 19.5 %all_to_all.11.returned_ref = bf16[64,4,512]{2,1,0:T(4,128)(2,1)S(1)} all-to-all(bf16[64,4,512]{2,1,0:T(4,128)(2,1)S(1)} %reshape.23), channel_id=1, replica_groups=mesh['rep'=12,'shard'=64] {'shard'}, dimensions={0} | all-to-all | bytes 524288 | tf_op jit(solution)/shard_map/all_to_all | solution.py:154
  153.6 0.8 shard_map.54
  (4 shorter events, 0.1 us)
Async XLA Ops:
  7.2 68.6 %reduce-scatter.2.cloned.1.call-start = ((), (), s32[]{:S(2)}) async-start(), calls=%async_computation.3 | async-start | bytes 2981888 | tf_op jit(solution)/shard_map/reduce_scatter | solution.py:136
  11.0 0.9 copy-start.1
  11.0 65.8 %copy-start = (f32[8,4,3584]{2,1,0:T(4,128)S(1)}, f32[8,4,3584]{2,1,0:T(4,128)}, u32[]{:S(2)}) copy-start(f32[8,4,3584]{2,1,0:T(4,128)} %momentum_ref.1) | copy-start | bytes 1376260
  107.0 3.4 %collective-permute-start = (f32[3,128,128]{2,1,0:T(8,128)S(1)}, f32[3,128,128]{2,1,0:T(8,128)S(1)}, u32[]{:S(2)}, u32[]{:S(2)}) collective-permute-start(f32[3,128,128]{2,1,0:T(8,128)S(1)} %shard_map.52), channel_id=1, source_target_pairs={{0,1},{1,0},{2,3},{3,2},{4,5},{5,4},{6,7},{7,6},{8,9},{9,8},{10,11... | collective-permute-start | bytes 589832 | tf_op jit(solution)/shard_map/ppermute | solution.py:152
  110.4 8.0 %collective-permute-start.1 = (f32[3,128,128]{2,1,0:T(8,128)S(1)}, f32[3,128,128]{2,1,0:T(8,128)S(1)}, u32[]{:S(2)}, u32[]{:S(2)}) collective-permute-start(f32[3,128,128]{2,1,0:T(8,128)S(1)} %add.11), channel_id=1, source_target_pairs={{0,2},{1,3},{2,0},{3,1},{4,6},{5,7},{6,4},{7,5},{8,10},{9,11},{10,... | collective-permute-start | bytes 589832 | tf_op jit(solution)/shard_map/ppermute | solution.py:152
  118.5 7.1 %collective-permute-start.2 = (f32[3,128,128]{2,1,0:T(8,128)S(1)}, f32[3,128,128]{2,1,0:T(8,128)S(1)}, u32[]{:S(2)}, u32[]{:S(2)}) collective-permute-start(f32[3,128,128]{2,1,0:T(8,128)S(1)} %add.12), channel_id=1, source_target_pairs={{0,16},{1,17},{2,18},{3,19},{4,20},{5,21},{6,22},{7,23},{8,24},{9,... | collective-permute-start | bytes 589832 | tf_op jit(solution)/shard_map/ppermute | solution.py:152
Sparse Core Ops, SparseCore 0:
  11.2 64.5 reduce-scatter.1

commit v2 on v1

v2 whole, which is shorter than its diff:
```python
import jax
import jax.numpy as jnp
from jax import lax
from jax.experimental import pallas as pl
from jax.experimental.pallas import tpu as pltpu
from jax.sharding import PartitionSpec as P

ITERS = 5
DECAY_RATE = 0.95
EPSILON = 1e-07
QUINTIC_FIRST = 3.4445
QUINTIC_SECOND = -4.775
QUINTIC_THIRD = 2.0315
UPDATE_SCALE = 64.0

MATS_HERE = 8
PIECE_ROWS = 4
COLS = 3584
ROWS = 256
HALF = ROWS // 2
PLANE_X = 4
PLANE_Y = 8
CORES = 2
SHARDS = PLANE_X * PLANE_Y * CORES
OWN_ROWS = PLANE_Y * PIECE_ROWS
BF = jnp.bfloat16
F32 = jnp.float32
CHUNK = (MATS_HERE, PIECE_ROWS, COLS)
PARAMS = pltpu.CompilerParams(vmem_limit_bytes=24 * 1024 * 1024)
NT = (((1,), (1,)), ((), ()))


def shard_index(x, y, core):
    return (x * PLANE_Y + y) * CORES + core


GROUPS_Y = [[shard_index(x, y, c) for y in range(PLANE_Y)] for x in range(PLANE_X) for c in range(CORES)]
GROUPS_X = [[shard_index(x, y, c) for x in range(PLANE_X)] for y in range(PLANE_Y) for c in range(CORES)]
OTHER_CORE = [(i, i ^ 1) for i in range(SHARDS)]


def vmem():
    return pl.BlockSpec(memory_space=pltpu.VMEM)


def smem():
    return pl.BlockSpec(memory_space=pltpu.SMEM)


def mask_kernel(codes_ref, mask_ref):
    group = lax.broadcasted_iota(jnp.int32, (128, 512), 0)
    column = lax.broadcasted_iota(jnp.int32, (128, 512), 1)
    spread = jnp.where((column >> 2) == group, 1.0, 0.0).astype(BF)
    place = lax.broadcasted_iota(jnp.int32, (32, 512), 1) & 3
    for block in range(7):
        code = codes_ref[:, block * 128 : (block + 1) * 128]
        pair = jnp.where(code == 0, 3, jnp.where(code == 1, 5, jnp.where(code == 2, 9, 0)))
        pair = jnp.where(code == 3, 6, jnp.where(code == 4, 10, jnp.where(code == 5, 12, pair)))
        wide = jnp.dot(pair.astype(F32).astype(BF), spread, preferred_element_type=F32).astype(jnp.int32)
        kept = ((wide >> place) & 1).astype(F32) * UPDATE_SCALE
        mask_ref[:, block * 512 : (block + 1) * 512] = kept.astype(BF)


def first_kernel(block_ref, grad_ref, down_ref, up_ref):
    for matrix in range(MATS_HERE):
        down_ref[matrix] = grad_ref[block_ref[0] * MATS_HERE + matrix]
        up_ref[matrix] = grad_ref[block_ref[1] * MATS_HERE + matrix]


def add_kernel(block_ref, grad_ref, received_ref, total_ref):
    for matrix in range(MATS_HERE):
        total_ref[matrix] = received_ref[matrix] + grad_ref[block_ref[0] * MATS_HERE + matrix]


def momentum_kernel(block_ref, grad_ref, down_ref, up_ref, momentum_ref, next_ref, out_ref):
    for matrix in range(MATS_HERE):
        own = grad_ref[block_ref[0] * MATS_HERE + matrix].astype(F32)
        summed = down_ref[matrix].astype(F32) + up_ref[matrix].astype(F32) + own
        value = DECAY_RATE * momentum_ref[matrix] + summed
        next_ref[matrix] = value
        out_ref[matrix] = value.astype(BF)


def split(value):
    high = value.astype(BF)
    return high, (value - high.astype(F32)).astype(BF)


def product(left, right, dims=(((1,), (0,)), ((), ()))):
    def one(a, b):
        return lax.dot_general(a, b, dims, preferred_element_type=F32)

    return one(left[0], right[0]) + (one(left[0], right[1]) + one(left[1], right[0]))


def orthogonal_kernel(place_ref, mine_ref, other_ref, out_ref, coef_ref):
    mine = mine_ref[...]
    other = other_ref[...]

    def block(a, b):
        return lax.dot_general(a, b, NT, preferred_element_type=F32)

    cross = block(mine, other)
    gram = jnp.concatenate(
        [
            jnp.concatenate([block(mine, mine), cross], axis=1),
            jnp.concatenate([cross.T, block(other, other)], axis=1),
        ],
        axis=0,
    )
    diagonal = lax.broadcasted_iota(jnp.int32, (ROWS, ROWS), 0) == lax.broadcasted_iota(jnp.int32, (ROWS, ROWS), 1)
    trace_sum = jnp.sum(jnp.where(diagonal, gram, 0.0))
    inverse = lax.rsqrt(jnp.full((1, 1), trace_sum + EPSILON, F32))
    scaled = gram * (inverse * inverse)
    first = jnp.where(diagonal, QUINTIC_FIRST, 0.0)
    square_form = scaled
    factor = None
    factor_scaled = split(scaled)
    for iteration in range(ITERS):
        parts = split(square_form)
        polynomial = split(first + QUINTIC_SECOND * square_form + QUINTIC_THIRD * product(parts, parts))
        factor = polynomial if factor is None else split(product(polynomial, factor))
        if iteration + 1 < ITERS:
            factor_scaled = split(product(polynomial, factor_scaled))
            square_form = product(factor_scaled, factor, NT)
    coef_ref[...] = (factor[0].astype(F32) + factor[1].astype(F32)) * inverse
    rows = pl.ds(pl.multiple_of(place_ref[0] * OWN_ROWS, OWN_ROWS), OWN_ROWS)
    coef = coef_ref[rows, :].astype(BF)
    out_ref[...] = (
        jnp.dot(coef[:, :HALF], mine, preferred_element_type=F32)
        + jnp.dot(coef[:, HALF:], other, preferred_element_type=F32)
    ).astype(BF)


def update_kernel(returned_ref, mask_ref, update_ref):
    for matrix in range(MATS_HERE):
        update_ref[matrix] = returned_ref[matrix] * mask_ref[matrix]


def call(kernel, outs, *args, scalars=0, scratch=()):
    return pl.pallas_call(
        kernel,
        out_shape=outs,
        in_specs=[smem() if i < scalars else vmem() for i in range(len(args))],
        out_specs=jax.tree.map(lambda _: vmem(), outs),
        scratch_shapes=list(scratch),
        compiler_params=PARAMS,
    )(*args)


def shaped(shape, dtype):
    return jax.ShapeDtypeStruct(shape, dtype)


def local(grad_parts, momentum, mask_codes):
    reps = lax.axis_size("rep")
    place = lax.axis_index("rep")
    grads = grad_parts[0]
    chunk = shaped(CHUNK, BF)

    def block(offset):
        return lax.rem(place + (offset + reps), reps).astype(jnp.int32).reshape(1)

    def send(value, step):
        return lax.ppermute(value, "rep", [(i, (i + step) % reps) for i in range(reps)])

    below = reps // 2
    above = reps - 1 - below
    down, up = call(first_kernel, (chunk, chunk), jnp.concatenate([block(-below), block(above)]), grads, scalars=1)
    down, up = send(down, -1), send(up, 1)
    codes = mask_codes.reshape(MATS_HERE * PIECE_ROWS, COLS // 4)
    for step in range(1, below):
        down = send(call(add_kernel, chunk, block(step - below), grads, down, scalars=1), -1)
        if step < above:
            up = send(call(add_kernel, chunk, block(above - step), grads, up, scalars=1), 1)
        if step == 2:
            up, codes = lax.optimization_barrier((up, codes))
    mask = call(mask_kernel, shaped((MATS_HERE * PIECE_ROWS, COLS), BF), codes).reshape(CHUNK)
    down, up, mask = lax.optimization_barrier((down, up, mask))
    momentum_next, outgoing = call(
        momentum_kernel, (shaped(CHUNK, F32), chunk), block(0), grads, down, up, momentum, scalars=1
    )
    pieces = lax.all_to_all(
        outgoing, "shard", split_axis=0, concat_axis=0, tiled=True, axis_index_groups=GROUPS_Y
    ).reshape(OWN_ROWS, COLS)
    mine = lax.all_gather(pieces, "shard", axis=0, tiled=True, axis_index_groups=GROUPS_X)
    other = lax.ppermute(mine, "shard", OTHER_CORE)
    own_place = (lax.axis_index("shard") // (PLANE_Y * CORES)).astype(jnp.int32).reshape(1)
    orthogonal = call(
        orthogonal_kernel,
        shaped((OWN_ROWS, COLS), BF),
        own_place,
        mine,
        other,
        scalars=1,
        scratch=[pltpu.VMEM((ROWS, ROWS), F32)],
    )
    returned = lax.all_to_all(
        orthogonal.reshape(CHUNK), "shard", split_axis=0, concat_axis=0, tiled=True, axis_index_groups=GROUPS_Y
    )
    update = call(update_kernel, chunk, returned, mask)
    return (momentum_next, update)


def solution(mesh):
    in_specs = (P("rep", None, "shard", None), P("rep", "shard", None), P("rep", "shard", None))
    out_specs = (P("rep", "shard", None), P("rep", "shard", None))
    return jax.shard_map(local, mesh=mesh, in_specs=in_specs, out_specs=out_specs, check_vma=False)
```

time: 162 us -> 137 us (0.85)
  waiting for transfers between devices: 73.8 us -> 9.82 us
  starting transfers between devices: 8.18 us -> 63.1 us
  between operations: 14.1 us -> 0.97 us
  blocking collectives: 48.5 us -> 40.9 us
  Pallas kernels: 10.6 us -> 15.5 us
    reduce_scatter x1 -> x0, waiting for transfers between devices: 63.4 us -> none  [local(): lax.psum_scatter(grad_parts[0].reshape(REPS * MATS_HERE, PIECE_ROWS * COL...]
    ppermute x3 -> x12, starting transfers between devices: 8.15 us -> 63.1 us  [the longest x11 50.4 us: send(): lax.ppermute(value, 'rep', [(i, (i + step) % reps) for i in range(reps)])]
    all_to_all x2, blocking collectives: 48.5 us -> 29.6 us  [the longest x1 15.6 us: local(): lax.all_to_all(outgoing, 'shard', split_axis=0, concat_axis=0, tiled=True...]
    all_gather x0 -> x1, blocking collectives: none -> 11.3 us  [local(): lax.all_gather(pieces, 'shard', axis=0, tiled=True, axis_index_groups=GRO...]
    pallas_call x5 -> x14, Pallas kernels: 10.6 us -> 15.5 us  [call(): pl.pallas_call(kernel, out_shape=outs, in_specs=[smem() if i < scalars el...]
    ppermute x3 -> x12, waiting for transfers between devices: 10.3 us -> 9.82 us  [the longest x11 7.75 us: send(): lax.ppermute(value, 'rep', [(i, (i + step) % reps) for i in range(reps)])]
    unnamed x5 -> x10, local copies, waits for them, and re-layouts: 4.7 us -> 4.42 us
  transfers between devices with their start and end apart: 4 -> 12, of which waited for: 4 -> 6; matrix products, arithmetic and copies ran while one was open for 0% -> 1% of each run, Pallas kernels for 0% -> 4%
where the time goes in v2:
time: 137 us; the launch traced here: 136 us
  starting transfers between devices  63.1 us (46%)
  blocking collectives  40.9 us (30%)
  Pallas kernels  15.5 us (11%)
  waiting for transfers between devices  9.82 us (7%)
  local copies, waits for them, and re-layouts  5.55 us (4%)
    ppermute x11, starting transfers between devices, send(): lax.ppermute(value, 'rep', [(i, (i + step) % reps) for i in range(reps)])  50.4 us
    all_to_all x1, blocking collectives, local(): lax.all_to_all(outgoing, 'shard', split_axis=0, concat_axis=0, tiled=True...  15.6 us
    pallas_call x14, Pallas kernels, call(): pl.pallas_call(kernel, out_shape=outs, in_specs=[smem() if i < scalars el...  15.5 us
    all_to_all x1, blocking collectives, local(): lax.all_to_all(orthogonal.reshape(CHUNK), 'shard', split_axis=0, concat_a...  14 us
    ppermute x1, starting transfers between devices, local(): other = lax.ppermute(mine, 'shard', OTHER_CORE)  12.7 us
    all_gather x1, blocking collectives, local(): lax.all_gather(pieces, 'shard', axis=0, tiled=True, axis_index_groups=GRO...  11.3 us
    ppermute x11, waiting for transfers between devices, send(): lax.ppermute(value, 'rep', [(i, (i + step) % reps) for i in range(reps)])  7.75 us
    unnamed x10, local copies, waits for them, and re-layouts  4.42 us
  transfers between devices with their start and end apart: 12, of which 6 were waited for; matrix products, arithmetic and copies ran while one was open for 1% of the time, Pallas kernels for 4%

profile of v2, /device:TPU:1, one launch (start us, length us, event | category | flops | bytes accessed | tf_op | source)
XLA Modules:
  0.0 135.9 jit_solution(1456321043282920862)
XLA Ops:
  0.7 0.1 pad_add_fusion.block_ref
  0.7 0.0 copy-start
  0.7 1.8 %copy-done = bf16[1,96,4,3584]{3,2,1,0:T(4,128)(2,1)S(1)} copy-done((bf16[1,96,4,3584]{3,2,1,0:T(4,128)(2,1)S(1)}, bf16[1,96,4,3584]{3,2,1,0:T(4,128)(2,1)}, u32[]{:S(2)}) %copy-start) | copy-done | bytes 2752536
  2.5 0.0 copy-start.1
  2.5 1.3 shard_map.50
  3.8 15.1 %collective-permute-start = (bf16[8,4,3584]{2,1,0:T(4,128)(2,1)S(1)}, bf16[8,4,3584]{2,1,0:T(4,128)(2,1)S(1)}, u32[]{:S(2)}, u32[]{:S(2)}) collective-permute-start(bf16[8,4,3584]{2,1,0:T(4,128)(2,1)S(1)} %get-tuple-element.11), channel_id=1, source_target_pairs={{0,704},{64,0},{128,64},{192,128},{256,192},{320,256},{384,320},{4... | collective-permute-start | bytes 688136 | tf_op jit(solution)/shard_map/ppermute | solution.py:165
  18.9 1.9 %collective-permute-start.6 = (bf16[8,4,3584]{2,1,0:T(4,128)(2,1)}, bf16[8,4,3584]{2,1,0:T(4,128)(2,1)S(1)}, u32[]{:S(2)}, u32[]{:S(2)}) collective-permute-start(bf16[8,4,3584]{2,1,0:T(4,128)(2,1)} %get-tuple-element.12), channel_id=1, source_target_pairs={{0,64},{64,128},{128,192},{192,256},{256,320},{320,384},{384,448},... | collective-permute-start | bytes 688136 | tf_op jit(solution)/shard_map/ppermute | solution.py:165
  20.8 2.3 %collective-permute-done.received_ref = bf16[8,4,3584]{2,1,0:T(4,128)(2,1)S(1)} collective-permute-done((bf16[8,4,3584]{2,1,0:T(4,128)(2,1)S(1)}, bf16[8,4,3584]{2,1,0:T(4,128)(2,1)S(1)}, u32[]{:S(2)}, u32[]{:S(2)}) %collective-permute-start) | collective-permute-done | bytes 229408 | tf_op jit(solution)/shard_map/ppermute | solution.py:165
  23.2 0.0 copy-done.1
  23.2 5.3 %collective-permute-start.1 = (bf16[8,4,3584]{2,1,0:T(4,128)(2,1)S(1)}, bf16[8,4,3584]{2,1,0:T(4,128)(2,1)S(1)}, u32[]{:S(2)}, u32[]{:S(2)}) collective-permute-start(bf16[8,4,3584]{2,1,0:T(4,128)(2,1)S(1)} %shard_map.51), channel_id=1, source_target_pairs={{0,704},{64,0},{128,64},{192,128},{256,192},{320,256},{384,320},{4... | collective-permute-start | bytes 688136 | tf_op jit(solution)/shard_map/ppermute | solution.py:165
  28.5 0.0 collective-permute-done.6.received_ref
  28.5 0.7 shard_map.56
  29.2 1.9 %collective-permute-start.7 = (bf16[8,4,3584]{2,1,0:T(4,128)(2,1)}, bf16[8,4,3584]{2,1,0:T(4,128)(2,1)S(1)}, u32[]{:S(2)}, u32[]{:S(2)}) collective-permute-start(bf16[8,4,3584]{2,1,0:T(4,128)(2,1)} %shard_map.56), channel_id=1, source_target_pairs={{0,64},{64,128},{128,192},{192,256},{256,320},{320,384},{384,448},... | collective-permute-start | bytes 688136 | tf_op jit(solution)/shard_map/ppermute | solution.py:165
  31.2 0.7 collective-permute-done.1.received_ref
  31.8 0.7 shard_map.52
  32.6 5.3 %collective-permute-start.2 = (bf16[8,4,3584]{2,1,0:T(4,128)(2,1)}, bf16[8,4,3584]{2,1,0:T(4,128)(2,1)S(1)}, u32[]{:S(2)}, u32[]{:S(2)}) collective-permute-start(bf16[8,4,3584]{2,1,0:T(4,128)(2,1)} %shard_map.52), channel_id=1, source_target_pairs={{0,704},{64,0},{128,64},{192,128},{256,192},{320,256},{384,320},{4... | collective-permute-start | bytes 688136 | tf_op jit(solution)/shard_map/ppermute | solution.py:165
  37.9 0.0 collective-permute-done.7.received_ref
  37.9 1.9 %collective-permute-start.8 = (bf16[8,4,3584]{2,1,0:T(4,128)(2,1)S(1)}, bf16[8,4,3584]{2,1,0:T(4,128)(2,1)S(1)}, u32[]{:S(2)}, u32[]{:S(2)}) collective-permute-start(bf16[8,4,3584]{2,1,0:T(4,128)(2,1)S(1)} %shard_map.57), channel_id=1, source_target_pairs={{0,64},{64,128},{128,192},{192,256},{256,320},{320,384},{384,448},... | collective-permute-start | bytes 688136 | tf_op jit(solution)/shard_map/ppermute | solution.py:165
  39.9 1.3 collective-permute-done.2.received_ref
  41.1 0.0 copy-start.3
  41.1 0.7 copy-done.3
  41.8 0.0 copy-start.4
  41.8 0.9 copy-done.4
  42.8 4.9 %collective-permute-start.3 = (bf16[8,4,3584]{2,1,0:T(4,128)(2,1)S(1)}, bf16[8,4,3584]{2,1,0:T(4,128)(2,1)}, u32[]{:S(2)}, u32[]{:S(2)}) collective-permute-start(bf16[8,4,3584]{2,1,0:T(4,128)(2,1)S(1)} %shard_map.53), channel_id=1, source_target_pairs={{0,704},{64,0},{128,64},{192,128},{256,192},{320,256},{384,320},{4... | collective-permute-start | bytes 688136 | tf_op jit(solution)/shard_map/ppermute | solution.py:165
  47.7 0.9 reshape.67.codes_ref
  48.7 0.0 collective-permute-done.8.received_ref
  48.7 1.9 %collective-permute-start.9 = (bf16[8,4,3584]{2,1,0:T(4,128)(2,1)S(1)}, bf16[8,4,3584]{2,1,0:T(4,128)(2,1)S(1)}, u32[]{:S(2)}, u32[]{:S(2)}) collective-permute-start(bf16[8,4,3584]{2,1,0:T(4,128)(2,1)S(1)} %shard_map.58), channel_id=1, source_target_pairs={{0,64},{64,128},{128,192},{192,256},{256,320},{320,384},{384,448},... | collective-permute-start | bytes 688136 | tf_op jit(solution)/shard_map/ppermute | solution.py:165
  50.6 0.0 collective-permute-done.3.received_ref
  50.7 1.7 %shard_map.54 = bf16[8,4,3584]{2,1,0:T(4,128)(2,1)} custom-call(s32[1]{0:T(128)} %bitcast.3.block_ref, bf16[96,4,3584]{2,1,0:T(4,128)(2,1)S(1)} %bitcast.21, bf16[8,4,3584]{2,1,0:T(4,128)(2,1)} %collective-permute-done.3.received_ref), custom_call_target="tpu_custom_call" | custom-call | tf_op jit(solution)/shard_map/pallas_call | solution.py:141
  52.3 5.1 %collective-permute-start.4 = (bf16[8,4,3584]{2,1,0:T(4,128)(2,1)}, bf16[8,4,3584]{2,1,0:T(4,128)(2,1)}, u32[]{:S(2)}, u32[]{:S(2)}) collective-permute-start(bf16[8,4,3584]{2,1,0:T(4,128)(2,1)} %shard_map.54), channel_id=1, source_target_pairs={{0,704},{64,0},{128,64},{192,128},{256,192},{320,256},{384,320},{4... | collective-permute-start | bytes 688136 | tf_op jit(solution)/shard_map/ppermute | solution.py:165
  57.5 0.0 collective-permute-done.9.received_ref
  57.5 0.7 shard_map.59
  58.2 1.9 %collective-permute-start.10 = (bf16[8,4,3584]{2,1,0:T(4,128)(2,1)}, bf16[8,4,3584]{2,1,0:T(4,128)(2,1)S(1)}, u32[]{:S(2)}, u32[]{:S(2)}) collective-permute-start(bf16[8,4,3584]{2,1,0:T(4,128)(2,1)} %shard_map.59), channel_id=1, source_target_pairs={{0,64},{64,128},{128,192},{192,256},{256,320},{320,384},{384,448},... | collective-permute-start | bytes 688136 | tf_op jit(solution)/shard_map/ppermute | solution.py:165
  60.1 0.6 collective-permute-done.4.received_ref
  60.7 1.6 %shard_map.55 = bf16[8,4,3584]{2,1,0:T(4,128)(2,1)} custom-call(s32[1]{0:T(128)} %bitcast.2.block_ref, bf16[96,4,3584]{2,1,0:T(4,128)(2,1)S(1)} %bitcast.23, bf16[8,4,3584]{2,1,0:T(4,128)(2,1)} %collective-permute-done.4.received_ref), custom_call_target="tpu_custom_call" | custom-call | tf_op jit(solution)/shard_map/pallas_call | solution.py:141
  62.3 5.0 %collective-permute-start.5 = (bf16[8,4,3584]{2,1,0:T(4,128)(2,1)}, bf16[8,4,3584]{2,1,0:T(4,128)(2,1)}, u32[]{:S(2)}, u32[]{:S(2)}) collective-permute-start(bf16[8,4,3584]{2,1,0:T(4,128)(2,1)} %shard_map.55), channel_id=1, source_target_pairs={{0,704},{64,0},{128,64},{192,128},{256,192},{320,256},{384,320},{4... | collective-permute-start | bytes 688136 | tf_op jit(solution)/shard_map/ppermute | solution.py:165
  67.4 0.3 shard_map.60
  67.7 0.1 reshape.68.mask_ref
  67.7 0.0 collective-permute-done.10.up_ref
  67.7 2.9 %collective-permute-done.5.down_ref = bf16[8,4,3584]{2,1,0:T(4,128)(2,1)} collective-permute-done((bf16[8,4,3584]{2,1,0:T(4,128)(2,1)}, bf16[8,4,3584]{2,1,0:T(4,128)(2,1)}, u32[]{:S(2)}, u32[]{:S(2)}) %collective-permute-start.5) | collective-permute-done | bytes 229408 | tf_op jit(solution)/shard_map/ppermute | solution.py:165
  70.6 0.0 copy-start.2
  70.6 1.0 copy-done.2
  71.6 1.8 %shard_map.61 = (f32[8,4,3584]{2,1,0:T(4,128)}, bf16[8,4,3584]{2,1,0:T(4,128)(2,1)S(1)}) custom-call(s32[1]{0:T(128)} %bitcast.block_ref, bf16[96,4,3584]{2,1,0:T(4,128)(2,1)S(1)} %bitcast.24, bf16[8,4,3584]{2,1,0:T(4,128)(2,1)} %collective-permute-done.5.down_ref, bf16[8,4,3584]{2,1,0:T(4,128)(2,1)S(1)} %collective-permute-done.10.up_ref, ...), custom_call_target="tpu_custom_call" | custom-call | tf_op jit(solution)/shard_map/pallas_call | solution.py:141
  73.5 15.6 %all_to_all.10 = bf16[8,4,3584]{2,1,0:T(4,128)(2,1)S(1)} all-to-all(bf16[8,4,3584]{2,1,0:T(4,128)(2,1)S(1)} %get-tuple-element.18), channel_id=1, replica_groups={{0,2,4,6,8,10,12,14},{1,3,5,7,9,11,13,15},{16,18,20,22,24,26,28,30},{17..., dimensions={0} | all-to-all | bytes 458752 | tf_op jit(solution)/shard_map/all_to_all | solution.py:183
  89.1 0.1 reshape.70
  89.1 11.3 %all_gather.3.mine_ref = bf16[128,3584]{1,0:T(8,128)(2,1)S(1)} all-gather(bf16[32,3584]{1,0:T(8,128)(2,1)S(1)} %reshape.70), channel_id=1, replica_groups={{0,16,32,48},{1,17,33,49},{2,18,34,50},{3,19,35,51},{4,20,36,52},{5,21,..., dimensions={0}, use_global_device_ids=true | all-gather | bytes 1146880 | tf_op jit(solution)/shard_map/all_gather | solution.py:186
  100.5 12.7 %collective-permute-start.11 = (bf16[128,3584]{1,0:T(8,128)(2,1)S(1)}, bf16[128,3584]{1,0:T(8,128)(2,1)S(1)}, u32[]{:S(2)}, u32[]{:S(2)}) collective-permute-start(bf16[128,3584]{1,0:T(8,128)(2,1)S(1)} %all_gather.3.mine_ref), channel_id=1, source_target_pairs={{0,1},{1,0},{2,3},{3,2},{4,5},{5,4},{6,7},{7,6},{8,9},{9,8},{10,11... | collective-permute-start | bytes 2752520 | tf_op jit(solution)/shard_map/ppermute | solution.py:187
  113.2 2.1 %collective-permute-done.11.other_ref = bf16[128,3584]{1,0:T(8,128)(2,1)S(1)} collective-permute-done((bf16[128,3584]{1,0:T(8,128)(2,1)S(1)}, bf16[128,3584]{1,0:T(8,128)(2,1)S(1)}, u32[]{:S(2)}, u32[]{:S(2)}) %collective-permute-start.11) | collective-permute-done | bytes 917536 | tf_op jit(solution)/shard_map/ppermute | solution.py:187
  115.2 5.9 %shard_map.62 = bf16[32,3584]{1,0:T(8,128)(2,1)S(1)} custom-call(s32[1]{0:T(128)} %bitcast.13.place_ref, bf16[128,3584]{1,0:T(8,128)(2,1)S(1)} %all_gather.3.mine_ref, bf16[128,3584]{1,0:T(8,128)(2,1)S(1)} %collective-permute-done.11.other_ref), custom_call_target="tpu_custom_call" | custom-call | tf_op jit(solution)/shard_map/pallas_call | solution.py:141
  121.2 0.1 reshape.71
  121.2 14.0 %all_to_all.11.returned_ref = bf16[8,4,3584]{2,1,0:T(4,128)(2,1)S(1)} all-to-all(bf16[8,4,3584]{2,1,0:T(4,128)(2,1)S(1)} %reshape.71), channel_id=1, replica_groups={{0,2,4,6,8,10,12,14},{1,3,5,7,9,11,13,15},{16,18,20,22,24,26,28,30},{17..., dimensions={0} | all-to-all | bytes 458752 | tf_op jit(solution)/shard_map/all_to_all | solution.py:198
  135.2 0.7 shard_map.63
  (4 shorter events, 0.1 us)
Async XLA Ops:
  0.7 1.8 %copy-start = (bf16[1,96,4,3584]{3,2,1,0:T(4,128)(2,1)S(1)}, bf16[1,96,4,3584]{3,2,1,0:T(4,128)(2,1)}, u32[]{:S(2)}) copy-start(bf16[1,96,4,3584]{3,2,1,0:T(4,128)(2,1)} %param.3) | copy-start | bytes 8257540
  2.5 20.6 %copy-start.1 = (bf16[1,96,4,3584]{3,2,1,0:T(4,128)(2,1)S(1)}, bf16[1,96,4,3584]{3,2,1,0:T(4,128)(2,1)}, u32[]{:S(2)}) copy-start(bf16[1,96,4,3584]{3,2,1,0:T(4,128)(2,1)} %param.3) | copy-start | bytes 8257540
  3.8 19.4 %collective-permute-start = (bf16[8,4,3584]{2,1,0:T(4,128)(2,1)S(1)}, bf16[8,4,3584]{2,1,0:T(4,128)(2,1)S(1)}, u32[]{:S(2)}, u32[]{:S(2)}) collective-permute-start(bf16[8,4,3584]{2,1,0:T(4,128)(2,1)S(1)} %get-tuple-element.11), channel_id=1, source_target_pairs={{0,704},{64,0},{128,64},{192,128},{256,192},{320,256},{384,320},{4... | collective-permute-start | bytes 688136 | tf_op jit(solution)/shard_map/ppermute | solution.py:165
  18.9 9.6 %collective-permute-start.6 = (bf16[8,4,3584]{2,1,0:T(4,128)(2,1)}, bf16[8,4,3584]{2,1,0:T(4,128)(2,1)S(1)}, u32[]{:S(2)}, u32[]{:S(2)}) collective-permute-start(bf16[8,4,3584]{2,1,0:T(4,128)(2,1)} %get-tuple-element.12), channel_id=1, source_target_pairs={{0,64},{64,128},{128,192},{192,256},{256,320},{320,384},{384,448},... | collective-permute-start | bytes 688136 | tf_op jit(solution)/shard_map/ppermute | solution.py:165
  23.2 8.7 %collective-permute-start.1 = (bf16[8,4,3584]{2,1,0:T(4,128)(2,1)S(1)}, bf16[8,4,3584]{2,1,0:T(4,128)(2,1)S(1)}, u32[]{:S(2)}, u32[]{:S(2)}) collective-permute-start(bf16[8,4,3584]{2,1,0:T(4,128)(2,1)S(1)} %shard_map.51), channel_id=1, source_target_pairs={{0,704},{64,0},{128,64},{192,128},{256,192},{320,256},{384,320},{4... | collective-permute-start | bytes 688136 | tf_op jit(solution)/shard_map/ppermute | solution.py:165
  29.2 8.6 %collective-permute-start.7 = (bf16[8,4,3584]{2,1,0:T(4,128)(2,1)}, bf16[8,4,3584]{2,1,0:T(4,128)(2,1)S(1)}, u32[]{:S(2)}, u32[]{:S(2)}) collective-permute-start(bf16[8,4,3584]{2,1,0:T(4,128)(2,1)} %shard_map.56), channel_id=1, source_target_pairs={{0,64},{64,128},{128,192},{192,256},{256,320},{320,384},{384,448},... | collective-permute-start | bytes 688136 | tf_op jit(solution)/shard_map/ppermute | solution.py:165
  32.6 8.6 %collective-permute-start.2 = (bf16[8,4,3584]{2,1,0:T(4,128)(2,1)}, bf16[8,4,3584]{2,1,0:T(4,128)(2,1)S(1)}, u32[]{:S(2)}, u32[]{:S(2)}) collective-permute-start(bf16[8,4,3584]{2,1,0:T(4,128)(2,1)} %shard_map.52), channel_id=1, source_target_pairs={{0,704},{64,0},{128,64},{192,128},{256,192},{320,256},{384,320},{4... | collective-permute-start | bytes 688136 | tf_op jit(solution)/shard_map/ppermute | solution.py:165
  37.9 10.8 %collective-permute-start.8 = (bf16[8,4,3584]{2,1,0:T(4,128)(2,1)S(1)}, bf16[8,4,3584]{2,1,0:T(4,128)(2,1)S(1)}, u32[]{:S(2)}, u32[]{:S(2)}) collective-permute-start(bf16[8,4,3584]{2,1,0:T(4,128)(2,1)S(1)} %shard_map.57), channel_id=1, source_target_pairs={{0,64},{64,128},{128,192},{192,256},{256,320},{320,384},{384,448},... | collective-permute-start | bytes 688136 | tf_op jit(solution)/shard_map/ppermute | solution.py:165
  41.1 0.7 copy-start.3
  41.8 0.9 copy-start.4
  42.8 7.9 %collective-permute-start.3 = (bf16[8,4,3584]{2,1,0:T(4,128)(2,1)S(1)}, bf16[8,4,3584]{2,1,0:T(4,128)(2,1)}, u32[]{:S(2)}, u32[]{:S(2)}) collective-permute-start(bf16[8,4,3584]{2,1,0:T(4,128)(2,1)S(1)} %shard_map.53), channel_id=1, source_target_pairs={{0,704},{64,0},{128,64},{192,128},{256,192},{320,256},{384,320},{4... | collective-permute-start | bytes 688136 | tf_op jit(solution)/shard_map/ppermute | solution.py:165
  48.7 8.7 %collective-permute-start.9 = (bf16[8,4,3584]{2,1,0:T(4,128)(2,1)S(1)}, bf16[8,4,3584]{2,1,0:T(4,128)(2,1)S(1)}, u32[]{:S(2)}, u32[]{:S(2)}) collective-permute-start(bf16[8,4,3584]{2,1,0:T(4,128)(2,1)S(1)} %shard_map.58), channel_id=1, source_target_pairs={{0,64},{64,128},{128,192},{192,256},{256,320},{320,384},{384,448},... | collective-permute-start | bytes 688136 | tf_op jit(solution)/shard_map/ppermute | solution.py:165
  52.3 8.4 %collective-permute-start.4 = (bf16[8,4,3584]{2,1,0:T(4,128)(2,1)}, bf16[8,4,3584]{2,1,0:T(4,128)(2,1)}, u32[]{:S(2)}, u32[]{:S(2)}) collective-permute-start(bf16[8,4,3584]{2,1,0:T(4,128)(2,1)} %shard_map.54), channel_id=1, source_target_pairs={{0,704},{64,0},{128,64},{192,128},{256,192},{320,256},{384,320},{4... | collective-permute-start | bytes 688136 | tf_op jit(solution)/shard_map/ppermute | solution.py:165
  58.2 9.6 %collective-permute-start.10 = (bf16[8,4,3584]{2,1,0:T(4,128)(2,1)}, bf16[8,4,3584]{2,1,0:T(4,128)(2,1)S(1)}, u32[]{:S(2)}, u32[]{:S(2)}) collective-permute-start(bf16[8,4,3584]{2,1,0:T(4,128)(2,1)} %shard_map.59), channel_id=1, source_target_pairs={{0,64},{64,128},{128,192},{192,256},{256,320},{320,384},{384,448},... | collective-permute-start | bytes 688136 | tf_op jit(solution)/shard_map/ppermute | solution.py:165
  62.3 8.3 %collective-permute-start.5 = (bf16[8,4,3584]{2,1,0:T(4,128)(2,1)}, bf16[8,4,3584]{2,1,0:T(4,128)(2,1)}, u32[]{:S(2)}, u32[]{:S(2)}) collective-permute-start(bf16[8,4,3584]{2,1,0:T(4,128)(2,1)} %shard_map.55), channel_id=1, source_target_pairs={{0,704},{64,0},{128,64},{192,128},{256,192},{320,256},{384,320},{4... | collective-permute-start | bytes 688136 | tf_op jit(solution)/shard_map/ppermute | solution.py:165
  70.6 1.0 copy-start.2
  100.5 14.8 %collective-permute-start.11 = (bf16[128,3584]{1,0:T(8,128)(2,1)S(1)}, bf16[128,3584]{1,0:T(8,128)(2,1)S(1)}, u32[]{:S(2)}, u32[]{:S(2)}) collective-permute-start(bf16[128,3584]{1,0:T(8,128)(2,1)S(1)} %all_gather.3.mine_ref), channel_id=1, source_target_pairs={{0,1},{1,0},{2,3},{3,2},{4,5},{5,4},{6,7},{7,6},{8,9},{9,8},{10,11... | collective-permute-start | bytes 2752520 | tf_op jit(solution)/shard_map/ppermute | solution.py:187

commit v3 on v2

--- a/solution.py
+++ b/solution.py
@@ -1,3 +1,5 @@
+import functools
+
 import jax
 import jax.numpy as jnp
 from jax import lax
@@ -13,6 +15,7 @@
 QUINTIC_THIRD = 2.0315
 UPDATE_SCALE = 64.0
 
+REPS = 12
 MATS_HERE = 8
 PIECE_ROWS = 4
 COLS = 3584
@@ -26,7 +29,7 @@
 BF = jnp.bfloat16
 F32 = jnp.float32
 CHUNK = (MATS_HERE, PIECE_ROWS, COLS)
-PARAMS = pltpu.CompilerParams(vmem_limit_bytes=24 * 1024 * 1024)
+PARAMS = pltpu.CompilerParams(vmem_limit_bytes=8 * 1024 * 1024)
 NT = (((1,), (1,)), ((), ()))
 
 
@@ -61,20 +64,24 @@
         mask_ref[:, block * 512 : (block + 1) * 512] = kept.astype(BF)
 
 
-def first_kernel(block_ref, grad_ref, down_ref, up_ref):
-    for matrix in range(MATS_HERE):
-        down_ref[matrix] = grad_ref[block_ref[0] * MATS_HERE + matrix]
-        up_ref[matrix] = grad_ref[block_ref[1] * MATS_HERE + matrix]
-
-
-def add_kernel(block_ref, grad_ref, received_ref, total_ref):
-    for matrix in range(MATS_HERE):
-        total_ref[matrix] = received_ref[matrix] + grad_ref[block_ref[0] * MATS_HERE + matrix]
-
-
-def momentum_kernel(block_ref, grad_ref, down_ref, up_ref, momentum_ref, next_ref, out_ref):
-    for matrix in range(MATS_HERE):
-        own = grad_ref[block_ref[0] * MATS_HERE + matrix].astype(F32)
+def grad_chunk(blocks_ref, grad_ref, offset, matrix):
+    return grad_ref[blocks_ref[offset % REPS] * MATS_HERE + matrix]
+
+
+def first_kernel(below, above, blocks_ref, grad_ref, down_ref, up_ref):
+    for matrix in range(MATS_HERE):
+        down_ref[matrix] = grad_chunk(blocks_ref, grad_ref, below, matrix)
+        up_ref[matrix] = grad_chunk(blocks_ref, grad_ref, above, matrix)
+
+
+def add_kernel(offset, blocks_ref, grad_ref, received_ref, total_ref):
+    for matrix in range(MATS_HERE):
+        total_ref[matrix] = received_ref[matrix] + grad_chunk(blocks_ref, grad_ref, offset, matrix)
+
+
+def momentum_kernel(blocks_ref, grad_ref, down_ref, up_ref, momentum_ref, next_ref, out_ref):
+    for matrix in range(MATS_HERE):
+        own = grad_chunk(blocks_ref, grad_ref, 0, matrix).astype(F32)
         summed = down_ref[matrix].astype(F32) + up_ref[matrix].astype(F32) + own
         value = DECAY_RATE * momentum_ref[matrix] + summed
         next_ref[matrix] = value
@@ -153,38 +160,39 @@
 
 
 def local(grad_parts, momentum, mask_codes):
-    reps = lax.axis_size("rep")
-    place = lax.axis_index("rep")
     grads = grad_parts[0]
     chunk = shaped(CHUNK, BF)
-
-    def block(offset):
-        return lax.rem(place + (offset + reps), reps).astype(jnp.int32).reshape(1)
+    blocks = lax.rem(lax.axis_index("rep") + lax.iota(jnp.int32, REPS), REPS)
 
     def send(value, step):
-        return lax.ppermute(value, "rep", [(i, (i + step) % reps) for i in range(reps)])
-
-    below = reps // 2
-    above = reps - 1 - below
-    down, up = call(first_kernel, (chunk, chunk), jnp.concatenate([block(-below), block(above)]), grads, scalars=1)
+        return lax.ppermute(value, "rep", [(i, (i + step) % REPS) for i in range(REPS)])
+
+    def add(offset, received):
+        return call(functools.partial(add_kernel, offset), chunk, blocks, grads, received, scalars=1)
+
+    below = REPS // 2
+    above = REPS - 1 - below
+    down, up = call(functools.partial(first_kernel, -below, above), (chunk, chunk), blocks, grads, scalars=1)
     down, up = send(down, -1), send(up, 1)
-    codes = mask_codes.reshape(MATS_HERE * PIECE_ROWS, COLS // 4)
     for step in range(1, below):
-        down = send(call(add_kernel, chunk, block(step - below), grads, down, scalars=1), -1)
+        down = send(add(step - below, down), -1)
         if step < above:
-            up = send(call(add_kernel, chunk, block(above - step), grads, up, scalars=1), 1)
-        if step == 2:
-            up, codes = lax.optimization_barrier((up, codes))
-    mask = call(mask_kernel, shaped((MATS_HERE * PIECE_ROWS, COLS), BF), codes).reshape(CHUNK)
-    down, up, mask = lax.optimization_barrier((down, up, mask))
+            up = send(add(above - step, up), 1)
     momentum_next, outgoing = call(
-        momentum_kernel, (shaped(CHUNK, F32), chunk), block(0), grads, down, up, momentum, scalars=1
+        momentum_kernel, (shaped(CHUNK, F32), chunk), blocks, grads, down, up, momentum, scalars=1
     )
     pieces = lax.all_to_all(
         outgoing, "shard", split_axis=0, concat_axis=0, tiled=True, axis_index_groups=GROUPS_Y
     ).reshape(OWN_ROWS, COLS)
     mine = lax.all_gather(pieces, "shard", axis=0, tiled=True, axis_index_groups=GROUPS_X)
+    mine, codes = lax.optimization_barrier((mine, mask_codes))
     other = lax.ppermute(mine, "shard", OTHER_CORE)
+    mask = call(
+        mask_kernel,
+        shaped((MATS_HERE * PIECE_ROWS, COLS), BF),
+        codes.reshape(MATS_HERE * PIECE_ROWS, COLS // 4),
+    ).reshape(CHUNK)
+    other, mask = lax.optimization_barrier((other, mask))
     own_place = (lax.axis_index("shard") // (PLANE_Y * CORES)).astype(jnp.int32).reshape(1)
     orthogonal = call(
         orthogonal_kernel,

time: 137 us -> 131 us (0.956)
  local copies, waits for them, and re-layouts: 5.55 us -> 2.01 us
  Pallas kernels: 15.5 us -> 14 us
    unnamed x10 -> x6, local copies, waits for them, and re-layouts: 4.42 us -> 1.79 us
    pallas_call x14, Pallas kernels: 15.5 us -> 14 us  [call(): pl.pallas_call(kernel, out_shape=outs, in_specs=[smem() if i < scalars el...]
  transfers between devices with their start and end apart: 12 -> 12, of which waited for: 6 -> 7; matrix products, arithmetic and copies ran while one was open for 1% -> 0% of each run, Pallas kernels for 4% -> 4%
where the time goes in v3:
time: 131 us; the launch traced here: 130 us
  starting transfers between devices  63.4 us (48%)
  blocking collectives  40.9 us (31%)
  Pallas kernels  14 us (11%)
  waiting for transfers between devices  9.03 us (7%)
  local copies, waits for them, and re-layouts  2.01 us (2%)
    ppermute x11, starting transfers between devices, send(): lax.ppermute(value, 'rep', [(i, (i + step) % REPS) for i in range(REPS)])  50.7 us
    all_to_all x1, blocking collectives, local(): lax.all_to_all(outgoing, 'shard', split_axis=0, concat_axis=0, tiled=True...  15.6 us
    pallas_call x14, Pallas kernels, call(): pl.pallas_call(kernel, out_shape=outs, in_specs=[smem() if i < scalars el...  14 us
    all_to_all x1, blocking collectives, local(): lax.all_to_all(orthogonal.reshape(CHUNK), 'shard', split_axis=0, concat_a...  14 us
    ppermute x1, starting transfers between devices, local(): other = lax.ppermute(mine, 'shard', OTHER_CORE)  12.7 us
    all_gather x1, blocking collectives, local(): lax.all_gather(pieces, 'shard', axis=0, tiled=True, axis_index_groups=GRO...  11.3 us
    ppermute x11, waiting for transfers between devices, send(): lax.ppermute(value, 'rep', [(i, (i + step) % REPS) for i in range(REPS)])  7.38 us
  transfers between devices with their start and end apart: 12, of which 7 were waited for; matrix products, arithmetic and copies ran while one was open for 0% of the time, Pallas kernels for 4%

profile of v3, /device:TPU:1, one launch (start us, length us, event | category | flops | bytes accessed | tf_op | source)
XLA Modules:
  0.0 130.3 jit_solution(6573162843140602810)
XLA Ops:
  0.7 0.0 copy-start
  0.7 1.8 %copy-done = bf16[1,96,4,3584]{3,2,1,0:T(4,128)(2,1)S(1)} copy-done((bf16[1,96,4,3584]{3,2,1,0:T(4,128)(2,1)S(1)}, bf16[1,96,4,3584]{3,2,1,0:T(4,128)(2,1)}, u32[]{:S(2)}) %copy-start) | copy-done | bytes 2752536
  2.4 0.6 shard_map.50
  3.0 15.1 %collective-permute-start = (bf16[8,4,3584]{2,1,0:T(4,128)(2,1)S(1)}, bf16[8,4,3584]{2,1,0:T(4,128)(2,1)S(1)}, u32[]{:S(2)}, u32[]{:S(2)}) collective-permute-start(bf16[8,4,3584]{2,1,0:T(4,128)(2,1)S(1)} %get-tuple-element.10), channel_id=1, source_target_pairs={{0,704},{64,0},{128,64},{192,128},{256,192},{320,256},{384,320},{4... | collective-permute-start | bytes 688136 | tf_op jit(solution)/shard_map/ppermute | solution.py:168
  18.2 1.9 %collective-permute-start.6 = (bf16[8,4,3584]{2,1,0:T(4,128)(2,1)S(1)}, bf16[8,4,3584]{2,1,0:T(4,128)(2,1)S(1)}, u32[]{:S(2)}, u32[]{:S(2)}) collective-permute-start(bf16[8,4,3584]{2,1,0:T(4,128)(2,1)S(1)} %get-tuple-element.11), channel_id=1, source_target_pairs={{0,64},{64,128},{128,192},{192,256},{256,320},{320,384},{384,448},... | collective-permute-start | bytes 688136 | tf_op jit(solution)/shard_map/ppermute | solution.py:168
  20.1 2.3 %collective-permute-done.received_ref = bf16[8,4,3584]{2,1,0:T(4,128)(2,1)S(1)} collective-permute-done((bf16[8,4,3584]{2,1,0:T(4,128)(2,1)S(1)}, bf16[8,4,3584]{2,1,0:T(4,128)(2,1)S(1)}, u32[]{:S(2)}, u32[]{:S(2)}) %collective-permute-start) | collective-permute-done | bytes 229408 | tf_op jit(solution)/shard_map/ppermute | solution.py:168
  22.4 0.6 shard_map.51
  23.0 5.3 %collective-permute-start.1 = (bf16[8,4,3584]{2,1,0:T(4,128)(2,1)S(1)}, bf16[8,4,3584]{2,1,0:T(4,128)(2,1)S(1)}, u32[]{:S(2)}, u32[]{:S(2)}) collective-permute-start(bf16[8,4,3584]{2,1,0:T(4,128)(2,1)S(1)} %shard_map.51), channel_id=1, source_target_pairs={{0,704},{64,0},{128,64},{192,128},{256,192},{320,256},{384,320},{4... | collective-permute-start | bytes 688136 | tf_op jit(solution)/shard_map/ppermute | solution.py:168
  28.3 0.0 collective-permute-done.6.received_ref
  28.3 0.6 shard_map.56
  28.9 1.9 %collective-permute-start.7 = (bf16[8,4,3584]{2,1,0:T(4,128)(2,1)S(1)}, bf16[8,4,3584]{2,1,0:T(4,128)(2,1)S(1)}, u32[]{:S(2)}, u32[]{:S(2)}) collective-permute-start(bf16[8,4,3584]{2,1,0:T(4,128)(2,1)S(1)} %shard_map.56), channel_id=1, source_target_pairs={{0,64},{64,128},{128,192},{192,256},{256,320},{320,384},{384,448},... | collective-permute-start | bytes 688136 | tf_op jit(solution)/shard_map/ppermute | solution.py:168
  30.8 0.8 collective-permute-done.1.received_ref
  31.6 0.6 shard_map.52
  32.2 5.3 %collective-permute-start.2 = (bf16[8,4,3584]{2,1,0:T(4,128)(2,1)S(1)}, bf16[8,4,3584]{2,1,0:T(4,128)(2,1)S(1)}, u32[]{:S(2)}, u32[]{:S(2)}) collective-permute-start(bf16[8,4,3584]{2,1,0:T(4,128)(2,1)S(1)} %shard_map.52), channel_id=1, source_target_pairs={{0,704},{64,0},{128,64},{192,128},{256,192},{320,256},{384,320},{4... | collective-permute-start | bytes 688136 | tf_op jit(solution)/shard_map/ppermute | solution.py:168
  37.5 0.0 collective-permute-done.7.received_ref
  37.5 0.6 shard_map.57
  38.1 1.9 %collective-permute-start.8 = (bf16[8,4,3584]{2,1,0:T(4,128)(2,1)S(1)}, bf16[8,4,3584]{2,1,0:T(4,128)(2,1)S(1)}, u32[]{:S(2)}, u32[]{:S(2)}) collective-permute-start(bf16[8,4,3584]{2,1,0:T(4,128)(2,1)S(1)} %shard_map.57), channel_id=1, source_target_pairs={{0,64},{64,128},{128,192},{192,256},{256,320},{320,384},{384,448},... | collective-permute-start | bytes 688136 | tf_op jit(solution)/shard_map/ppermute | solution.py:168
  40.1 0.4 collective-permute-done.2.received_ref
  40.5 0.6 shard_map.53
  41.1 5.0 %collective-permute-start.3 = (bf16[8,4,3584]{2,1,0:T(4,128)(2,1)S(1)}, bf16[8,4,3584]{2,1,0:T(4,128)(2,1)S(1)}, u32[]{:S(2)}, u32[]{:S(2)}) collective-permute-start(bf16[8,4,3584]{2,1,0:T(4,128)(2,1)S(1)} %shard_map.53), channel_id=1, source_target_pairs={{0,704},{64,0},{128,64},{192,128},{256,192},{320,256},{384,320},{4... | collective-permute-start | bytes 688136 | tf_op jit(solution)/shard_map/ppermute | solution.py:168
  46.1 0.0 collective-permute-done.8.received_ref
  46.1 0.6 shard_map.58
  46.7 1.9 %collective-permute-start.9 = (bf16[8,4,3584]{2,1,0:T(4,128)(2,1)S(1)}, bf16[8,4,3584]{2,1,0:T(4,128)(2,1)S(1)}, u32[]{:S(2)}, u32[]{:S(2)}) collective-permute-start(bf16[8,4,3584]{2,1,0:T(4,128)(2,1)S(1)} %shard_map.58), channel_id=1, source_target_pairs={{0,64},{64,128},{128,192},{192,256},{256,320},{320,384},{384,448},... | collective-permute-start | bytes 688136 | tf_op jit(solution)/shard_map/ppermute | solution.py:168
  48.6 0.4 collective-permute-done.3.received_ref
  49.0 0.6 shard_map.54
  49.6 0.0 copy-start.1
  49.6 5.2 %collective-permute-start.4 = (bf16[8,4,3584]{2,1,0:T(4,128)(2,1)S(1)}, bf16[8,4,3584]{2,1,0:T(4,128)(2,1)S(1)}, u32[]{:S(2)}, u32[]{:S(2)}) collective-permute-start(bf16[8,4,3584]{2,1,0:T(4,128)(2,1)S(1)} %shard_map.54), channel_id=1, source_target_pairs={{0,704},{64,0},{128,64},{192,128},{256,192},{320,256},{384,320},{4... | collective-permute-start | bytes 688136 | tf_op jit(solution)/shard_map/ppermute | solution.py:168
  54.8 0.0 collective-permute-done.9.received_ref
  54.8 0.6 shard_map.59
  55.4 1.9 %collective-permute-start.10 = (bf16[8,4,3584]{2,1,0:T(4,128)(2,1)S(1)}, bf16[8,4,3584]{2,1,0:T(4,128)(2,1)S(1)}, u32[]{:S(2)}, u32[]{:S(2)}) collective-permute-start(bf16[8,4,3584]{2,1,0:T(4,128)(2,1)S(1)} %shard_map.59), channel_id=1, source_target_pairs={{0,64},{64,128},{128,192},{192,256},{256,320},{320,384},{384,448},... | collective-permute-start | bytes 688136 | tf_op jit(solution)/shard_map/ppermute | solution.py:168
  57.3 0.4 collective-permute-done.4.received_ref
  57.7 0.6 shard_map.55
  58.3 0.0 copy-start.2
  58.3 5.2 %collective-permute-start.5 = (bf16[8,4,3584]{2,1,0:T(4,128)(2,1)S(1)}, bf16[8,4,3584]{2,1,0:T(4,128)(2,1)S(1)}, u32[]{:S(2)}, u32[]{:S(2)}) collective-permute-start(bf16[8,4,3584]{2,1,0:T(4,128)(2,1)S(1)} %shard_map.55), channel_id=1, source_target_pairs={{0,704},{64,0},{128,64},{192,128},{256,192},{320,256},{384,320},{4... | collective-permute-start | bytes 688136 | tf_op jit(solution)/shard_map/ppermute | solution.py:168
  63.5 0.0 collective-permute-done.10.up_ref
  63.5 2.9 %collective-permute-done.5.down_ref = bf16[8,4,3584]{2,1,0:T(4,128)(2,1)S(1)} collective-permute-done((bf16[8,4,3584]{2,1,0:T(4,128)(2,1)S(1)}, bf16[8,4,3584]{2,1,0:T(4,128)(2,1)S(1)}, u32[]{:S(2)}, u32[]{:S(2)}) %collective-permute-start.5) | collective-permute-done | bytes 229408 | tf_op jit(solution)/shard_map/ppermute | solution.py:168
  66.4 0.0 copy-done.1
  66.4 1.4 %shard_map.60 = (f32[8,4,3584]{2,1,0:T(4,128)}, bf16[8,4,3584]{2,1,0:T(4,128)(2,1)S(1)}) custom-call(s32[12]{0:T(128)S(1)} %add_remainder_fusion.blocks_ref, bf16[96,4,3584]{2,1,0:T(4,128)(2,1)S(1)} %bitcast.12, bf16[8,4,3584]{2,1,0:T(4,128)(2,1)S(1)} %collective-permute-done.5.down_ref, bf16[8,4,3584]{2,1,0:T(4,128)(2,1)S(1)} %collective-permute-done.10.up_ref, ...), custom_call_target="tpu_custom_call" | custom-call | tf_op jit(solution)/shard_map/pallas_call | solution.py:148
  67.8 15.6 %all_to_all.10 = bf16[8,4,3584]{2,1,0:T(4,128)(2,1)S(1)} all-to-all(bf16[8,4,3584]{2,1,0:T(4,128)(2,1)S(1)} %get-tuple-element.13), channel_id=1, replica_groups={{0,2,4,6,8,10,12,14},{1,3,5,7,9,11,13,15},{16,18,20,22,24,26,28,30},{17..., dimensions={0} | all-to-all | bytes 458752 | tf_op jit(solution)/shard_map/all_to_all | solution.py:184
  83.4 0.1 reshape.20
  83.5 11.3 %all_gather.3.mine_ref = bf16[128,3584]{1,0:T(8,128)(2,1)S(1)} all-gather(bf16[32,3584]{1,0:T(8,128)(2,1)S(1)} %reshape.20), channel_id=1, replica_groups={{0,16,32,48},{1,17,33,49},{2,18,34,50},{3,19,35,51},{4,20,36,52},{5,21,..., dimensions={0}, use_global_device_ids=true | all-gather | bytes 1146880 | tf_op jit(solution)/shard_map/all_gather | solution.py:187
  94.8 12.7 %collective-permute-start.11 = (bf16[128,3584]{1,0:T(8,128)(2,1)S(1)}, bf16[128,3584]{1,0:T(8,128)(2,1)S(1)}, u32[]{:S(2)}, u32[]{:S(2)}) collective-permute-start(bf16[128,3584]{1,0:T(8,128)(2,1)S(1)} %all_gather.3.mine_ref), channel_id=1, source_target_pairs={{0,1},{1,0},{2,3},{3,2},{4,5},{5,4},{6,7},{7,6},{8,9},{9,8},{10,11... | collective-permute-start | bytes 2752520 | tf_op jit(solution)/shard_map/ppermute | solution.py:189
  107.5 0.0 copy-done.2
  107.6 0.3 shard_map.61
  107.9 0.1 reshape.22.mask_ref
  107.9 1.7 %collective-permute-done.11.other_ref = bf16[128,3584]{1,0:T(8,128)(2,1)S(1)} collective-permute-done((bf16[128,3584]{1,0:T(8,128)(2,1)S(1)}, bf16[128,3584]{1,0:T(8,128)(2,1)S(1)}, u32[]{:S(2)}, u32[]{:S(2)}) %collective-permute-start.11) | collective-permute-done | bytes 917536 | tf_op jit(solution)/shard_map/ppermute | solution.py:189
  109.6 5.9 %shard_map.62 = bf16[32,3584]{1,0:T(8,128)(2,1)S(1)} custom-call(s32[1]{0:T(128)} %bitcast.1.place_ref, bf16[128,3584]{1,0:T(8,128)(2,1)S(1)} %all_gather.3.mine_ref, bf16[128,3584]{1,0:T(8,128)(2,1)S(1)} %collective-permute-done.11.other_ref), custom_call_target="tpu_custom_call" | custom-call | tf_op jit(solution)/shard_map/pallas_call | solution.py:148
  115.5 0.1 reshape.23
  115.6 14.0 %all_to_all.11.returned_ref = bf16[8,4,3584]{2,1,0:T(4,128)(2,1)S(1)} all-to-all(bf16[8,4,3584]{2,1,0:T(4,128)(2,1)S(1)} %reshape.23), channel_id=1, replica_groups={{0,2,4,6,8,10,12,14},{1,3,5,7,9,11,13,15},{16,18,20,22,24,26,28,30},{17..., dimensions={0} | all-to-all | bytes 458752 | tf_op jit(solution)/shard_map/all_to_all | solution.py:206
  129.6 0.7 shard_map.63
  (2 shorter events, 0.1 us)
Async XLA Ops:
  0.7 1.8 %copy-start = (bf16[1,96,4,3584]{3,2,1,0:T(4,128)(2,1)S(1)}, bf16[1,96,4,3584]{3,2,1,0:T(4,128)(2,1)}, u32[]{:S(2)}) copy-start(bf16[1,96,4,3584]{3,2,1,0:T(4,128)(2,1)} %param.3) | copy-start | bytes 8257540
  3.0 19.4 %collective-permute-start = (bf16[8,4,3584]{2,1,0:T(4,128)(2,1)S(1)}, bf16[8,4,3584]{2,1,0:T(4,128)(2,1)S(1)}, u32[]{:S(2)}, u32[]{:S(2)}) collective-permute-start(bf16[8,4,3584]{2,1,0:T(4,128)(2,1)S(1)} %get-tuple-element.10), channel_id=1, source_target_pairs={{0,704},{64,0},{128,64},{192,128},{256,192},{320,256},{384,320},{4... | collective-permute-start | bytes 688136 | tf_op jit(solution)/shard_map/ppermute | solution.py:168
  18.2 10.2 %collective-permute-start.6 = (bf16[8,4,3584]{2,1,0:T(4,128)(2,1)S(1)}, bf16[8,4,3584]{2,1,0:T(4,128)(2,1)S(1)}, u32[]{:S(2)}, u32[]{:S(2)}) collective-permute-start(bf16[8,4,3584]{2,1,0:T(4,128)(2,1)S(1)} %get-tuple-element.11), channel_id=1, source_target_pairs={{0,64},{64,128},{128,192},{192,256},{256,320},{320,384},{384,448},... | collective-permute-start | bytes 688136 | tf_op jit(solution)/shard_map/ppermute | solution.py:168
  23.0 8.7 %collective-permute-start.1 = (bf16[8,4,3584]{2,1,0:T(4,128)(2,1)S(1)}, bf16[8,4,3584]{2,1,0:T(4,128)(2,1)S(1)}, u32[]{:S(2)}, u32[]{:S(2)}) collective-permute-start(bf16[8,4,3584]{2,1,0:T(4,128)(2,1)S(1)} %shard_map.51), channel_id=1, source_target_pairs={{0,704},{64,0},{128,64},{192,128},{256,192},{320,256},{384,320},{4... | collective-permute-start | bytes 688136 | tf_op jit(solution)/shard_map/ppermute | solution.py:168
  28.9 8.6 %collective-permute-start.7 = (bf16[8,4,3584]{2,1,0:T(4,128)(2,1)S(1)}, bf16[8,4,3584]{2,1,0:T(4,128)(2,1)S(1)}, u32[]{:S(2)}, u32[]{:S(2)}) collective-permute-start(bf16[8,4,3584]{2,1,0:T(4,128)(2,1)S(1)} %shard_map.56), channel_id=1, source_target_pairs={{0,64},{64,128},{128,192},{192,256},{256,320},{320,384},{384,448},... | collective-permute-start | bytes 688136 | tf_op jit(solution)/shard_map/ppermute | solution.py:168
  32.2 8.3 %collective-permute-start.2 = (bf16[8,4,3584]{2,1,0:T(4,128)(2,1)S(1)}, bf16[8,4,3584]{2,1,0:T(4,128)(2,1)S(1)}, u32[]{:S(2)}, u32[]{:S(2)}) collective-permute-start(bf16[8,4,3584]{2,1,0:T(4,128)(2,1)S(1)} %shard_map.52), channel_id=1, source_target_pairs={{0,704},{64,0},{128,64},{192,128},{256,192},{320,256},{384,320},{4... | collective-permute-start | bytes 688136 | tf_op jit(solution)/shard_map/ppermute | solution.py:168
  38.1 8.0 %collective-permute-start.8 = (bf16[8,4,3584]{2,1,0:T(4,128)(2,1)S(1)}, bf16[8,4,3584]{2,1,0:T(4,128)(2,1)S(1)}, u32[]{:S(2)}, u32[]{:S(2)}) collective-permute-start(bf16[8,4,3584]{2,1,0:T(4,128)(2,1)S(1)} %shard_map.57), channel_id=1, source_target_pairs={{0,64},{64,128},{128,192},{192,256},{256,320},{320,384},{384,448},... | collective-permute-start | bytes 688136 | tf_op jit(solution)/shard_map/ppermute | solution.py:168
  41.1 8.0 %collective-permute-start.3 = (bf16[8,4,3584]{2,1,0:T(4,128)(2,1)S(1)}, bf16[8,4,3584]{2,1,0:T(4,128)(2,1)S(1)}, u32[]{:S(2)}, u32[]{:S(2)}) collective-permute-start(bf16[8,4,3584]{2,1,0:T(4,128)(2,1)S(1)} %shard_map.53), channel_id=1, source_target_pairs={{0,704},{64,0},{128,64},{192,128},{256,192},{320,256},{384,320},{4... | collective-permute-start | bytes 688136 | tf_op jit(solution)/shard_map/ppermute | solution.py:168
  46.7 8.1 %collective-permute-start.9 = (bf16[8,4,3584]{2,1,0:T(4,128)(2,1)S(1)}, bf16[8,4,3584]{2,1,0:T(4,128)(2,1)S(1)}, u32[]{:S(2)}, u32[]{:S(2)}) collective-permute-start(bf16[8,4,3584]{2,1,0:T(4,128)(2,1)S(1)} %shard_map.58), channel_id=1, source_target_pairs={{0,64},{64,128},{128,192},{192,256},{256,320},{320,384},{384,448},... | collective-permute-start | bytes 688136 | tf_op jit(solution)/shard_map/ppermute | solution.py:168
  49.6 16.8 %copy-start.1 = (f32[8,4,3584]{2,1,0:T(4,128)S(1)}, f32[8,4,3584]{2,1,0:T(4,128)}, u32[]{:S(2)}) copy-start(f32[8,4,3584]{2,1,0:T(4,128)} %momentum_ref.1) | copy-start | bytes 1376260
  49.6 8.1 %collective-permute-start.4 = (bf16[8,4,3584]{2,1,0:T(4,128)(2,1)S(1)}, bf16[8,4,3584]{2,1,0:T(4,128)(2,1)S(1)}, u32[]{:S(2)}, u32[]{:S(2)}) collective-permute-start(bf16[8,4,3584]{2,1,0:T(4,128)(2,1)S(1)} %shard_map.54), channel_id=1, source_target_pairs={{0,704},{64,0},{128,64},{192,128},{256,192},{320,256},{384,320},{4... | collective-permute-start | bytes 688136 | tf_op jit(solution)/shard_map/ppermute | solution.py:168
  55.4 8.1 %collective-permute-start.10 = (bf16[8,4,3584]{2,1,0:T(4,128)(2,1)S(1)}, bf16[8,4,3584]{2,1,0:T(4,128)(2,1)S(1)}, u32[]{:S(2)}, u32[]{:S(2)}) collective-permute-start(bf16[8,4,3584]{2,1,0:T(4,128)(2,1)S(1)} %shard_map.59), channel_id=1, source_target_pairs={{0,64},{64,128},{128,192},{192,256},{256,320},{320,384},{384,448},... | collective-permute-start | bytes 688136 | tf_op jit(solution)/shard_map/ppermute | solution.py:168
  58.3 49.2 %copy-start.2 = (s32[8,4,896]{2,1,0:T(4,128)S(1)}, s32[8,4,896]{2,1,0:T(4,128)}, u32[]{:S(2)}) copy-start(s32[8,4,896]{2,1,0:T(4,128)} %param.5) | copy-start | bytes 344068
  58.3 8.1 %collective-permute-start.5 = (bf16[8,4,3584]{2,1,0:T(4,128)(2,1)S(1)}, bf16[8,4,3584]{2,1,0:T(4,128)(2,1)S(1)}, u32[]{:S(2)}, u32[]{:S(2)}) collective-permute-start(bf16[8,4,3584]{2,1,0:T(4,128)(2,1)S(1)} %shard_map.55), channel_id=1, source_target_pairs={{0,704},{64,0},{128,64},{192,128},{256,192},{320,256},{384,320},{4... | collective-permute-start | bytes 688136 | tf_op jit(solution)/shard_map/ppermute | solution.py:168
  94.8 14.8 %collective-permute-start.11 = (bf16[128,3584]{1,0:T(8,128)(2,1)S(1)}, bf16[128,3584]{1,0:T(8,128)(2,1)S(1)}, u32[]{:S(2)}, u32[]{:S(2)}) collective-permute-start(bf16[128,3584]{1,0:T(8,128)(2,1)S(1)} %all_gather.3.mine_ref), channel_id=1, source_target_pairs={{0,1},{1,0},{2,3},{3,2},{4,5},{5,4},{6,7},{7,6},{8,9},{9,8},{10,11... | collective-permute-start | bytes 2752520 | tf_op jit(solution)/shard_map/ppermute | solution.py:189

commit v4 on v3

--- a/solution.py
+++ b/solution.py
@@ -29,6 +29,8 @@
 BF = jnp.bfloat16
 F32 = jnp.float32
 CHUNK = (MATS_HERE, PIECE_ROWS, COLS)
+TILES = COLS // 512
+VIEW = (MATS_HERE * TILES, 4 * PIECE_ROWS, 128)
 PARAMS = pltpu.CompilerParams(vmem_limit_bytes=8 * 1024 * 1024)
 NT = (((1,), (1,)), ((), ()))
 
@@ -64,28 +66,47 @@
         mask_ref[:, block * 512 : (block + 1) * 512] = kept.astype(BF)
 
 
-def grad_chunk(blocks_ref, grad_ref, offset, matrix):
-    return grad_ref[blocks_ref[offset % REPS] * MATS_HERE + matrix]
-
-
-def first_kernel(below, above, blocks_ref, grad_ref, down_ref, up_ref):
-    for matrix in range(MATS_HERE):
-        down_ref[matrix] = grad_chunk(blocks_ref, grad_ref, below, matrix)
-        up_ref[matrix] = grad_chunk(blocks_ref, grad_ref, above, matrix)
+def as_tiles(array):
+    split_up = array.reshape(-1, PIECE_ROWS, TILES, 4, 128)
+    return split_up.transpose(0, 2, 3, 1, 4).reshape(-1, 4 * PIECE_ROWS, 128)
+
+
+def as_rows(tiles):
+    split_up = tiles.reshape(-1, TILES, 4, PIECE_ROWS, 128)
+    return split_up.transpose(0, 3, 1, 2, 4).reshape(-1, PIECE_ROWS, COLS)
+
+
+def grad_chunk(blocks_ref, grad_ref, offset):
+    return grad_ref.at[pl.ds(blocks_ref[offset % REPS] * VIEW[0], VIEW[0])]
+
+
+def first_kernel(below, above, blocks_ref, grad_ref, down_ref, up_ref, sems):
+    copies = [
+        pltpu.make_async_copy(grad_chunk(blocks_ref, grad_ref, below), down_ref, sems.at[0]),
+        pltpu.make_async_copy(grad_chunk(blocks_ref, grad_ref, above), up_ref, sems.at[1]),
+    ]
+    for copy in copies:
+        copy.start()
+    for copy in copies:
+        copy.wait()
 
 
 def add_kernel(offset, blocks_ref, grad_ref, received_ref, total_ref):
-    for matrix in range(MATS_HERE):
-        total_ref[matrix] = received_ref[matrix] + grad_chunk(blocks_ref, grad_ref, offset, matrix)
-
-
-def momentum_kernel(blocks_ref, grad_ref, down_ref, up_ref, momentum_ref, next_ref, out_ref):
-    for matrix in range(MATS_HERE):
-        own = grad_chunk(blocks_ref, grad_ref, 0, matrix).astype(F32)
-        summed = down_ref[matrix].astype(F32) + up_ref[matrix].astype(F32) + own
-        value = DECAY_RATE * momentum_ref[matrix] + summed
-        next_ref[matrix] = value
-        out_ref[matrix] = value.astype(BF)
+    total_ref[...] = received_ref[...] + grad_chunk(blocks_ref, grad_ref, offset)[...]
+
+
+def summed_momentum(blocks_ref, grad_ref, down_ref, up_ref, momentum_ref):
+    own = grad_chunk(blocks_ref, grad_ref, 0)[...].astype(F32)
+    summed = down_ref[...].astype(F32) + up_ref[...].astype(F32) + own
+    return DECAY_RATE * momentum_ref[...] + summed
+
+
+def outgoing_kernel(blocks_ref, grad_ref, down_ref, up_ref, momentum_ref, out_ref):
+    out_ref[...] = summed_momentum(blocks_ref, grad_ref, down_ref, up_ref, momentum_ref).astype(BF)
+
+
+def momentum_kernel(blocks_ref, grad_ref, down_ref, up_ref, momentum_ref, next_ref):
+    next_ref[...] = summed_momentum(blocks_ref, grad_ref, down_ref, up_ref, momentum_ref)
 
 
 def split(value):
@@ -140,15 +161,19 @@
 
 
 def update_kernel(returned_ref, mask_ref, update_ref):
-    for matrix in range(MATS_HERE):
-        update_ref[matrix] = returned_ref[matrix] * mask_ref[matrix]
-
-
-def call(kernel, outs, *args, scalars=0, scratch=()):
+    update_ref[...] = returned_ref[...] * mask_ref[...]
+
+
+def call(kernel, outs, *args, scalars=0, scratch=(), in_hbm=()):
+    def place(index):
+        if index < scalars:
+            return smem()
+        return pl.BlockSpec(memory_space=pltpu.HBM) if index in in_hbm else vmem()
+
     return pl.pallas_call(
         kernel,
         out_shape=outs,
-        in_specs=[smem() if i < scalars else vmem() for i in range(len(args))],
+        in_specs=[place(i) for i in range(len(args))],
         out_specs=jax.tree.map(lambda _: vmem(), outs),
         scratch_shapes=list(scratch),
         compiler_params=PARAMS,
@@ -160,8 +185,9 @@
 
 
 def local(grad_parts, momentum, mask_codes):
-    grads = grad_parts[0]
-    chunk = shaped(CHUNK, BF)
+    grads = as_tiles(grad_parts[0])
+    momentum = as_tiles(momentum)
+    chunk = shaped(VIEW, BF)
     blocks = lax.rem(lax.axis_index("rep") + lax.iota(jnp.int32, REPS), REPS)
 
     def send(value, step):
@@ -172,27 +198,35 @@
 
     below = REPS // 2
     above = REPS - 1 - below
-    down, up = call(functools.partial(first_kernel, -below, above), (chunk, chunk), blocks, grads, scalars=1)
+    down, up = call(
+        functools.partial(first_kernel, -below, above),
+        (chunk, chunk),
+        blocks,
+        grads,
+        scalars=1,
+        in_hbm=(1,),
+        scratch=[pltpu.SemaphoreType.DMA((2,))],
+    )
     down, up = send(down, -1), send(up, 1)
     for step in range(1, below):
         down = send(add(step - below, down), -1)
         if step < above:
             up = send(add(above - step, up), 1)
-    momentum_next, outgoing = call(
-        momentum_kernel, (shaped(CHUNK, F32), chunk), blocks, grads, down, up, momentum, scalars=1
-    )
+    parts = (blocks, grads, down, up, momentum)
+    outgoing = as_rows(call(outgoing_kernel, chunk, *parts, scalars=1))
     pieces = lax.all_to_all(
         outgoing, "shard", split_axis=0, concat_axis=0, tiled=True, axis_index_groups=GROUPS_Y
     ).reshape(OWN_ROWS, COLS)
     mine = lax.all_gather(pieces, "shard", axis=0, tiled=True, axis_index_groups=GROUPS_X)
-    mine, codes = lax.optimization_barrier((mine, mask_codes))
+    mine, codes, parts = lax.optimization_barrier((mine, mask_codes, parts))
     other = lax.ppermute(mine, "shard", OTHER_CORE)
     mask = call(
         mask_kernel,
         shaped((MATS_HERE * PIECE_ROWS, COLS), BF),
         codes.reshape(MATS_HERE * PIECE_ROWS, COLS // 4),
     ).reshape(CHUNK)
-    other, mask = lax.optimization_barrier((other, mask))
+    momentum_next = call(momentum_kernel, shaped(VIEW, F32), *parts, scalars=1)
+    other, mask, momentum_next = lax.optimization_barrier((other, mask, momentum_next))
     own_place = (lax.axis_index("shard") // (PLANE_Y * CORES)).astype(jnp.int32).reshape(1)
     orthogonal = call(
         orthogonal_kernel,
@@ -206,8 +240,8 @@
     returned = lax.all_to_all(
         orthogonal.reshape(CHUNK), "shard", split_axis=0, concat_axis=0, tiled=True, axis_index_groups=GROUPS_Y
     )
-    update = call(update_kernel, chunk, returned, mask)
-    return (momentum_next, update)
+    update = call(update_kernel, chunk, as_tiles(returned), as_tiles(mask))
+    return (as_rows(momentum_next), as_rows(update))
 
 
 def solution(mesh):

time: 131 us -> 139 us (1.061)
  local copies, waits for them, and re-layouts: 2.01 us -> 6.78 us
  Pallas kernels: 14 us -> 16.9 us
  blocking collectives: 40.9 us -> 43.1 us
  waiting for transfers between devices: 9.03 us -> 7.28 us
    pallas_call x14 -> x15, Pallas kernels: 14 us -> 16.9 us  [call(): pl.pallas_call(kernel, out_shape=outs, in_specs=[place(i) for i in range(...]
    unnamed x6 -> x20, local copies, waits for them, and re-layouts: 1.79 us -> 4.27 us
    all_gather x1, blocking collectives: 11.3 us -> 13.3 us  [local(): lax.all_gather(pieces, 'shard', axis=0, tiled=True, axis_index_groups=GRO...]
    ppermute x1, waiting for transfers between devices: 1.65 us -> 0.01 us  [local(): other = lax.ppermute(mine, 'shard', OTHER_CORE)]
  transfers between devices with their start and end apart: 12 -> 12, of which waited for: 7 -> 6; matrix products, arithmetic and copies ran while one was open for 0% -> 1% of each run, Pallas kernels for 4% -> 5%
where the time goes in v4:
time: 139 us; the launch traced here: 138 us
  starting transfers between devices  63.1 us (45%)
  blocking collectives  43.1 us (31%)
  Pallas kernels  16.9 us (12%)
  waiting for transfers between devices  7.28 us (5%)
  local copies, waits for them, and re-layouts  6.78 us (5%)
    ppermute x11, starting transfers between devices, send(): lax.ppermute(value, 'rep', [(i, (i + step) % REPS) for i in range(REPS)])  50.6 us
    pallas_call x15, Pallas kernels, call(): pl.pallas_call(kernel, out_shape=outs, in_specs=[place(i) for i in range(...  16.9 us
    all_to_all x1, blocking collectives, local(): lax.all_to_all(outgoing, 'shard', split_axis=0, concat_axis=0, tiled=True...  15.7 us
    all_to_all x1, blocking collectives, local(): lax.all_to_all(orthogonal.reshape(CHUNK), 'shard', split_axis=0, concat_a...  14.1 us
    all_gather x1, blocking collectives, local(): lax.all_gather(pieces, 'shard', axis=0, tiled=True, axis_index_groups=GRO...  13.3 us
    ppermute x1, starting transfers between devices, local(): other = lax.ppermute(mine, 'shard', OTHER_CORE)  12.5 us
    ppermute x11, waiting for transfers between devices, send(): lax.ppermute(value, 'rep', [(i, (i + step) % REPS) for i in range(REPS)])  7.28 us
    unnamed x20, local copies, waits for them, and re-layouts  4.27 us
  transfers between devices with their start and end apart: 12, of which 6 were waited for; matrix products, arithmetic and copies ran while one was open for 1% of the time, Pallas kernels for 5%

profile of v4, /device:TPU:1, one launch (start us, length us, event | category | flops | bytes accessed | tf_op | source)
XLA Modules:
  0.0 138.2 jit_solution(608242372003251358)
XLA Ops:
  0.7 0.0 copy-start.8
  0.7 0.0 copy-start
  0.7 1.8 %copy-done = bf16[1,96,4,3584]{3,2,1,0:T(4,128)(2,1)S(1)} copy-done((bf16[1,96,4,3584]{3,2,1,0:T(4,128)(2,1)S(1)}, bf16[1,96,4,3584]{3,2,1,0:T(4,128)(2,1)}, u32[]{:S(2)}) %copy-start) | copy-done | bytes 2752536
  2.4 1.2 shard_map.50
  3.6 15.1 %collective-permute-start = (bf16[56,16,128]{2,1,0:T(8,128)(2,1)S(1)}, bf16[56,16,128]{2,1,0:T(8,128)(2,1)S(1)}, u32[]{:S(2)}, u32[]{:S(2)}) collective-permute-start(bf16[56,16,128]{2,1,0:T(8,128)(2,1)S(1)} %get-tuple-element.14), channel_id=1, source_target_pairs={{0,704},{64,0},{128,64},{192,128},{256,192},{320,256},{384,320},{4... | collective-permute-start | bytes 688136 | tf_op jit(solution)/shard_map/ppermute | solution.py:194
  18.8 1.9 %collective-permute-start.6 = (bf16[56,16,128]{2,1,0:T(8,128)(2,1)S(1)}, bf16[56,16,128]{2,1,0:T(8,128)(2,1)S(1)}, u32[]{:S(2)}, u32[]{:S(2)}) collective-permute-start(bf16[56,16,128]{2,1,0:T(8,128)(2,1)S(1)} %get-tuple-element.15), channel_id=1, source_target_pairs={{0,64},{64,128},{128,192},{192,256},{256,320},{320,384},{384,448},... | collective-permute-start | bytes 688136 | tf_op jit(solution)/shard_map/ppermute | solution.py:194
  20.7 2.3 %collective-permute-done.received_ref = bf16[56,16,128]{2,1,0:T(8,128)(2,1)S(1)} collective-permute-done((bf16[56,16,128]{2,1,0:T(8,128)(2,1)S(1)}, bf16[56,16,128]{2,1,0:T(8,128)(2,1)S(1)}, u32[]{:S(2)}, u32[]{:S(2)}) %collective-permute-start) | collective-permute-done | bytes 229408 | tf_op jit(solution)/shard_map/ppermute | solution.py:194
  23.0 0.6 shard_map.51
  23.6 5.3 %collective-permute-start.1 = (bf16[56,16,128]{2,1,0:T(8,128)(2,1)S(1)}, bf16[56,16,128]{2,1,0:T(8,128)(2,1)S(1)}, u32[]{:S(2)}, u32[]{:S(2)}) collective-permute-start(bf16[56,16,128]{2,1,0:T(8,128)(2,1)S(1)} %shard_map.51), channel_id=1, source_target_pairs={{0,704},{64,0},{128,64},{192,128},{256,192},{320,256},{384,320},{4... | collective-permute-start | bytes 688136 | tf_op jit(solution)/shard_map/ppermute | solution.py:194
  28.9 0.0 collective-permute-done.6.received_ref
  28.9 0.6 shard_map.56
  29.5 1.9 %collective-permute-start.7 = (bf16[56,16,128]{2,1,0:T(8,128)(2,1)S(1)}, bf16[56,16,128]{2,1,0:T(8,128)(2,1)S(1)}, u32[]{:S(2)}, u32[]{:S(2)}) collective-permute-start(bf16[56,16,128]{2,1,0:T(8,128)(2,1)S(1)} %shard_map.56), channel_id=1, source_target_pairs={{0,64},{64,128},{128,192},{192,256},{256,320},{320,384},{384,448},... | collective-permute-start | bytes 688136 | tf_op jit(solution)/shard_map/ppermute | solution.py:194
  31.5 0.8 collective-permute-done.1.received_ref
  32.3 0.6 shard_map.52
  32.9 5.3 %collective-permute-start.2 = (bf16[56,16,128]{2,1,0:T(8,128)(2,1)S(1)}, bf16[56,16,128]{2,1,0:T(8,128)(2,1)S(1)}, u32[]{:S(2)}, u32[]{:S(2)}) collective-permute-start(bf16[56,16,128]{2,1,0:T(8,128)(2,1)S(1)} %shard_map.52), channel_id=1, source_target_pairs={{0,704},{64,0},{128,64},{192,128},{256,192},{320,256},{384,320},{4... | collective-permute-start | bytes 688136 | tf_op jit(solution)/shard_map/ppermute | solution.py:194
  38.2 0.0 collective-permute-done.7.received_ref
  38.2 0.6 shard_map.57
  38.8 1.9 %collective-permute-start.8 = (bf16[56,16,128]{2,1,0:T(8,128)(2,1)S(1)}, bf16[56,16,128]{2,1,0:T(8,128)(2,1)S(1)}, u32[]{:S(2)}, u32[]{:S(2)}) collective-permute-start(bf16[56,16,128]{2,1,0:T(8,128)(2,1)S(1)} %shard_map.57), channel_id=1, source_target_pairs={{0,64},{64,128},{128,192},{192,256},{256,320},{320,384},{384,448},... | collective-permute-start | bytes 688136 | tf_op jit(solution)/shard_map/ppermute | solution.py:194
  40.7 0.4 collective-permute-done.2.received_ref
  41.1 0.6 shard_map.53
  41.7 5.0 %collective-permute-start.3 = (bf16[56,16,128]{2,1,0:T(8,128)(2,1)S(1)}, bf16[56,16,128]{2,1,0:T(8,128)(2,1)S(1)}, u32[]{:S(2)}, u32[]{:S(2)}) collective-permute-start(bf16[56,16,128]{2,1,0:T(8,128)(2,1)S(1)} %shard_map.53), channel_id=1, source_target_pairs={{0,704},{64,0},{128,64},{192,128},{256,192},{320,256},{384,320},{4... | collective-permute-start | bytes 688136 | tf_op jit(solution)/shard_map/ppermute | solution.py:194
  46.8 0.0 collective-permute-done.8.received_ref
  46.8 0.6 shard_map.58
  47.4 1.9 %collective-permute-start.9 = (bf16[56,16,128]{2,1,0:T(8,128)(2,1)S(1)}, bf16[56,16,128]{2,1,0:T(8,128)(2,1)S(1)}, u32[]{:S(2)}, u32[]{:S(2)}) collective-permute-start(bf16[56,16,128]{2,1,0:T(8,128)(2,1)S(1)} %shard_map.58), channel_id=1, source_target_pairs={{0,64},{64,128},{128,192},{192,256},{256,320},{320,384},{384,448},... | collective-permute-start | bytes 688136 | tf_op jit(solution)/shard_map/ppermute | solution.py:194
  49.3 0.4 collective-permute-done.3.received_ref
  49.7 0.6 shard_map.54
  50.3 0.0 copy-start.2
  50.3 5.2 %collective-permute-start.4 = (bf16[56,16,128]{2,1,0:T(8,128)(2,1)S(1)}, bf16[56,16,128]{2,1,0:T(8,128)(2,1)S(1)}, u32[]{:S(2)}, u32[]{:S(2)}) collective-permute-start(bf16[56,16,128]{2,1,0:T(8,128)(2,1)S(1)} %shard_map.54), channel_id=1, source_target_pairs={{0,704},{64,0},{128,64},{192,128},{256,192},{320,256},{384,320},{4... | collective-permute-start | bytes 688136 | tf_op jit(solution)/shard_map/ppermute | solution.py:194
  55.5 0.0 collective-permute-done.9.received_ref
  55.5 0.6 shard_map.59
  56.1 1.9 %collective-permute-start.10 = (bf16[56,16,128]{2,1,0:T(8,128)(2,1)S(1)}, bf16[56,16,128]{2,1,0:T(8,128)(2,1)S(1)}, u32[]{:S(2)}, u32[]{:S(2)}) collective-permute-start(bf16[56,16,128]{2,1,0:T(8,128)(2,1)S(1)} %shard_map.59), channel_id=1, source_target_pairs={{0,64},{64,128},{128,192},{192,256},{256,320},{320,384},{384,448},... | collective-permute-start | bytes 688136 | tf_op jit(solution)/shard_map/ppermute | solution.py:194
  58.0 0.4 collective-permute-done.4.received_ref
  58.4 0.6 shard_map.55
  59.0 5.0 %collective-permute-start.5 = (bf16[56,16,128]{2,1,0:T(8,128)(2,1)S(1)}, bf16[56,16,128]{2,1,0:T(8,128)(2,1)S(1)}, u32[]{:S(2)}, u32[]{:S(2)}) collective-permute-start(bf16[56,16,128]{2,1,0:T(8,128)(2,1)S(1)} %shard_map.55), channel_id=1, source_target_pairs={{0,704},{64,0},{128,64},{192,128},{256,192},{320,256},{384,320},{4... | collective-permute-start | bytes 688136 | tf_op jit(solution)/shard_map/ppermute | solution.py:194
  64.0 0.0 collective-permute-done.10.up_ref
  64.1 0.0 copy-start.4
  64.1 2.9 %collective-permute-done.5.down_ref = bf16[56,16,128]{2,1,0:T(8,128)(2,1)S(1)} collective-permute-done((bf16[56,16,128]{2,1,0:T(8,128)(2,1)S(1)}, bf16[56,16,128]{2,1,0:T(8,128)(2,1)S(1)}, u32[]{:S(2)}, u32[]{:S(2)}) %collective-permute-start.5) | collective-permute-done | bytes 229408 | tf_op jit(solution)/shard_map/ppermute | solution.py:194
  67.0 0.0 copy-start.6
  67.0 0.0 copy-done.8
  67.0 0.0 copy-done.2
  67.0 0.0 copy-start.1
  67.0 0.7 shard_map.60
  67.7 0.0 copy-done.4
  67.7 0.0 copy-done.6
  67.7 15.7 %all_to_all.10 = bf16[8,4,3584]{2,1,0:T(4,128)(2,1)S(1)} all-to-all(bf16[8,4,3584]{2,1,0:T(4,128)(2,1)S(1)} %bitcast.52), channel_id=1, replica_groups={{0,2,4,6,8,10,12,14},{1,3,5,7,9,11,13,15},{16,18,20,22,24,26,28,30},{17..., dimensions={0} | all-to-all | bytes 458752 | tf_op jit(solution)/shard_map/all_to_all | solution.py:217
  83.4 0.8 reshape.63
  84.2 13.3 %all_gather.3.mine_ref = bf16[128,3584]{1,0:T(8,128)(2,1)} all-gather(bf16[32,3584]{1,0:T(8,128)(2,1)} %reshape.63), channel_id=1, replica_groups={{0,16,32,48},{1,17,33,49},{2,18,34,50},{3,19,35,51},{4,20,36,52},{5,21,..., dimensions={0}, use_global_device_ids=true | all-gather | bytes 1146880 | tf_op jit(solution)/shard_map/all_gather | solution.py:220
  97.5 12.5 %collective-permute-start.11 = (bf16[128,3584]{1,0:T(8,128)(2,1)}, bf16[128,3584]{1,0:T(8,128)(2,1)}, u32[]{:S(2)}, u32[]{:S(2)}) collective-permute-start(bf16[128,3584]{1,0:T(8,128)(2,1)} %all_gather.3.mine_ref), channel_id=1, source_target_pairs={{0,1},{1,0},{2,3},{3,2},{4,5},{5,4},{6,7},{7,6},{8,9},{9,8},{10,11... | collective-permute-start | bytes 2752520 | tf_op jit(solution)/shard_map/ppermute | solution.py:222
  110.0 0.9 reshape.64.codes_ref
  110.9 0.3 shard_map.61
  111.2 0.7 reshape.65
  112.0 0.0 copy-done.1
  112.0 0.0 copy-start.5
  112.0 0.9 copy-done.5
  112.9 0.0 copy-start.7
  112.9 0.9 copy-done.7
  113.9 0.6 copy-done.9
  114.4 1.4 %shard_map.62 = f32[56,16,128]{2,1,0:T(8,128)} custom-call(s32[12]{0:T(128)S(1)} %copy-done.9, bf16[672,16,128]{2,1,0:T(8,128)(2,1)S(1)} %bitcast.47, bf16[56,16,128]{2,1,0:T(8,128)(2,1)S(1)} %copy-done.7, bf16[56,16,128]{2,1,0:T(8,128)(2,1)S(1)} %copy-done.5, f32[56,16,128]{2,1,0:T(8,128)S(1)} %bitcast.49), custom_call_target="tpu_custom_call" | custom-call | tf_op jit(solution)/shard_map/pallas_call | solution.py:173
  115.9 0.0 collective-permute-done.11.other_ref
  115.9 7.4 %shard_map.63 = bf16[32,3584]{1,0:T(8,128)(2,1)S(1)} custom-call(s32[1]{0:T(128)} %bitcast.14.place_ref, bf16[128,3584]{1,0:T(8,128)(2,1)} %all_gather.3.mine_ref, bf16[128,3584]{1,0:T(8,128)(2,1)} %collective-permute-done.11.other_ref), custom_call_target="tpu_custom_call" | custom-call | tf_op jit(solution)/shard_map/pallas_call | solution.py:173
  123.2 0.1 reshape.69
  123.3 14.1 %all_to_all.11 = bf16[8,4,3584]{2,1,0:T(4,128)(2,1)S(1)} all-to-all(bf16[8,4,3584]{2,1,0:T(4,128)(2,1)S(1)} %reshape.69), channel_id=1, replica_groups={{0,2,4,6,8,10,12,14},{1,3,5,7,9,11,13,15},{16,18,20,22,24,26,28,30},{17..., dimensions={0} | all-to-all | bytes 458752 | tf_op jit(solution)/shard_map/all_to_all | solution.py:240
  137.4 0.0 copy-done.3
  137.4 0.7 shard_map.64
  (3 shorter events, 0.0 us)
Async XLA Ops:
  0.7 66.3 %copy-start.8 = (s32[12]{0:T(128)}, s32[12]{0:T(128)S(1)}, u32[]{:S(2)}) copy-start(s32[12]{0:T(128)S(1)} %add_remainder_fusion.blocks_ref) | copy-start | bytes 148
  0.7 1.8 %copy-start = (bf16[1,96,4,3584]{3,2,1,0:T(4,128)(2,1)S(1)}, bf16[1,96,4,3584]{3,2,1,0:T(4,128)(2,1)}, u32[]{:S(2)}) copy-start(bf16[1,96,4,3584]{3,2,1,0:T(4,128)(2,1)} %param.3) | copy-start | bytes 8257540
  3.6 19.4 %collective-permute-start = (bf16[56,16,128]{2,1,0:T(8,128)(2,1)S(1)}, bf16[56,16,128]{2,1,0:T(8,128)(2,1)S(1)}, u32[]{:S(2)}, u32[]{:S(2)}) collective-permute-start(bf16[56,16,128]{2,1,0:T(8,128)(2,1)S(1)} %get-tuple-element.14), channel_id=1, source_target_pairs={{0,704},{64,0},{128,64},{192,128},{256,192},{320,256},{384,320},{4... | collective-permute-start | bytes 688136 | tf_op jit(solution)/shard_map/ppermute | solution.py:194
  18.8 10.2 %collective-permute-start.6 = (bf16[56,16,128]{2,1,0:T(8,128)(2,1)S(1)}, bf16[56,16,128]{2,1,0:T(8,128)(2,1)S(1)}, u32[]{:S(2)}, u32[]{:S(2)}) collective-permute-start(bf16[56,16,128]{2,1,0:T(8,128)(2,1)S(1)} %get-tuple-element.15), channel_id=1, source_target_pairs={{0,64},{64,128},{128,192},{192,256},{256,320},{320,384},{384,448},... | collective-permute-start | bytes 688136 | tf_op jit(solution)/shard_map/ppermute | solution.py:194
  23.6 8.7 %collective-permute-start.1 = (bf16[56,16,128]{2,1,0:T(8,128)(2,1)S(1)}, bf16[56,16,128]{2,1,0:T(8,128)(2,1)S(1)}, u32[]{:S(2)}, u32[]{:S(2)}) collective-permute-start(bf16[56,16,128]{2,1,0:T(8,128)(2,1)S(1)} %shard_map.51), channel_id=1, source_target_pairs={{0,704},{64,0},{128,64},{192,128},{256,192},{320,256},{384,320},{4... | collective-permute-start | bytes 688136 | tf_op jit(solution)/shard_map/ppermute | solution.py:194
  29.5 8.6 %collective-permute-start.7 = (bf16[56,16,128]{2,1,0:T(8,128)(2,1)S(1)}, bf16[56,16,128]{2,1,0:T(8,128)(2,1)S(1)}, u32[]{:S(2)}, u32[]{:S(2)}) collective-permute-start(bf16[56,16,128]{2,1,0:T(8,128)(2,1)S(1)} %shard_map.56), channel_id=1, source_target_pairs={{0,64},{64,128},{128,192},{192,256},{256,320},{320,384},{384,448},... | collective-permute-start | bytes 688136 | tf_op jit(solution)/shard_map/ppermute | solution.py:194
  32.9 8.3 %collective-permute-start.2 = (bf16[56,16,128]{2,1,0:T(8,128)(2,1)S(1)}, bf16[56,16,128]{2,1,0:T(8,128)(2,1)S(1)}, u32[]{:S(2)}, u32[]{:S(2)}) collective-permute-start(bf16[56,16,128]{2,1,0:T(8,128)(2,1)S(1)} %shard_map.52), channel_id=1, source_target_pairs={{0,704},{64,0},{128,64},{192,128},{256,192},{320,256},{384,320},{4... | collective-permute-start | bytes 688136 | tf_op jit(solution)/shard_map/ppermute | solution.py:194
  38.8 8.0 %collective-permute-start.8 = (bf16[56,16,128]{2,1,0:T(8,128)(2,1)S(1)}, bf16[56,16,128]{2,1,0:T(8,128)(2,1)S(1)}, u32[]{:S(2)}, u32[]{:S(2)}) collective-permute-start(bf16[56,16,128]{2,1,0:T(8,128)(2,1)S(1)} %shard_map.57), channel_id=1, source_target_pairs={{0,64},{64,128},{128,192},{192,256},{256,320},{320,384},{384,448},... | collective-permute-start | bytes 688136 | tf_op jit(solution)/shard_map/ppermute | solution.py:194
  41.7 8.0 %collective-permute-start.3 = (bf16[56,16,128]{2,1,0:T(8,128)(2,1)S(1)}, bf16[56,16,128]{2,1,0:T(8,128)(2,1)S(1)}, u32[]{:S(2)}, u32[]{:S(2)}) collective-permute-start(bf16[56,16,128]{2,1,0:T(8,128)(2,1)S(1)} %shard_map.53), channel_id=1, source_target_pairs={{0,704},{64,0},{128,64},{192,128},{256,192},{320,256},{384,320},{4... | collective-permute-start | bytes 688136 | tf_op jit(solution)/shard_map/ppermute | solution.py:194
  47.4 8.1 %collective-permute-start.9 = (bf16[56,16,128]{2,1,0:T(8,128)(2,1)S(1)}, bf16[56,16,128]{2,1,0:T(8,128)(2,1)S(1)}, u32[]{:S(2)}, u32[]{:S(2)}) collective-permute-start(bf16[56,16,128]{2,1,0:T(8,128)(2,1)S(1)} %shard_map.58), channel_id=1, source_target_pairs={{0,64},{64,128},{128,192},{192,256},{256,320},{320,384},{384,448},... | collective-permute-start | bytes 688136 | tf_op jit(solution)/shard_map/ppermute | solution.py:194
  50.3 16.7 %copy-start.2 = (f32[8,4,3584]{2,1,0:T(4,128)S(1)}, f32[8,4,3584]{2,1,0:T(4,128)}, u32[]{:S(2)}) copy-start(f32[8,4,3584]{2,1,0:T(4,128)} %param.4) | copy-start | bytes 1376260
  50.3 8.1 %collective-permute-start.4 = (bf16[56,16,128]{2,1,0:T(8,128)(2,1)S(1)}, bf16[56,16,128]{2,1,0:T(8,128)(2,1)S(1)}, u32[]{:S(2)}, u32[]{:S(2)}) collective-permute-start(bf16[56,16,128]{2,1,0:T(8,128)(2,1)S(1)} %shard_map.54), channel_id=1, source_target_pairs={{0,704},{64,0},{128,64},{192,128},{256,192},{320,256},{384,320},{4... | collective-permute-start | bytes 688136 | tf_op jit(solution)/shard_map/ppermute | solution.py:194
  56.1 8.0 %collective-permute-start.10 = (bf16[56,16,128]{2,1,0:T(8,128)(2,1)S(1)}, bf16[56,16,128]{2,1,0:T(8,128)(2,1)S(1)}, u32[]{:S(2)}, u32[]{:S(2)}) collective-permute-start(bf16[56,16,128]{2,1,0:T(8,128)(2,1)S(1)} %shard_map.59), channel_id=1, source_target_pairs={{0,64},{64,128},{128,192},{192,256},{256,320},{320,384},{384,448},... | collective-permute-start | bytes 688136 | tf_op jit(solution)/shard_map/ppermute | solution.py:194
  59.0 8.0 %collective-permute-start.5 = (bf16[56,16,128]{2,1,0:T(8,128)(2,1)S(1)}, bf16[56,16,128]{2,1,0:T(8,128)(2,1)S(1)}, u32[]{:S(2)}, u32[]{:S(2)}) collective-permute-start(bf16[56,16,128]{2,1,0:T(8,128)(2,1)S(1)} %shard_map.55), channel_id=1, source_target_pairs={{0,704},{64,0},{128,64},{192,128},{256,192},{320,256},{384,320},{4... | collective-permute-start | bytes 688136 | tf_op jit(solution)/shard_map/ppermute | solution.py:194
  64.1 3.6 %copy-start.4 = (bf16[56,16,128]{2,1,0:T(8,128)(2,1)}, bf16[56,16,128]{2,1,0:T(8,128)(2,1)S(1)}, u32[]{:S(2)}) copy-start(bf16[56,16,128]{2,1,0:T(8,128)(2,1)S(1)} %collective-permute-done.10.up_ref) | copy-start | bytes 688132
  67.0 0.7 copy-start.6
  67.0 45.0 %copy-start.1 = (bf16[1,96,4,3584]{3,2,1,0:T(4,128)(2,1)S(1)}, bf16[1,96,4,3584]{3,2,1,0:T(4,128)(2,1)}, u32[]{:S(2)}) copy-start(bf16[1,96,4,3584]{3,2,1,0:T(4,128)(2,1)} %param.3) | copy-start | bytes 8257540
  97.5 18.4 %collective-permute-start.11 = (bf16[128,3584]{1,0:T(8,128)(2,1)}, bf16[128,3584]{1,0:T(8,128)(2,1)}, u32[]{:S(2)}, u32[]{:S(2)}) collective-permute-start(bf16[128,3584]{1,0:T(8,128)(2,1)} %all_gather.3.mine_ref), channel_id=1, source_target_pairs={{0,1},{1,0},{2,3},{3,2},{4,5},{5,4},{6,7},{7,6},{8,9},{9,8},{10,11... | collective-permute-start | bytes 2752520 | tf_op jit(solution)/shard_map/ppermute | solution.py:222
  112.0 0.9 copy-start.5
  112.9 0.9 copy-start.7
  113.8 0.6 copy-start.9
  114.4 23.0 %copy-start.3 = (bf16[8,4,3584]{2,1,0:T(4,128)(2,1)S(1)}, bf16[8,4,3584]{2,1,0:T(4,128)(2,1)}, u32[]{:S(2)}) copy-start(bf16[8,4,3584]{2,1,0:T(4,128)(2,1)} %reshape.65) | copy-start | bytes 688132

commit v5 on v3

--- a/solution.py
+++ b/solution.py
@@ -46,10 +46,6 @@
     return pl.BlockSpec(memory_space=pltpu.VMEM)
 
 
-def smem():
-    return pl.BlockSpec(memory_space=pltpu.SMEM)
-
-
 def mask_kernel(codes_ref, mask_ref):
     group = lax.broadcasted_iota(jnp.int32, (128, 512), 0)
     column = lax.broadcasted_iota(jnp.int32, (128, 512), 1)
@@ -64,24 +60,28 @@
         mask_ref[:, block * 512 : (block + 1) * 512] = kept.astype(BF)
 
 
-def grad_chunk(blocks_ref, grad_ref, offset, matrix):
-    return grad_ref[blocks_ref[offset % REPS] * MATS_HERE + matrix]
-
-
-def first_kernel(below, above, blocks_ref, grad_ref, down_ref, up_ref):
-    for matrix in range(MATS_HERE):
-        down_ref[matrix] = grad_chunk(blocks_ref, grad_ref, below, matrix)
-        up_ref[matrix] = grad_chunk(blocks_ref, grad_ref, above, matrix)
-
-
-def add_kernel(offset, blocks_ref, grad_ref, received_ref, total_ref):
-    for matrix in range(MATS_HERE):
-        total_ref[matrix] = received_ref[matrix] + grad_chunk(blocks_ref, grad_ref, offset, matrix)
-
-
-def momentum_kernel(blocks_ref, grad_ref, down_ref, up_ref, momentum_ref, next_ref, out_ref):
-    for matrix in range(MATS_HERE):
-        own = grad_chunk(blocks_ref, grad_ref, 0, matrix).astype(F32)
+def chunk_start(offset):
+    place = lax.rem(lax.axis_index("rep") + offset % REPS, REPS)
+    return place * MATS_HERE
+
+
+def first_kernel(below, above, grad_ref, down_ref, up_ref):
+    start_down, start_up = chunk_start(below), chunk_start(above)
+    for matrix in range(MATS_HERE):
+        down_ref[matrix] = grad_ref[start_down + matrix]
+        up_ref[matrix] = grad_ref[start_up + matrix]
+
+
+def add_kernel(offset, grad_ref, received_ref, total_ref):
+    start = chunk_start(offset)
+    for matrix in range(MATS_HERE):
+        total_ref[matrix] = received_ref[matrix] + grad_ref[start + matrix]
+
+
+def momentum_kernel(grad_ref, down_ref, up_ref, momentum_ref, next_ref, out_ref):
+    start = chunk_start(0)
+    for matrix in range(MATS_HERE):
+        own = grad_ref[start + matrix].astype(F32)
         summed = down_ref[matrix].astype(F32) + up_ref[matrix].astype(F32) + own
         value = DECAY_RATE * momentum_ref[matrix] + summed
         next_ref[matrix] = value
@@ -100,7 +100,7 @@
     return one(left[0], right[0]) + (one(left[0], right[1]) + one(left[1], right[0]))
 
 
-def orthogonal_kernel(place_ref, mine_ref, other_ref, out_ref, coef_ref):
+def orthogonal_kernel(mine_ref, other_ref, out_ref, coef_ref):
     mine = mine_ref[...]
     other = other_ref[...]
 
@@ -131,7 +131,8 @@
             factor_scaled = split(product(polynomial, factor_scaled))
             square_form = product(factor_scaled, factor, NT)
     coef_ref[...] = (factor[0].astype(F32) + factor[1].astype(F32)) * inverse
-    rows = pl.ds(pl.multiple_of(place_ref[0] * OWN_ROWS, OWN_ROWS), OWN_ROWS)
+    place_x = lax.div(lax.axis_index("shard"), PLANE_Y * CORES)
+    rows = pl.ds(pl.multiple_of(place_x * OWN_ROWS, OWN_ROWS), OWN_ROWS)
     coef = coef_ref[rows, :].astype(BF)
     out_ref[...] = (
         jnp.dot(coef[:, :HALF], mine, preferred_element_type=F32)
@@ -144,11 +145,11 @@
         update_ref[matrix] = returned_ref[matrix] * mask_ref[matrix]
 
 
-def call(kernel, outs, *args, scalars=0, scratch=()):
+def call(kernel, outs, *args, scratch=()):
     return pl.pallas_call(
         kernel,
         out_shape=outs,
-        in_specs=[smem() if i < scalars else vmem() for i in range(len(args))],
+        in_specs=[vmem() for _ in args],
         out_specs=jax.tree.map(lambda _: vmem(), outs),
         scratch_shapes=list(scratch),
         compiler_params=PARAMS,
@@ -162,25 +163,22 @@
 def local(grad_parts, momentum, mask_codes):
     grads = grad_parts[0]
     chunk = shaped(CHUNK, BF)
-    blocks = lax.rem(lax.axis_index("rep") + lax.iota(jnp.int32, REPS), REPS)
 
     def send(value, step):
         return lax.ppermute(value, "rep", [(i, (i + step) % REPS) for i in range(REPS)])
 
     def add(offset, received):
-        return call(functools.partial(add_kernel, offset), chunk, blocks, grads, received, scalars=1)
+        return call(functools.partial(add_kernel, offset), chunk, grads, received)
 
     below = REPS // 2
     above = REPS - 1 - below
-    down, up = call(functools.partial(first_kernel, -below, above), (chunk, chunk), blocks, grads, scalars=1)
+    down, up = call(functools.partial(first_kernel, -below, above), (chunk, chunk), grads)
     down, up = send(down, -1), send(up, 1)
     for step in range(1, below):
         down = send(add(step - below, down), -1)
         if step < above:
             up = send(add(above - step, up), 1)
-    momentum_next, outgoing = call(
-        momentum_kernel, (shaped(CHUNK, F32), chunk), blocks, grads, down, up, momentum, scalars=1
-    )
+    momentum_next, outgoing = call(momentum_kernel, (shaped(CHUNK, F32), chunk), grads, down, up, momentum)
     pieces = lax.all_to_all(
         outgoing, "shard", split_axis=0, concat_axis=0, tiled=True, axis_index_groups=GROUPS_Y
     ).reshape(OWN_ROWS, COLS)
@@ -193,14 +191,11 @@
         codes.reshape(MATS_HERE * PIECE_ROWS, COLS // 4),
     ).reshape(CHUNK)
     other, mask = lax.optimization_barrier((other, mask))
-    own_place = (lax.axis_index("shard") // (PLANE_Y * CORES)).astype(jnp.int32).reshape(1)
     orthogonal = call(
         orthogonal_kernel,
         shaped((OWN_ROWS, COLS), BF),
-        own_place,
         mine,
         other,
-        scalars=1,
         scratch=[pltpu.VMEM((ROWS, ROWS), F32)],
     )
     returned = lax.all_to_all(

time: 131 us -> 127 us (0.969)
  Pallas kernels: 14 us -> 8.11 us
  waiting for transfers between devices: 9.03 us -> 11.2 us
    pallas_call x14, Pallas kernels: 14 us -> 8.11 us  [call(): pl.pallas_call(kernel, out_shape=outs, in_specs=[vmem() for _ in args], o...]
    ppermute x11, waiting for transfers between devices: 7.38 us -> 9.49 us  [send(): lax.ppermute(value, 'rep', [(i, (i + step) % REPS) for i in range(REPS)])]
  transfers between devices with their start and end apart: 12 -> 12, of which waited for: 7 -> 7; matrix products, arithmetic and copies ran while one was open for 0% -> 0% of each run, Pallas kernels for 4% -> 0%
where the time goes in v5:
time: 127 us; the launch traced here: 126 us
  starting transfers between devices  63.4 us (50%)
  blocking collectives  40.9 us (32%)
  waiting for transfers between devices  11.2 us (9%)
  Pallas kernels  8.11 us (6%)
  local copies, waits for them, and re-layouts  2.01 us (2%)
    ppermute x11, starting transfers between devices, send(): lax.ppermute(value, 'rep', [(i, (i + step) % REPS) for i in range(REPS)])  50.7 us
    all_to_all x1, blocking collectives, local(): lax.all_to_all(outgoing, 'shard', split_axis=0, concat_axis=0, tiled=True...  15.6 us
    all_to_all x1, blocking collectives, local(): lax.all_to_all(orthogonal.reshape(CHUNK), 'shard', split_axis=0, concat_a...  13.9 us
    ppermute x1, starting transfers between devices, local(): other = lax.ppermute(mine, 'shard', OTHER_CORE)  12.7 us
    all_gather x1, blocking collectives, local(): lax.all_gather(pieces, 'shard', axis=0, tiled=True, axis_index_groups=GRO...  11.3 us
    ppermute x11, waiting for transfers between devices, send(): lax.ppermute(value, 'rep', [(i, (i + step) % REPS) for i in range(REPS)])  9.49 us
    pallas_call x14, Pallas kernels, call(): pl.pallas_call(kernel, out_shape=outs, in_specs=[vmem() for _ in args], o...  8.11 us
  transfers between devices with their start and end apart: 12, of which 7 were waited for; matrix products, arithmetic and copies ran while one was open for 0% of the time, Pallas kernels for 0%

profile of v5, /device:TPU:1, one launch (start us, length us, event | category | flops | bytes accessed | tf_op | source)
XLA Modules:
  0.0 126.4 jit_solution(16672514631233443671)
XLA Ops:
  0.6 0.0 copy-start
  0.6 1.8 %copy-done = bf16[1,96,4,3584]{3,2,1,0:T(4,128)(2,1)S(1)} copy-done((bf16[1,96,4,3584]{3,2,1,0:T(4,128)(2,1)S(1)}, bf16[1,96,4,3584]{3,2,1,0:T(4,128)(2,1)}, u32[]{:S(2)}) %copy-start) | copy-done | bytes 2752536
  2.4 15.1 %collective-permute-start = (bf16[8,4,3584]{2,1,0:T(4,128)(2,1)S(1)}, bf16[8,4,3584]{2,1,0:T(4,128)(2,1)S(1)}, u32[]{:S(2)}, u32[]{:S(2)}) collective-permute-start(bf16[8,4,3584]{2,1,0:T(4,128)(2,1)S(1)} %get-tuple-element.10), channel_id=1, source_target_pairs={{0,704},{64,0},{128,64},{192,128},{256,192},{320,256},{384,320},{4... | collective-permute-start | bytes 688136 | tf_op jit(solution)/shard_map/ppermute | solution.py:168
  17.6 1.9 %collective-permute-start.6 = (bf16[8,4,3584]{2,1,0:T(4,128)(2,1)S(1)}, bf16[8,4,3584]{2,1,0:T(4,128)(2,1)S(1)}, u32[]{:S(2)}, u32[]{:S(2)}) collective-permute-start(bf16[8,4,3584]{2,1,0:T(4,128)(2,1)S(1)} %get-tuple-element.11), channel_id=1, source_target_pairs={{0,64},{64,128},{128,192},{192,256},{256,320},{320,384},{384,448},... | collective-permute-start | bytes 688136 | tf_op jit(solution)/shard_map/ppermute | solution.py:168
  19.5 2.3 %collective-permute-done.received_ref = bf16[8,4,3584]{2,1,0:T(4,128)(2,1)S(1)} collective-permute-done((bf16[8,4,3584]{2,1,0:T(4,128)(2,1)S(1)}, bf16[8,4,3584]{2,1,0:T(4,128)(2,1)S(1)}, u32[]{:S(2)}, u32[]{:S(2)}) %collective-permute-start) | collective-permute-done | bytes 229408 | tf_op jit(solution)/shard_map/ppermute | solution.py:168
  21.9 5.3 %collective-permute-start.1 = (bf16[8,4,3584]{2,1,0:T(4,128)(2,1)S(1)}, bf16[8,4,3584]{2,1,0:T(4,128)(2,1)S(1)}, u32[]{:S(2)}, u32[]{:S(2)}) collective-permute-start(bf16[8,4,3584]{2,1,0:T(4,128)(2,1)S(1)} %shard_map.51), channel_id=1, source_target_pairs={{0,704},{64,0},{128,64},{192,128},{256,192},{320,256},{384,320},{4... | collective-permute-start | bytes 688136 | tf_op jit(solution)/shard_map/ppermute | solution.py:168
  27.2 0.0 collective-permute-done.6.received_ref
  27.3 1.9 %collective-permute-start.7 = (bf16[8,4,3584]{2,1,0:T(4,128)(2,1)S(1)}, bf16[8,4,3584]{2,1,0:T(4,128)(2,1)S(1)}, u32[]{:S(2)}, u32[]{:S(2)}) collective-permute-start(bf16[8,4,3584]{2,1,0:T(4,128)(2,1)S(1)} %shard_map.56), channel_id=1, source_target_pairs={{0,64},{64,128},{128,192},{192,256},{256,320},{320,384},{384,448},... | collective-permute-start | bytes 688136 | tf_op jit(solution)/shard_map/ppermute | solution.py:168
  29.2 1.3 %collective-permute-done.1.received_ref = bf16[8,4,3584]{2,1,0:T(4,128)(2,1)S(1)} collective-permute-done((bf16[8,4,3584]{2,1,0:T(4,128)(2,1)S(1)}, bf16[8,4,3584]{2,1,0:T(4,128)(2,1)S(1)}, u32[]{:S(2)}, u32[]{:S(2)}) %collective-permute-start.1) | collective-permute-done | bytes 229408 | tf_op jit(solution)/shard_map/ppermute | solution.py:168
  30.5 5.3 %collective-permute-start.2 = (bf16[8,4,3584]{2,1,0:T(4,128)(2,1)S(1)}, bf16[8,4,3584]{2,1,0:T(4,128)(2,1)S(1)}, u32[]{:S(2)}, u32[]{:S(2)}) collective-permute-start(bf16[8,4,3584]{2,1,0:T(4,128)(2,1)S(1)} %shard_map.52), channel_id=1, source_target_pairs={{0,704},{64,0},{128,64},{192,128},{256,192},{320,256},{384,320},{4... | collective-permute-start | bytes 688136 | tf_op jit(solution)/shard_map/ppermute | solution.py:168
  35.9 0.0 collective-permute-done.7.received_ref
  35.9 1.9 %collective-permute-start.8 = (bf16[8,4,3584]{2,1,0:T(4,128)(2,1)S(1)}, bf16[8,4,3584]{2,1,0:T(4,128)(2,1)S(1)}, u32[]{:S(2)}, u32[]{:S(2)}) collective-permute-start(bf16[8,4,3584]{2,1,0:T(4,128)(2,1)S(1)} %shard_map.57), channel_id=1, source_target_pairs={{0,64},{64,128},{128,192},{192,256},{256,320},{320,384},{384,448},... | collective-permute-start | bytes 688136 | tf_op jit(solution)/shard_map/ppermute | solution.py:168
  37.9 1.0 collective-permute-done.2.received_ref
  38.8 5.0 %collective-permute-start.3 = (bf16[8,4,3584]{2,1,0:T(4,128)(2,1)S(1)}, bf16[8,4,3584]{2,1,0:T(4,128)(2,1)S(1)}, u32[]{:S(2)}, u32[]{:S(2)}) collective-permute-start(bf16[8,4,3584]{2,1,0:T(4,128)(2,1)S(1)} %shard_map.53), channel_id=1, source_target_pairs={{0,704},{64,0},{128,64},{192,128},{256,192},{320,256},{384,320},{4... | collective-permute-start | bytes 688136 | tf_op jit(solution)/shard_map/ppermute | solution.py:168
  43.9 0.0 collective-permute-done.8.received_ref
  43.9 1.9 %collective-permute-start.9 = (bf16[8,4,3584]{2,1,0:T(4,128)(2,1)S(1)}, bf16[8,4,3584]{2,1,0:T(4,128)(2,1)S(1)}, u32[]{:S(2)}, u32[]{:S(2)}) collective-permute-start(bf16[8,4,3584]{2,1,0:T(4,128)(2,1)S(1)} %shard_map.58), channel_id=1, source_target_pairs={{0,64},{64,128},{128,192},{192,256},{256,320},{320,384},{384,448},... | collective-permute-start | bytes 688136 | tf_op jit(solution)/shard_map/ppermute | solution.py:168
  45.9 1.0 collective-permute-done.3.received_ref
  46.9 0.0 copy-start.1
  46.9 5.2 %collective-permute-start.4 = (bf16[8,4,3584]{2,1,0:T(4,128)(2,1)S(1)}, bf16[8,4,3584]{2,1,0:T(4,128)(2,1)S(1)}, u32[]{:S(2)}, u32[]{:S(2)}) collective-permute-start(bf16[8,4,3584]{2,1,0:T(4,128)(2,1)S(1)} %shard_map.54), channel_id=1, source_target_pairs={{0,704},{64,0},{128,64},{192,128},{256,192},{320,256},{384,320},{4... | collective-permute-start | bytes 688136 | tf_op jit(solution)/shard_map/ppermute | solution.py:168
  52.0 0.0 collective-permute-done.9.received_ref
  52.1 1.9 %collective-permute-start.10 = (bf16[8,4,3584]{2,1,0:T(4,128)(2,1)S(1)}, bf16[8,4,3584]{2,1,0:T(4,128)(2,1)S(1)}, u32[]{:S(2)}, u32[]{:S(2)}) collective-permute-start(bf16[8,4,3584]{2,1,0:T(4,128)(2,1)S(1)} %shard_map.59), channel_id=1, source_target_pairs={{0,64},{64,128},{128,192},{192,256},{256,320},{320,384},{384,448},... | collective-permute-start | bytes 688136 | tf_op jit(solution)/shard_map/ppermute | solution.py:168
  54.0 1.0 collective-permute-done.4.received_ref
  55.0 0.0 copy-start.2
  55.0 5.2 %collective-permute-start.5 = (bf16[8,4,3584]{2,1,0:T(4,128)(2,1)S(1)}, bf16[8,4,3584]{2,1,0:T(4,128)(2,1)S(1)}, u32[]{:S(2)}, u32[]{:S(2)}) collective-permute-start(bf16[8,4,3584]{2,1,0:T(4,128)(2,1)S(1)} %shard_map.55), channel_id=1, source_target_pairs={{0,704},{64,0},{128,64},{192,128},{256,192},{320,256},{384,320},{4... | collective-permute-start | bytes 688136 | tf_op jit(solution)/shard_map/ppermute | solution.py:168
  60.2 0.0 collective-permute-done.10.up_ref
  60.2 2.9 %collective-permute-done.5.down_ref = bf16[8,4,3584]{2,1,0:T(4,128)(2,1)S(1)} collective-permute-done((bf16[8,4,3584]{2,1,0:T(4,128)(2,1)S(1)}, bf16[8,4,3584]{2,1,0:T(4,128)(2,1)S(1)}, u32[]{:S(2)}, u32[]{:S(2)}) %collective-permute-start.5) | collective-permute-done | bytes 229408 | tf_op jit(solution)/shard_map/ppermute | solution.py:168
  63.1 0.0 copy-done.1
  63.1 0.9 shard_map.60
  64.0 15.6 %all_to_all.10 = bf16[8,4,3584]{2,1,0:T(4,128)(2,1)S(1)} all-to-all(bf16[8,4,3584]{2,1,0:T(4,128)(2,1)S(1)} %get-tuple-element.13), channel_id=1, replica_groups={{0,2,4,6,8,10,12,14},{1,3,5,7,9,11,13,15},{16,18,20,22,24,26,28,30},{17..., dimensions={0} | all-to-all | bytes 458752 | tf_op jit(solution)/shard_map/all_to_all | solution.py:182
  79.6 0.1 reshape.16
  79.7 11.3 %all_gather.3.mine_ref = bf16[128,3584]{1,0:T(8,128)(2,1)S(1)} all-gather(bf16[32,3584]{1,0:T(8,128)(2,1)S(1)} %reshape.16), channel_id=1, replica_groups={{0,16,32,48},{1,17,33,49},{2,18,34,50},{3,19,35,51},{4,20,36,52},{5,21,..., dimensions={0}, use_global_device_ids=true | all-gather | bytes 1146880 | tf_op jit(solution)/shard_map/all_gather | solution.py:185
  91.0 12.7 %collective-permute-start.11 = (bf16[128,3584]{1,0:T(8,128)(2,1)S(1)}, bf16[128,3584]{1,0:T(8,128)(2,1)S(1)}, u32[]{:S(2)}, u32[]{:S(2)}) collective-permute-start(bf16[128,3584]{1,0:T(8,128)(2,1)S(1)} %all_gather.3.mine_ref), channel_id=1, source_target_pairs={{0,1},{1,0},{2,3},{3,2},{4,5},{5,4},{6,7},{7,6},{8,9},{9,8},{10,11... | collective-permute-start | bytes 2752520 | tf_op jit(solution)/shard_map/ppermute | solution.py:187
  103.7 0.0 copy-done.2
  103.7 0.3 shard_map.61
  104.0 0.1 reshape.18.mask_ref
  104.1 1.7 %collective-permute-done.11.other_ref = bf16[128,3584]{1,0:T(8,128)(2,1)S(1)} collective-permute-done((bf16[128,3584]{1,0:T(8,128)(2,1)S(1)}, bf16[128,3584]{1,0:T(8,128)(2,1)S(1)}, u32[]{:S(2)}, u32[]{:S(2)}) %collective-permute-start.11) | collective-permute-done | bytes 917536 | tf_op jit(solution)/shard_map/ppermute | solution.py:187
  105.8 5.9 %shard_map.62 = bf16[32,3584]{1,0:T(8,128)(2,1)S(1)} custom-call(bf16[128,3584]{1,0:T(8,128)(2,1)S(1)} %all_gather.3.mine_ref, bf16[128,3584]{1,0:T(8,128)(2,1)S(1)} %collective-permute-done.11.other_ref), custom_call_target="tpu_custom_call" | custom-call | tf_op jit(solution)/shard_map/pallas_call | solution.py:149
  111.7 0.1 reshape.19
  111.8 13.9 %all_to_all.11.returned_ref = bf16[8,4,3584]{2,1,0:T(4,128)(2,1)S(1)} all-to-all(bf16[8,4,3584]{2,1,0:T(4,128)(2,1)S(1)} %reshape.19), channel_id=1, replica_groups={{0,2,4,6,8,10,12,14},{1,3,5,7,9,11,13,15},{16,18,20,22,24,26,28,30},{17..., dimensions={0} | all-to-all | bytes 458752 | tf_op jit(solution)/shard_map/all_to_all | solution.py:201
  125.7 0.7 shard_map.63
  (11 shorter events, 0.4 us)
Async XLA Ops:
  0.6 1.8 %copy-start = (bf16[1,96,4,3584]{3,2,1,0:T(4,128)(2,1)S(1)}, bf16[1,96,4,3584]{3,2,1,0:T(4,128)(2,1)}, u32[]{:S(2)}) copy-start(bf16[1,96,4,3584]{3,2,1,0:T(4,128)(2,1)} %param.3) | copy-start | bytes 8257540
  2.4 19.4 %collective-permute-start = (bf16[8,4,3584]{2,1,0:T(4,128)(2,1)S(1)}, bf16[8,4,3584]{2,1,0:T(4,128)(2,1)S(1)}, u32[]{:S(2)}, u32[]{:S(2)}) collective-permute-start(bf16[8,4,3584]{2,1,0:T(4,128)(2,1)S(1)} %get-tuple-element.10), channel_id=1, source_target_pairs={{0,704},{64,0},{128,64},{192,128},{256,192},{320,256},{384,320},{4... | collective-permute-start | bytes 688136 | tf_op jit(solution)/shard_map/ppermute | solution.py:168
  17.6 9.6 %collective-permute-start.6 = (bf16[8,4,3584]{2,1,0:T(4,128)(2,1)S(1)}, bf16[8,4,3584]{2,1,0:T(4,128)(2,1)S(1)}, u32[]{:S(2)}, u32[]{:S(2)}) collective-permute-start(bf16[8,4,3584]{2,1,0:T(4,128)(2,1)S(1)} %get-tuple-element.11), channel_id=1, source_target_pairs={{0,64},{64,128},{128,192},{192,256},{256,320},{320,384},{384,448},... | collective-permute-start | bytes 688136 | tf_op jit(solution)/shard_map/ppermute | solution.py:168
  21.9 8.7 %collective-permute-start.1 = (bf16[8,4,3584]{2,1,0:T(4,128)(2,1)S(1)}, bf16[8,4,3584]{2,1,0:T(4,128)(2,1)S(1)}, u32[]{:S(2)}, u32[]{:S(2)}) collective-permute-start(bf16[8,4,3584]{2,1,0:T(4,128)(2,1)S(1)} %shard_map.51), channel_id=1, source_target_pairs={{0,704},{64,0},{128,64},{192,128},{256,192},{320,256},{384,320},{4... | collective-permute-start | bytes 688136 | tf_op jit(solution)/shard_map/ppermute | solution.py:168
  27.3 8.6 %collective-permute-start.7 = (bf16[8,4,3584]{2,1,0:T(4,128)(2,1)S(1)}, bf16[8,4,3584]{2,1,0:T(4,128)(2,1)S(1)}, u32[]{:S(2)}, u32[]{:S(2)}) collective-permute-start(bf16[8,4,3584]{2,1,0:T(4,128)(2,1)S(1)} %shard_map.56), channel_id=1, source_target_pairs={{0,64},{64,128},{128,192},{192,256},{256,320},{320,384},{384,448},... | collective-permute-start | bytes 688136 | tf_op jit(solution)/shard_map/ppermute | solution.py:168
  30.5 8.3 %collective-permute-start.2 = (bf16[8,4,3584]{2,1,0:T(4,128)(2,1)S(1)}, bf16[8,4,3584]{2,1,0:T(4,128)(2,1)S(1)}, u32[]{:S(2)}, u32[]{:S(2)}) collective-permute-start(bf16[8,4,3584]{2,1,0:T(4,128)(2,1)S(1)} %shard_map.52), channel_id=1, source_target_pairs={{0,704},{64,0},{128,64},{192,128},{256,192},{320,256},{384,320},{4... | collective-permute-start | bytes 688136 | tf_op jit(solution)/shard_map/ppermute | solution.py:168
  35.9 8.0 %collective-permute-start.8 = (bf16[8,4,3584]{2,1,0:T(4,128)(2,1)S(1)}, bf16[8,4,3584]{2,1,0:T(4,128)(2,1)S(1)}, u32[]{:S(2)}, u32[]{:S(2)}) collective-permute-start(bf16[8,4,3584]{2,1,0:T(4,128)(2,1)S(1)} %shard_map.57), channel_id=1, source_target_pairs={{0,64},{64,128},{128,192},{192,256},{256,320},{320,384},{384,448},... | collective-permute-start | bytes 688136 | tf_op jit(solution)/shard_map/ppermute | solution.py:168
  38.8 8.0 %collective-permute-start.3 = (bf16[8,4,3584]{2,1,0:T(4,128)(2,1)S(1)}, bf16[8,4,3584]{2,1,0:T(4,128)(2,1)S(1)}, u32[]{:S(2)}, u32[]{:S(2)}) collective-permute-start(bf16[8,4,3584]{2,1,0:T(4,128)(2,1)S(1)} %shard_map.53), channel_id=1, source_target_pairs={{0,704},{64,0},{128,64},{192,128},{256,192},{320,256},{384,320},{4... | collective-permute-start | bytes 688136 | tf_op jit(solution)/shard_map/ppermute | solution.py:168
  43.9 8.1 %collective-permute-start.9 = (bf16[8,4,3584]{2,1,0:T(4,128)(2,1)S(1)}, bf16[8,4,3584]{2,1,0:T(4,128)(2,1)S(1)}, u32[]{:S(2)}, u32[]{:S(2)}) collective-permute-start(bf16[8,4,3584]{2,1,0:T(4,128)(2,1)S(1)} %shard_map.58), channel_id=1, source_target_pairs={{0,64},{64,128},{128,192},{192,256},{256,320},{320,384},{384,448},... | collective-permute-start | bytes 688136 | tf_op jit(solution)/shard_map/ppermute | solution.py:168
  46.9 16.3 %copy-start.1 = (f32[8,4,3584]{2,1,0:T(4,128)S(1)}, f32[8,4,3584]{2,1,0:T(4,128)}, u32[]{:S(2)}) copy-start(f32[8,4,3584]{2,1,0:T(4,128)} %momentum_ref.1) | copy-start | bytes 1376260
  46.9 8.1 %collective-permute-start.4 = (bf16[8,4,3584]{2,1,0:T(4,128)(2,1)S(1)}, bf16[8,4,3584]{2,1,0:T(4,128)(2,1)S(1)}, u32[]{:S(2)}, u32[]{:S(2)}) collective-permute-start(bf16[8,4,3584]{2,1,0:T(4,128)(2,1)S(1)} %shard_map.54), channel_id=1, source_target_pairs={{0,704},{64,0},{128,64},{192,128},{256,192},{320,256},{384,320},{4... | collective-permute-start | bytes 688136 | tf_op jit(solution)/shard_map/ppermute | solution.py:168
  52.1 8.1 %collective-permute-start.10 = (bf16[8,4,3584]{2,1,0:T(4,128)(2,1)S(1)}, bf16[8,4,3584]{2,1,0:T(4,128)(2,1)S(1)}, u32[]{:S(2)}, u32[]{:S(2)}) collective-permute-start(bf16[8,4,3584]{2,1,0:T(4,128)(2,1)S(1)} %shard_map.59), channel_id=1, source_target_pairs={{0,64},{64,128},{128,192},{192,256},{256,320},{320,384},{384,448},... | collective-permute-start | bytes 688136 | tf_op jit(solution)/shard_map/ppermute | solution.py:168
  55.0 48.7 %copy-start.2 = (s32[8,4,896]{2,1,0:T(4,128)S(1)}, s32[8,4,896]{2,1,0:T(4,128)}, u32[]{:S(2)}) copy-start(s32[8,4,896]{2,1,0:T(4,128)} %param.5) | copy-start | bytes 344068
  55.0 8.1 %collective-permute-start.5 = (bf16[8,4,3584]{2,1,0:T(4,128)(2,1)S(1)}, bf16[8,4,3584]{2,1,0:T(4,128)(2,1)S(1)}, u32[]{:S(2)}, u32[]{:S(2)}) collective-permute-start(bf16[8,4,3584]{2,1,0:T(4,128)(2,1)S(1)} %shard_map.55), channel_id=1, source_target_pairs={{0,704},{64,0},{128,64},{192,128},{256,192},{320,256},{384,320},{4... | collective-permute-start | bytes 688136 | tf_op jit(solution)/shard_map/ppermute | solution.py:168
  91.0 14.8 %collective-permute-start.11 = (bf16[128,3584]{1,0:T(8,128)(2,1)S(1)}, bf16[128,3584]{1,0:T(8,128)(2,1)S(1)}, u32[]{:S(2)}, u32[]{:S(2)}) collective-permute-start(bf16[128,3584]{1,0:T(8,128)(2,1)S(1)} %all_gather.3.mine_ref), channel_id=1, source_target_pairs={{0,1},{1,0},{2,3},{3,2},{4,5},{5,4},{6,7},{7,6},{8,9},{9,8},{10,11... | collective-permute-start | bytes 2752520 | tf_op jit(solution)/shard_map/ppermute | solution.py:187

commit v6 on v5

--- a/solution.py
+++ b/solution.py
@@ -50,14 +50,17 @@
     group = lax.broadcasted_iota(jnp.int32, (128, 512), 0)
     column = lax.broadcasted_iota(jnp.int32, (128, 512), 1)
     spread = jnp.where((column >> 2) == group, 1.0, 0.0).astype(BF)
-    place = lax.broadcasted_iota(jnp.int32, (32, 512), 1) & 3
+    place = lax.broadcasted_iota(jnp.int32, (MATS_HERE * PIECE_ROWS, 512), 1) & 3
     for block in range(7):
-        code = codes_ref[:, block * 128 : (block + 1) * 128]
+        here = slice(block * 128, (block + 1) * 128)
+        code = jnp.concatenate([codes_ref[matrix, :, here] for matrix in range(MATS_HERE)], axis=0)
         pair = jnp.where(code == 0, 3, jnp.where(code == 1, 5, jnp.where(code == 2, 9, 0)))
         pair = jnp.where(code == 3, 6, jnp.where(code == 4, 10, jnp.where(code == 5, 12, pair)))
         wide = jnp.dot(pair.astype(F32).astype(BF), spread, preferred_element_type=F32).astype(jnp.int32)
         kept = ((wide >> place) & 1).astype(F32) * UPDATE_SCALE
-        mask_ref[:, block * 512 : (block + 1) * 512] = kept.astype(BF)
+        for matrix in range(MATS_HERE):
+            rows = kept[matrix * PIECE_ROWS : (matrix + 1) * PIECE_ROWS]
+            mask_ref[matrix, :, block * 512 : (block + 1) * 512] = rows.astype(BF)
 
 
 def chunk_start(offset):
@@ -78,14 +81,18 @@
         total_ref[matrix] = received_ref[matrix] + grad_ref[start + matrix]
 
 
-def momentum_kernel(grad_ref, down_ref, up_ref, momentum_ref, next_ref, out_ref):
+def momentum_kernel(grad_ref, down_ref, up_ref, momentum_ref, *refs):
+    out_ref = refs[-1]
     start = chunk_start(0)
     for matrix in range(MATS_HERE):
         own = grad_ref[start + matrix].astype(F32)
         summed = down_ref[matrix].astype(F32) + up_ref[matrix].astype(F32) + own
-        value = DECAY_RATE * momentum_ref[matrix] + summed
-        next_ref[matrix] = value
-        out_ref[matrix] = value.astype(BF)
+        out_ref[matrix] = (DECAY_RATE * momentum_ref[matrix] + summed).astype(out_ref.dtype)
+
+
+def merge_kernel(pieces_ref, rows_ref):
+    pieces = [pieces_ref[source].astype(F32) for source in range(PLANE_Y)]
+    rows_ref[...] = jnp.concatenate(pieces, axis=0).astype(BF)
 
 
 def split(value):
@@ -100,18 +107,23 @@
     return one(left[0], right[0]) + (one(left[0], right[1]) + one(left[1], right[0]))
 
 
-def orthogonal_kernel(mine_ref, other_ref, out_ref, coef_ref):
+def gram_block(a, b):
+    return lax.dot_general(a, b, NT, preferred_element_type=F32)
+
+
+def own_gram_kernel(mine_ref, own_ref):
+    mine = mine_ref[...]
+    own_ref[...] = gram_block(mine, mine)
+
+
+def orthogonal_kernel(own_ref, mine_ref, other_ref, out_ref, square_ref):
     mine = mine_ref[...]
     other = other_ref[...]
-
-    def block(a, b):
-        return lax.dot_general(a, b, NT, preferred_element_type=F32)
-
-    cross = block(mine, other)
+    cross = gram_block(mine, other)
     gram = jnp.concatenate(
         [
-            jnp.concatenate([block(mine, mine), cross], axis=1),
-            jnp.concatenate([cross.T, block(other, other)], axis=1),
+            jnp.concatenate([own_ref[...], cross], axis=1),
+            jnp.concatenate([cross.T, gram_block(other, other)], axis=1),
         ],
         axis=0,
     )
@@ -123,17 +135,23 @@
     square_form = scaled
     factor = None
     factor_scaled = split(scaled)
-    for iteration in range(ITERS):
+    for iteration in range(ITERS - 1):
         parts = split(square_form)
         polynomial = split(first + QUINTIC_SECOND * square_form + QUINTIC_THIRD * product(parts, parts))
         factor = polynomial if factor is None else split(product(polynomial, factor))
-        if iteration + 1 < ITERS:
-            factor_scaled = split(product(polynomial, factor_scaled))
-            square_form = product(factor_scaled, factor, NT)
-    coef_ref[...] = (factor[0].astype(F32) + factor[1].astype(F32)) * inverse
-    place_x = lax.div(lax.axis_index("shard"), PLANE_Y * CORES)
-    rows = pl.ds(pl.multiple_of(place_x * OWN_ROWS, OWN_ROWS), OWN_ROWS)
-    coef = coef_ref[rows, :].astype(BF)
+        factor_scaled = split(product(polynomial, factor_scaled))
+        square_form = product(factor_scaled, factor, NT)
+    start = pl.multiple_of(lax.div(lax.axis_index("shard"), PLANE_Y * CORES) * OWN_ROWS, OWN_ROWS)
+    square_ref[...] = square_form
+    own = square_ref[pl.ds(start, OWN_ROWS), :]
+    column = lax.broadcasted_iota(jnp.int32, (OWN_ROWS, ROWS), 1)
+    row = lax.broadcasted_iota(jnp.int32, (OWN_ROWS, ROWS), 0) + start
+    polynomial = split(
+        jnp.where(row == column, QUINTIC_FIRST, 0.0)
+        + QUINTIC_SECOND * own
+        + QUINTIC_THIRD * product(split(own), split(square_form))
+    )
+    coef = (product(polynomial, factor) * inverse).astype(BF)
     out_ref[...] = (
         jnp.dot(coef[:, :HALF], mine, preferred_element_type=F32)
         + jnp.dot(coef[:, HALF:], other, preferred_element_type=F32)
@@ -178,22 +196,23 @@
         down = send(add(step - below, down), -1)
         if step < above:
             up = send(add(above - step, up), 1)
-    momentum_next, outgoing = call(momentum_kernel, (shaped(CHUNK, F32), chunk), grads, down, up, momentum)
-    pieces = lax.all_to_all(
-        outgoing, "shard", split_axis=0, concat_axis=0, tiled=True, axis_index_groups=GROUPS_Y
-    ).reshape(OWN_ROWS, COLS)
+        if step == 2:
+            up, codes = lax.optimization_barrier((up, mask_codes))
+            mask = call(mask_kernel, chunk, codes)
+        if step == 4:
+            up, mask = lax.optimization_barrier((up, mask))
+    outgoing = call(momentum_kernel, chunk, grads, down, up, momentum)
+    pieces = lax.all_to_all(outgoing, "shard", split_axis=0, concat_axis=0, tiled=True, axis_index_groups=GROUPS_Y)
+    pieces = call(merge_kernel, shaped((OWN_ROWS, COLS), BF), pieces)
     mine = lax.all_gather(pieces, "shard", axis=0, tiled=True, axis_index_groups=GROUPS_X)
-    mine, codes = lax.optimization_barrier((mine, mask_codes))
     other = lax.ppermute(mine, "shard", OTHER_CORE)
-    mask = call(
-        mask_kernel,
-        shaped((MATS_HERE * PIECE_ROWS, COLS), BF),
-        codes.reshape(MATS_HERE * PIECE_ROWS, COLS // 4),
-    ).reshape(CHUNK)
-    other, mask = lax.optimization_barrier((other, mask))
+    own_gram = call(own_gram_kernel, shaped((HALF, HALF), F32), mine)
+    momentum_next = call(momentum_kernel, shaped(CHUNK, F32), grads, down, up, momentum, own_gram)
+    other, own_gram, momentum_next = lax.optimization_barrier((other, own_gram, momentum_next))
     orthogonal = call(
         orthogonal_kernel,
         shaped((OWN_ROWS, COLS), BF),
+        own_gram,
         mine,
         other,
         scratch=[pltpu.VMEM((ROWS, ROWS), F32)],

time: 127 us -> 126 us (level)
    pallas_call x14 -> x17, Pallas kernels: 8.11 us -> 7.98 us  [call(): pl.pallas_call(kernel, out_shape=outs, in_specs=[vmem() for _ in args], o...]
  transfers between devices with their start and end apart: 12 -> 12, of which waited for: 7 -> 7; matrix products, arithmetic and copies ran while one was open for 0% -> 0% of each run, Pallas kernels for 0% -> 1%
where the time goes in v6:
time: 126 us; the launch traced here: 125 us
  starting transfers between devices  63.4 us (50%)
  blocking collectives  40.9 us (32%)
  waiting for transfers between devices  9.97 us (8%)
  Pallas kernels  7.98 us (6%)
  local copies, waits for them, and re-layouts  1.86 us (1%)
    ppermute x11, starting transfers between devices, send(): lax.ppermute(value, 'rep', [(i, (i + step) % REPS) for i in range(REPS)])  50.7 us
    all_to_all x1, blocking collectives, local(): lax.all_to_all(outgoing, 'shard', split_axis=0, concat_axis=0, tiled=True...  15.6 us
    all_to_all x1, blocking collectives, local(): lax.all_to_all(orthogonal.reshape(CHUNK), 'shard', split_axis=0, concat_a...  14 us
    ppermute x1, starting transfers between devices, local(): other = lax.ppermute(mine, 'shard', OTHER_CORE)  12.7 us
    all_gather x1, blocking collectives, local(): lax.all_gather(pieces, 'shard', axis=0, tiled=True, axis_index_groups=GRO...  11.3 us
    ppermute x11, waiting for transfers between devices, send(): lax.ppermute(value, 'rep', [(i, (i + step) % REPS) for i in range(REPS)])  9.18 us
    pallas_call x17, Pallas kernels, call(): pl.pallas_call(kernel, out_shape=outs, in_specs=[vmem() for _ in args], o...  7.98 us
  transfers between devices with their start and end apart: 12, of which 7 were waited for; matrix products, arithmetic and copies ran while one was open for 0% of the time, Pallas kernels for 1%

profile of v6, /device:TPU:1, one launch (start us, length us, event | category | flops | bytes accessed | tf_op | source)
XLA Modules:
  0.0 125.0 jit_solution(2471000879300174355)
XLA Ops:
  0.6 0.0 copy-start
  0.6 1.8 %copy-done = bf16[1,96,4,3584]{3,2,1,0:T(4,128)(2,1)S(1)} copy-done((bf16[1,96,4,3584]{3,2,1,0:T(4,128)(2,1)S(1)}, bf16[1,96,4,3584]{3,2,1,0:T(4,128)(2,1)}, u32[]{:S(2)}) %copy-start) | copy-done | bytes 2752536
  2.4 15.1 %collective-permute-start = (bf16[8,4,3584]{2,1,0:T(4,128)(2,1)S(1)}, bf16[8,4,3584]{2,1,0:T(4,128)(2,1)S(1)}, u32[]{:S(2)}, u32[]{:S(2)}) collective-permute-start(bf16[8,4,3584]{2,1,0:T(4,128)(2,1)S(1)} %get-tuple-element.11), channel_id=1, source_target_pairs={{0,704},{64,0},{128,64},{192,128},{256,192},{320,256},{384,320},{4... | collective-permute-start | bytes 688136 | tf_op jit(solution)/shard_map/ppermute | solution.py:186
  17.6 1.9 %collective-permute-start.6 = (bf16[8,4,3584]{2,1,0:T(4,128)(2,1)S(1)}, bf16[8,4,3584]{2,1,0:T(4,128)(2,1)S(1)}, u32[]{:S(2)}, u32[]{:S(2)}) collective-permute-start(bf16[8,4,3584]{2,1,0:T(4,128)(2,1)S(1)} %get-tuple-element.12), channel_id=1, source_target_pairs={{0,64},{64,128},{128,192},{192,256},{256,320},{320,384},{384,448},... | collective-permute-start | bytes 688136 | tf_op jit(solution)/shard_map/ppermute | solution.py:186
  19.5 2.3 %collective-permute-done.received_ref = bf16[8,4,3584]{2,1,0:T(4,128)(2,1)S(1)} collective-permute-done((bf16[8,4,3584]{2,1,0:T(4,128)(2,1)S(1)}, bf16[8,4,3584]{2,1,0:T(4,128)(2,1)S(1)}, u32[]{:S(2)}, u32[]{:S(2)}) %collective-permute-start) | collective-permute-done | bytes 229408 | tf_op jit(solution)/shard_map/ppermute | solution.py:186
  21.9 5.3 %collective-permute-start.1 = (bf16[8,4,3584]{2,1,0:T(4,128)(2,1)S(1)}, bf16[8,4,3584]{2,1,0:T(4,128)(2,1)S(1)}, u32[]{:S(2)}, u32[]{:S(2)}) collective-permute-start(bf16[8,4,3584]{2,1,0:T(4,128)(2,1)S(1)} %shard_map.51), channel_id=1, source_target_pairs={{0,704},{64,0},{128,64},{192,128},{256,192},{320,256},{384,320},{4... | collective-permute-start | bytes 688136 | tf_op jit(solution)/shard_map/ppermute | solution.py:186
  27.2 0.0 collective-permute-done.6.received_ref
  27.3 1.9 %collective-permute-start.7 = (bf16[8,4,3584]{2,1,0:T(4,128)(2,1)S(1)}, bf16[8,4,3584]{2,1,0:T(4,128)(2,1)S(1)}, u32[]{:S(2)}, u32[]{:S(2)}) collective-permute-start(bf16[8,4,3584]{2,1,0:T(4,128)(2,1)S(1)} %shard_map.56), channel_id=1, source_target_pairs={{0,64},{64,128},{128,192},{192,256},{256,320},{320,384},{384,448},... | collective-permute-start | bytes 688136 | tf_op jit(solution)/shard_map/ppermute | solution.py:186
  29.2 1.3 %collective-permute-done.1.received_ref = bf16[8,4,3584]{2,1,0:T(4,128)(2,1)S(1)} collective-permute-done((bf16[8,4,3584]{2,1,0:T(4,128)(2,1)S(1)}, bf16[8,4,3584]{2,1,0:T(4,128)(2,1)S(1)}, u32[]{:S(2)}, u32[]{:S(2)}) %collective-permute-start.1) | collective-permute-done | bytes 229408 | tf_op jit(solution)/shard_map/ppermute | solution.py:186
  30.6 5.3 %collective-permute-start.2 = (bf16[8,4,3584]{2,1,0:T(4,128)(2,1)S(1)}, bf16[8,4,3584]{2,1,0:T(4,128)(2,1)S(1)}, u32[]{:S(2)}, u32[]{:S(2)}) collective-permute-start(bf16[8,4,3584]{2,1,0:T(4,128)(2,1)S(1)} %shard_map.52), channel_id=1, source_target_pairs={{0,704},{64,0},{128,64},{192,128},{256,192},{320,256},{384,320},{4... | collective-permute-start | bytes 688136 | tf_op jit(solution)/shard_map/ppermute | solution.py:186
  35.9 0.0 collective-permute-done.7.received_ref
  35.9 1.9 %collective-permute-start.8 = (bf16[8,4,3584]{2,1,0:T(4,128)(2,1)S(1)}, bf16[8,4,3584]{2,1,0:T(4,128)(2,1)S(1)}, u32[]{:S(2)}, u32[]{:S(2)}) collective-permute-start(bf16[8,4,3584]{2,1,0:T(4,128)(2,1)S(1)} %shard_map.57), channel_id=1, source_target_pairs={{0,64},{64,128},{128,192},{192,256},{256,320},{320,384},{384,448},... | collective-permute-start | bytes 688136 | tf_op jit(solution)/shard_map/ppermute | solution.py:186
  37.9 1.0 collective-permute-done.2.received_ref
  38.9 5.0 %collective-permute-start.3 = (bf16[8,4,3584]{2,1,0:T(4,128)(2,1)S(1)}, bf16[8,4,3584]{2,1,0:T(4,128)(2,1)S(1)}, u32[]{:S(2)}, u32[]{:S(2)}) collective-permute-start(bf16[8,4,3584]{2,1,0:T(4,128)(2,1)S(1)} %shard_map.53), channel_id=1, source_target_pairs={{0,704},{64,0},{128,64},{192,128},{256,192},{320,256},{384,320},{4... | collective-permute-start | bytes 688136 | tf_op jit(solution)/shard_map/ppermute | solution.py:186
  43.9 0.0 collective-permute-done.8.received_ref
  43.9 1.9 %collective-permute-start.9 = (bf16[8,4,3584]{2,1,0:T(4,128)(2,1)S(1)}, bf16[8,4,3584]{2,1,0:T(4,128)(2,1)S(1)}, u32[]{:S(2)}, u32[]{:S(2)}) collective-permute-start(bf16[8,4,3584]{2,1,0:T(4,128)(2,1)S(1)} %shard_map.58), channel_id=1, source_target_pairs={{0,64},{64,128},{128,192},{192,256},{256,320},{320,384},{384,448},... | collective-permute-start | bytes 688136 | tf_op jit(solution)/shard_map/ppermute | solution.py:186
  45.9 1.0 collective-permute-done.3.received_ref
  46.9 0.0 copy-start.3
  46.9 0.0 copy-start.1
  46.9 0.0 copy-start.2
  46.9 5.3 %collective-permute-start.4 = (bf16[8,4,3584]{2,1,0:T(4,128)(2,1)S(1)}, bf16[8,4,3584]{2,1,0:T(4,128)(2,1)S(1)}, u32[]{:S(2)}, u32[]{:S(2)}) collective-permute-start(bf16[8,4,3584]{2,1,0:T(4,128)(2,1)S(1)} %shard_map.54), channel_id=1, source_target_pairs={{0,704},{64,0},{128,64},{192,128},{256,192},{320,256},{384,320},{4... | collective-permute-start | bytes 688136 | tf_op jit(solution)/shard_map/ppermute | solution.py:186
  52.2 0.0 collective-permute-done.9.received_ref
  52.3 1.9 %collective-permute-start.10 = (bf16[8,4,3584]{2,1,0:T(4,128)(2,1)S(1)}, bf16[8,4,3584]{2,1,0:T(4,128)(2,1)S(1)}, u32[]{:S(2)}, u32[]{:S(2)}) collective-permute-start(bf16[8,4,3584]{2,1,0:T(4,128)(2,1)S(1)} %shard_map.59), channel_id=1, source_target_pairs={{0,64},{64,128},{128,192},{192,256},{256,320},{320,384},{384,448},... | collective-permute-start | bytes 688136 | tf_op jit(solution)/shard_map/ppermute | solution.py:186
  54.2 1.0 collective-permute-done.4.received_ref
  55.2 5.0 %collective-permute-start.5 = (bf16[8,4,3584]{2,1,0:T(4,128)(2,1)S(1)}, bf16[8,4,3584]{2,1,0:T(4,128)(2,1)S(1)}, u32[]{:S(2)}, u32[]{:S(2)}) collective-permute-start(bf16[8,4,3584]{2,1,0:T(4,128)(2,1)S(1)} %shard_map.55), channel_id=1, source_target_pairs={{0,704},{64,0},{128,64},{192,128},{256,192},{320,256},{384,320},{4... | collective-permute-start | bytes 688136 | tf_op jit(solution)/shard_map/ppermute | solution.py:186
  60.2 0.0 copy-done.3
  60.2 0.3 shard_map.60.mask_ref
  60.5 0.0 collective-permute-done.10.up_ref
  60.5 2.6 %collective-permute-done.5.down_ref = bf16[8,4,3584]{2,1,0:T(4,128)(2,1)S(1)} collective-permute-done((bf16[8,4,3584]{2,1,0:T(4,128)(2,1)S(1)}, bf16[8,4,3584]{2,1,0:T(4,128)(2,1)S(1)}, u32[]{:S(2)}, u32[]{:S(2)}) %collective-permute-start.5) | collective-permute-done | bytes 229408 | tf_op jit(solution)/shard_map/ppermute | solution.py:186
  63.1 0.0 copy-done.1
  63.1 0.0 copy-done.2
  63.1 0.2 shard_map.61
  63.3 15.6 %all_to_all.10.pieces_ref = bf16[8,4,3584]{2,1,0:T(4,128)(2,1)S(1)} all-to-all(bf16[8,4,3584]{2,1,0:T(4,128)(2,1)S(1)} %shard_map.61), channel_id=1, replica_groups={{0,2,4,6,8,10,12,14},{1,3,5,7,9,11,13,15},{16,18,20,22,24,26,28,30},{17..., dimensions={0} | all-to-all | bytes 458752 | tf_op jit(solution)/shard_map/all_to_all | solution.py:205
  78.9 0.1 shard_map.62
  79.0 11.3 %all_gather.3.mine_ref = bf16[128,3584]{1,0:T(8,128)(2,1)S(1)} all-gather(bf16[32,3584]{1,0:T(8,128)(2,1)S(1)} %shard_map.62), channel_id=1, replica_groups={{0,16,32,48},{1,17,33,49},{2,18,34,50},{3,19,35,51},{4,20,36,52},{5,21,..., dimensions={0}, use_global_device_ids=true | all-gather | bytes 1146880 | tf_op jit(solution)/shard_map/all_gather | solution.py:207
  90.3 12.7 %collective-permute-start.11 = (bf16[128,3584]{1,0:T(8,128)(2,1)S(1)}, bf16[128,3584]{1,0:T(8,128)(2,1)S(1)}, u32[]{:S(2)}, u32[]{:S(2)}) collective-permute-start(bf16[128,3584]{1,0:T(8,128)(2,1)S(1)} %all_gather.3.mine_ref), channel_id=1, source_target_pairs={{0,1},{1,0},{2,3},{3,2},{4,5},{5,4},{6,7},{7,6},{8,9},{9,8},{10,11... | collective-permute-start | bytes 2752520 | tf_op jit(solution)/shard_map/ppermute | solution.py:208
  103.0 0.4 shard_map.63.refs_0_.own_ref
  103.4 0.9 shard_map.64
  104.3 0.8 collective-permute-done.11.other_ref
  105.1 5.2 %shard_map.65 = bf16[32,3584]{1,0:T(8,128)(2,1)S(1)} custom-call(f32[128,128]{1,0:T(8,128)S(1)} %shard_map.63.refs_0_.own_ref, bf16[128,3584]{1,0:T(8,128)(2,1)S(1)} %all_gather.3.mine_ref, bf16[128,3584]{1,0:T(8,128)(2,1)S(1)} %collective-permute-done.11.other_ref), custom_call_target="tpu_custom_call" | custom-call | tf_op jit(solution)/shard_map/pallas_call | solution.py:167
  110.2 0.1 reshape.7
  110.3 14.0 %all_to_all.11.returned_ref = bf16[8,4,3584]{2,1,0:T(4,128)(2,1)S(1)} all-to-all(bf16[8,4,3584]{2,1,0:T(4,128)(2,1)S(1)} %reshape.7), channel_id=1, replica_groups={{0,2,4,6,8,10,12,14},{1,3,5,7,9,11,13,15},{16,18,20,22,24,26,28,30},{17..., dimensions={0} | all-to-all | bytes 458752 | tf_op jit(solution)/shard_map/all_to_all | solution.py:220
  124.3 0.7 shard_map.66
  (10 shorter events, 0.3 us)
Async XLA Ops:
  0.6 1.8 %copy-start = (bf16[1,96,4,3584]{3,2,1,0:T(4,128)(2,1)S(1)}, bf16[1,96,4,3584]{3,2,1,0:T(4,128)(2,1)}, u32[]{:S(2)}) copy-start(bf16[1,96,4,3584]{3,2,1,0:T(4,128)(2,1)} %param.3) | copy-start | bytes 8257540
  2.4 19.4 %collective-permute-start = (bf16[8,4,3584]{2,1,0:T(4,128)(2,1)S(1)}, bf16[8,4,3584]{2,1,0:T(4,128)(2,1)S(1)}, u32[]{:S(2)}, u32[]{:S(2)}) collective-permute-start(bf16[8,4,3584]{2,1,0:T(4,128)(2,1)S(1)} %get-tuple-element.11), channel_id=1, source_target_pairs={{0,704},{64,0},{128,64},{192,128},{256,192},{320,256},{384,320},{4... | collective-permute-start | bytes 688136 | tf_op jit(solution)/shard_map/ppermute | solution.py:186
  17.6 9.6 %collective-permute-start.6 = (bf16[8,4,3584]{2,1,0:T(4,128)(2,1)S(1)}, bf16[8,4,3584]{2,1,0:T(4,128)(2,1)S(1)}, u32[]{:S(2)}, u32[]{:S(2)}) collective-permute-start(bf16[8,4,3584]{2,1,0:T(4,128)(2,1)S(1)} %get-tuple-element.12), channel_id=1, source_target_pairs={{0,64},{64,128},{128,192},{192,256},{256,320},{320,384},{384,448},... | collective-permute-start | bytes 688136 | tf_op jit(solution)/shard_map/ppermute | solution.py:186
  21.9 8.7 %collective-permute-start.1 = (bf16[8,4,3584]{2,1,0:T(4,128)(2,1)S(1)}, bf16[8,4,3584]{2,1,0:T(4,128)(2,1)S(1)}, u32[]{:S(2)}, u32[]{:S(2)}) collective-permute-start(bf16[8,4,3584]{2,1,0:T(4,128)(2,1)S(1)} %shard_map.51), channel_id=1, source_target_pairs={{0,704},{64,0},{128,64},{192,128},{256,192},{320,256},{384,320},{4... | collective-permute-start | bytes 688136 | tf_op jit(solution)/shard_map/ppermute | solution.py:186
  27.3 8.6 %collective-permute-start.7 = (bf16[8,4,3584]{2,1,0:T(4,128)(2,1)S(1)}, bf16[8,4,3584]{2,1,0:T(4,128)(2,1)S(1)}, u32[]{:S(2)}, u32[]{:S(2)}) collective-permute-start(bf16[8,4,3584]{2,1,0:T(4,128)(2,1)S(1)} %shard_map.56), channel_id=1, source_target_pairs={{0,64},{64,128},{128,192},{192,256},{256,320},{320,384},{384,448},... | collective-permute-start | bytes 688136 | tf_op jit(solution)/shard_map/ppermute | solution.py:186
  30.6 8.3 %collective-permute-start.2 = (bf16[8,4,3584]{2,1,0:T(4,128)(2,1)S(1)}, bf16[8,4,3584]{2,1,0:T(4,128)(2,1)S(1)}, u32[]{:S(2)}, u32[]{:S(2)}) collective-permute-start(bf16[8,4,3584]{2,1,0:T(4,128)(2,1)S(1)} %shard_map.52), channel_id=1, source_target_pairs={{0,704},{64,0},{128,64},{192,128},{256,192},{320,256},{384,320},{4... | collective-permute-start | bytes 688136 | tf_op jit(solution)/shard_map/ppermute | solution.py:186
  35.9 8.0 %collective-permute-start.8 = (bf16[8,4,3584]{2,1,0:T(4,128)(2,1)S(1)}, bf16[8,4,3584]{2,1,0:T(4,128)(2,1)S(1)}, u32[]{:S(2)}, u32[]{:S(2)}) collective-permute-start(bf16[8,4,3584]{2,1,0:T(4,128)(2,1)S(1)} %shard_map.57), channel_id=1, source_target_pairs={{0,64},{64,128},{128,192},{192,256},{256,320},{320,384},{384,448},... | collective-permute-start | bytes 688136 | tf_op jit(solution)/shard_map/ppermute | solution.py:186
  38.9 8.0 %collective-permute-start.3 = (bf16[8,4,3584]{2,1,0:T(4,128)(2,1)S(1)}, bf16[8,4,3584]{2,1,0:T(4,128)(2,1)S(1)}, u32[]{:S(2)}, u32[]{:S(2)}) collective-permute-start(bf16[8,4,3584]{2,1,0:T(4,128)(2,1)S(1)} %shard_map.53), channel_id=1, source_target_pairs={{0,704},{64,0},{128,64},{192,128},{256,192},{320,256},{384,320},{4... | collective-permute-start | bytes 688136 | tf_op jit(solution)/shard_map/ppermute | solution.py:186
  43.9 8.2 %collective-permute-start.9 = (bf16[8,4,3584]{2,1,0:T(4,128)(2,1)S(1)}, bf16[8,4,3584]{2,1,0:T(4,128)(2,1)S(1)}, u32[]{:S(2)}, u32[]{:S(2)}) collective-permute-start(bf16[8,4,3584]{2,1,0:T(4,128)(2,1)S(1)} %shard_map.58), channel_id=1, source_target_pairs={{0,64},{64,128},{128,192},{192,256},{256,320},{320,384},{384,448},... | collective-permute-start | bytes 688136 | tf_op jit(solution)/shard_map/ppermute | solution.py:186
  46.9 13.3 %copy-start.3 = (s32[8,4,896]{2,1,0:T(4,128)S(1)}, s32[8,4,896]{2,1,0:T(4,128)}, u32[]{:S(2)}) copy-start(s32[8,4,896]{2,1,0:T(4,128)} %codes_ref) | copy-start | bytes 344068
  46.9 16.3 %copy-start.1 = (bf16[1,96,4,3584]{3,2,1,0:T(4,128)(2,1)S(1)}, bf16[1,96,4,3584]{3,2,1,0:T(4,128)(2,1)}, u32[]{:S(2)}) copy-start(bf16[1,96,4,3584]{3,2,1,0:T(4,128)(2,1)} %param.3) | copy-start | bytes 8257540
  46.9 16.3 %copy-start.2 = (f32[8,4,3584]{2,1,0:T(4,128)S(1)}, f32[8,4,3584]{2,1,0:T(4,128)}, u32[]{:S(2)}) copy-start(f32[8,4,3584]{2,1,0:T(4,128)} %momentum_ref.3) | copy-start | bytes 1376260
  46.9 8.2 %collective-permute-start.4 = (bf16[8,4,3584]{2,1,0:T(4,128)(2,1)S(1)}, bf16[8,4,3584]{2,1,0:T(4,128)(2,1)S(1)}, u32[]{:S(2)}, u32[]{:S(2)}) collective-permute-start(bf16[8,4,3584]{2,1,0:T(4,128)(2,1)S(1)} %shard_map.54), channel_id=1, source_target_pairs={{0,704},{64,0},{128,64},{192,128},{256,192},{320,256},{384,320},{4... | collective-permute-start | bytes 688136 | tf_op jit(solution)/shard_map/ppermute | solution.py:186
  52.3 8.3 %collective-permute-start.10 = (bf16[8,4,3584]{2,1,0:T(4,128)(2,1)S(1)}, bf16[8,4,3584]{2,1,0:T(4,128)(2,1)S(1)}, u32[]{:S(2)}, u32[]{:S(2)}) collective-permute-start(bf16[8,4,3584]{2,1,0:T(4,128)(2,1)S(1)} %shard_map.59), channel_id=1, source_target_pairs={{0,64},{64,128},{128,192},{192,256},{256,320},{320,384},{384,448},... | collective-permute-start | bytes 688136 | tf_op jit(solution)/shard_map/ppermute | solution.py:186
  55.2 8.0 %collective-permute-start.5 = (bf16[8,4,3584]{2,1,0:T(4,128)(2,1)S(1)}, bf16[8,4,3584]{2,1,0:T(4,128)(2,1)S(1)}, u32[]{:S(2)}, u32[]{:S(2)}) collective-permute-start(bf16[8,4,3584]{2,1,0:T(4,128)(2,1)S(1)} %shard_map.55), channel_id=1, source_target_pairs={{0,704},{64,0},{128,64},{192,128},{256,192},{320,256},{384,320},{4... | collective-permute-start | bytes 688136 | tf_op jit(solution)/shard_map/ppermute | solution.py:186
  90.3 14.8 %collective-permute-start.11 = (bf16[128,3584]{1,0:T(8,128)(2,1)S(1)}, bf16[128,3584]{1,0:T(8,128)(2,1)S(1)}, u32[]{:S(2)}, u32[]{:S(2)}) collective-permute-start(bf16[128,3584]{1,0:T(8,128)(2,1)S(1)} %all_gather.3.mine_ref), channel_id=1, source_target_pairs={{0,1},{1,0},{2,3},{3,2},{4,5},{5,4},{6,7},{7,6},{8,9},{9,8},{10,11... | collective-permute-start | bytes 2752520 | tf_op jit(solution)/shard_map/ppermute | solution.py:208

commit v7 on v6

--- a/solution.py
+++ b/solution.py
@@ -119,11 +119,12 @@
 def orthogonal_kernel(own_ref, mine_ref, other_ref, out_ref, square_ref):
     mine = mine_ref[...]
     other = other_ref[...]
-    cross = gram_block(mine, other)
+    beside = gram_block(jnp.concatenate([mine, other], axis=0), other)
+    cross = beside[:HALF]
     gram = jnp.concatenate(
         [
             jnp.concatenate([own_ref[...], cross], axis=1),
-            jnp.concatenate([cross.T, gram_block(other, other)], axis=1),
+            jnp.concatenate([cross.T, beside[HALF:]], axis=1),
         ],
         axis=0,
     )
@@ -152,10 +153,11 @@
         + QUINTIC_THIRD * product(split(own), split(square_form))
     )
     coef = (product(polynomial, factor) * inverse).astype(BF)
-    out_ref[...] = (
-        jnp.dot(coef[:, :HALF], mine, preferred_element_type=F32)
-        + jnp.dot(coef[:, HALF:], other, preferred_element_type=F32)
-    ).astype(BF)
+    own_rows = jnp.dot(coef[:, :HALF], mine, preferred_element_type=F32) + jnp.dot(
+        coef[:, HALF:], other, preferred_element_type=F32
+    )
+    for target in range(PLANE_Y):
+        out_ref[target] = own_rows[target * PIECE_ROWS : (target + 1) * PIECE_ROWS].astype(BF)
 
 
 def update_kernel(returned_ref, mask_ref, update_ref):
@@ -211,14 +213,14 @@
     other, own_gram, momentum_next = lax.optimization_barrier((other, own_gram, momentum_next))
     orthogonal = call(
         orthogonal_kernel,
-        shaped((OWN_ROWS, COLS), BF),
+        chunk,
         own_gram,
         mine,
         other,
         scratch=[pltpu.VMEM((ROWS, ROWS), F32)],
     )
     returned = lax.all_to_all(
-        orthogonal.reshape(CHUNK), "shard", split_axis=0, concat_axis=0, tiled=True, axis_index_groups=GROUPS_Y
+        orthogonal, "shard", split_axis=0, concat_axis=0, tiled=True, axis_index_groups=GROUPS_Y
     )
     update = call(update_kernel, chunk, returned, mask)
     return (momentum_next, update)

time: 126 us -> 126 us (level)
  no operation moved by 1% of the time
where the time goes in v7:
time: 126 us; the launch traced here: 125 us
  starting transfers between devices  63.4 us (50%)
  blocking collectives  40.9 us (32%)
  waiting for transfers between devices  9.97 us (8%)
  Pallas kernels  8.47 us (7%)
  local copies, waits for them, and re-layouts  1.79 us (1%)
    ppermute x11, starting transfers between devices, send(): lax.ppermute(value, 'rep', [(i, (i + step) % REPS) for i in range(REPS)])  50.7 us
    all_to_all x1, blocking collectives, local(): lax.all_to_all(outgoing, 'shard', split_axis=0, concat_axis=0, tiled=True...  15.6 us
    all_to_all x1, blocking collectives, local(): lax.all_to_all(orthogonal, 'shard', split_axis=0, concat_axis=0, tiled=Tr...  14 us
    ppermute x1, starting transfers between devices, local(): other = lax.ppermute(mine, 'shard', OTHER_CORE)  12.7 us
    all_gather x1, blocking collectives, local(): lax.all_gather(pieces, 'shard', axis=0, tiled=True, axis_index_groups=GRO...  11.3 us
    ppermute x11, waiting for transfers between devices, send(): lax.ppermute(value, 'rep', [(i, (i + step) % REPS) for i in range(REPS)])  9.18 us
    pallas_call x17, Pallas kernels, call(): pl.pallas_call(kernel, out_shape=outs, in_specs=[vmem() for _ in args], o...  8.47 us
  transfers between devices with their start and end apart: 12, of which 7 were waited for; matrix products, arithmetic and copies ran while one was open for 0% of the time, Pallas kernels for 1%

profile of v7, /device:TPU:1, one launch (start us, length us, event | category | flops | bytes accessed | tf_op | source)
XLA Modules:
  0.0 125.4 jit_solution(14648308331952678064)
XLA Ops:
  0.6 0.0 copy-start
  0.6 1.8 %copy-done = bf16[1,96,4,3584]{3,2,1,0:T(4,128)(2,1)S(1)} copy-done((bf16[1,96,4,3584]{3,2,1,0:T(4,128)(2,1)S(1)}, bf16[1,96,4,3584]{3,2,1,0:T(4,128)(2,1)}, u32[]{:S(2)}) %copy-start) | copy-done | bytes 2752536
  2.4 15.1 %collective-permute-start = (bf16[8,4,3584]{2,1,0:T(4,128)(2,1)S(1)}, bf16[8,4,3584]{2,1,0:T(4,128)(2,1)S(1)}, u32[]{:S(2)}, u32[]{:S(2)}) collective-permute-start(bf16[8,4,3584]{2,1,0:T(4,128)(2,1)S(1)} %get-tuple-element.11), channel_id=1, source_target_pairs={{0,704},{64,0},{128,64},{192,128},{256,192},{320,256},{384,320},{4... | collective-permute-start | bytes 688136 | tf_op jit(solution)/shard_map/ppermute | solution.py:188
  17.6 1.9 %collective-permute-start.6 = (bf16[8,4,3584]{2,1,0:T(4,128)(2,1)S(1)}, bf16[8,4,3584]{2,1,0:T(4,128)(2,1)S(1)}, u32[]{:S(2)}, u32[]{:S(2)}) collective-permute-start(bf16[8,4,3584]{2,1,0:T(4,128)(2,1)S(1)} %get-tuple-element.12), channel_id=1, source_target_pairs={{0,64},{64,128},{128,192},{192,256},{256,320},{320,384},{384,448},... | collective-permute-start | bytes 688136 | tf_op jit(solution)/shard_map/ppermute | solution.py:188
  19.5 2.3 %collective-permute-done.received_ref = bf16[8,4,3584]{2,1,0:T(4,128)(2,1)S(1)} collective-permute-done((bf16[8,4,3584]{2,1,0:T(4,128)(2,1)S(1)}, bf16[8,4,3584]{2,1,0:T(4,128)(2,1)S(1)}, u32[]{:S(2)}, u32[]{:S(2)}) %collective-permute-start) | collective-permute-done | bytes 229408 | tf_op jit(solution)/shard_map/ppermute | solution.py:188
  21.9 5.3 %collective-permute-start.1 = (bf16[8,4,3584]{2,1,0:T(4,128)(2,1)S(1)}, bf16[8,4,3584]{2,1,0:T(4,128)(2,1)S(1)}, u32[]{:S(2)}, u32[]{:S(2)}) collective-permute-start(bf16[8,4,3584]{2,1,0:T(4,128)(2,1)S(1)} %shard_map.51), channel_id=1, source_target_pairs={{0,704},{64,0},{128,64},{192,128},{256,192},{320,256},{384,320},{4... | collective-permute-start | bytes 688136 | tf_op jit(solution)/shard_map/ppermute | solution.py:188
  27.2 0.0 collective-permute-done.6.received_ref
  27.3 1.9 %collective-permute-start.7 = (bf16[8,4,3584]{2,1,0:T(4,128)(2,1)S(1)}, bf16[8,4,3584]{2,1,0:T(4,128)(2,1)S(1)}, u32[]{:S(2)}, u32[]{:S(2)}) collective-permute-start(bf16[8,4,3584]{2,1,0:T(4,128)(2,1)S(1)} %shard_map.56), channel_id=1, source_target_pairs={{0,64},{64,128},{128,192},{192,256},{256,320},{320,384},{384,448},... | collective-permute-start | bytes 688136 | tf_op jit(solution)/shard_map/ppermute | solution.py:188
  29.2 1.3 %collective-permute-done.1.received_ref = bf16[8,4,3584]{2,1,0:T(4,128)(2,1)S(1)} collective-permute-done((bf16[8,4,3584]{2,1,0:T(4,128)(2,1)S(1)}, bf16[8,4,3584]{2,1,0:T(4,128)(2,1)S(1)}, u32[]{:S(2)}, u32[]{:S(2)}) %collective-permute-start.1) | collective-permute-done | bytes 229408 | tf_op jit(solution)/shard_map/ppermute | solution.py:188
  30.6 5.3 %collective-permute-start.2 = (bf16[8,4,3584]{2,1,0:T(4,128)(2,1)S(1)}, bf16[8,4,3584]{2,1,0:T(4,128)(2,1)S(1)}, u32[]{:S(2)}, u32[]{:S(2)}) collective-permute-start(bf16[8,4,3584]{2,1,0:T(4,128)(2,1)S(1)} %shard_map.52), channel_id=1, source_target_pairs={{0,704},{64,0},{128,64},{192,128},{256,192},{320,256},{384,320},{4... | collective-permute-start | bytes 688136 | tf_op jit(solution)/shard_map/ppermute | solution.py:188
  35.9 0.0 collective-permute-done.7.received_ref
  35.9 1.9 %collective-permute-start.8 = (bf16[8,4,3584]{2,1,0:T(4,128)(2,1)S(1)}, bf16[8,4,3584]{2,1,0:T(4,128)(2,1)S(1)}, u32[]{:S(2)}, u32[]{:S(2)}) collective-permute-start(bf16[8,4,3584]{2,1,0:T(4,128)(2,1)S(1)} %shard_map.57), channel_id=1, source_target_pairs={{0,64},{64,128},{128,192},{192,256},{256,320},{320,384},{384,448},... | collective-permute-start | bytes 688136 | tf_op jit(solution)/shard_map/ppermute | solution.py:188
  37.9 1.0 collective-permute-done.2.received_ref
  38.9 5.0 %collective-permute-start.3 = (bf16[8,4,3584]{2,1,0:T(4,128)(2,1)S(1)}, bf16[8,4,3584]{2,1,0:T(4,128)(2,1)S(1)}, u32[]{:S(2)}, u32[]{:S(2)}) collective-permute-start(bf16[8,4,3584]{2,1,0:T(4,128)(2,1)S(1)} %shard_map.53), channel_id=1, source_target_pairs={{0,704},{64,0},{128,64},{192,128},{256,192},{320,256},{384,320},{4... | collective-permute-start | bytes 688136 | tf_op jit(solution)/shard_map/ppermute | solution.py:188
  43.9 0.0 collective-permute-done.8.received_ref
  43.9 1.9 %collective-permute-start.9 = (bf16[8,4,3584]{2,1,0:T(4,128)(2,1)S(1)}, bf16[8,4,3584]{2,1,0:T(4,128)(2,1)S(1)}, u32[]{:S(2)}, u32[]{:S(2)}) collective-permute-start(bf16[8,4,3584]{2,1,0:T(4,128)(2,1)S(1)} %shard_map.58), channel_id=1, source_target_pairs={{0,64},{64,128},{128,192},{192,256},{256,320},{320,384},{384,448},... | collective-permute-start | bytes 688136 | tf_op jit(solution)/shard_map/ppermute | solution.py:188
  45.9 1.0 collective-permute-done.3.received_ref
  46.9 0.0 copy-start.3
  46.9 0.0 copy-start.1
  46.9 0.0 copy-start.2
  46.9 5.3 %collective-permute-start.4 = (bf16[8,4,3584]{2,1,0:T(4,128)(2,1)S(1)}, bf16[8,4,3584]{2,1,0:T(4,128)(2,1)S(1)}, u32[]{:S(2)}, u32[]{:S(2)}) collective-permute-start(bf16[8,4,3584]{2,1,0:T(4,128)(2,1)S(1)} %shard_map.54), channel_id=1, source_target_pairs={{0,704},{64,0},{128,64},{192,128},{256,192},{320,256},{384,320},{4... | collective-permute-start | bytes 688136 | tf_op jit(solution)/shard_map/ppermute | solution.py:188
  52.2 0.0 collective-permute-done.9.received_ref
  52.3 1.9 %collective-permute-start.10 = (bf16[8,4,3584]{2,1,0:T(4,128)(2,1)S(1)}, bf16[8,4,3584]{2,1,0:T(4,128)(2,1)S(1)}, u32[]{:S(2)}, u32[]{:S(2)}) collective-permute-start(bf16[8,4,3584]{2,1,0:T(4,128)(2,1)S(1)} %shard_map.59), channel_id=1, source_target_pairs={{0,64},{64,128},{128,192},{192,256},{256,320},{320,384},{384,448},... | collective-permute-start | bytes 688136 | tf_op jit(solution)/shard_map/ppermute | solution.py:188
  54.2 1.0 collective-permute-done.4.received_ref
  55.2 5.0 %collective-permute-start.5 = (bf16[8,4,3584]{2,1,0:T(4,128)(2,1)S(1)}, bf16[8,4,3584]{2,1,0:T(4,128)(2,1)S(1)}, u32[]{:S(2)}, u32[]{:S(2)}) collective-permute-start(bf16[8,4,3584]{2,1,0:T(4,128)(2,1)S(1)} %shard_map.55), channel_id=1, source_target_pairs={{0,704},{64,0},{128,64},{192,128},{256,192},{320,256},{384,320},{4... | collective-permute-start | bytes 688136 | tf_op jit(solution)/shard_map/ppermute | solution.py:188
  60.2 0.0 copy-done.3
  60.2 0.3 shard_map.60.mask_ref
  60.5 0.0 collective-permute-done.10.up_ref
  60.5 2.6 %collective-permute-done.5.down_ref = bf16[8,4,3584]{2,1,0:T(4,128)(2,1)S(1)} collective-permute-done((bf16[8,4,3584]{2,1,0:T(4,128)(2,1)S(1)}, bf16[8,4,3584]{2,1,0:T(4,128)(2,1)S(1)}, u32[]{:S(2)}, u32[]{:S(2)}) %collective-permute-start.5) | collective-permute-done | bytes 229408 | tf_op jit(solution)/shard_map/ppermute | solution.py:188
  63.1 0.0 copy-done.1
  63.1 0.0 copy-done.2
  63.1 0.2 shard_map.61
  63.3 15.6 %all_to_all.10.pieces_ref = bf16[8,4,3584]{2,1,0:T(4,128)(2,1)S(1)} all-to-all(bf16[8,4,3584]{2,1,0:T(4,128)(2,1)S(1)} %shard_map.61), channel_id=1, replica_groups={{0,2,4,6,8,10,12,14},{1,3,5,7,9,11,13,15},{16,18,20,22,24,26,28,30},{17..., dimensions={0} | all-to-all | bytes 458752 | tf_op jit(solution)/shard_map/all_to_all | solution.py:207
  78.9 0.1 shard_map.62
  79.0 11.3 %all_gather.3.mine_ref = bf16[128,3584]{1,0:T(8,128)(2,1)S(1)} all-gather(bf16[32,3584]{1,0:T(8,128)(2,1)S(1)} %shard_map.62), channel_id=1, replica_groups={{0,16,32,48},{1,17,33,49},{2,18,34,50},{3,19,35,51},{4,20,36,52},{5,21,..., dimensions={0}, use_global_device_ids=true | all-gather | bytes 1146880 | tf_op jit(solution)/shard_map/all_gather | solution.py:209
  90.3 12.7 %collective-permute-start.11 = (bf16[128,3584]{1,0:T(8,128)(2,1)S(1)}, bf16[128,3584]{1,0:T(8,128)(2,1)S(1)}, u32[]{:S(2)}, u32[]{:S(2)}) collective-permute-start(bf16[128,3584]{1,0:T(8,128)(2,1)S(1)} %all_gather.3.mine_ref), channel_id=1, source_target_pairs={{0,1},{1,0},{2,3},{3,2},{4,5},{5,4},{6,7},{7,6},{8,9},{9,8},{10,11... | collective-permute-start | bytes 2752520 | tf_op jit(solution)/shard_map/ppermute | solution.py:210
  103.0 0.4 shard_map.63.refs_0_.own_ref
  103.4 0.9 shard_map.64
  104.3 0.8 collective-permute-done.11.other_ref
  105.1 5.6 %shard_map.65 = bf16[8,4,3584]{2,1,0:T(4,128)(2,1)S(1)} custom-call(f32[128,128]{1,0:T(8,128)S(1)} %shard_map.63.refs_0_.own_ref, bf16[128,3584]{1,0:T(8,128)(2,1)S(1)} %all_gather.3.mine_ref, bf16[128,3584]{1,0:T(8,128)(2,1)S(1)} %collective-permute-done.11.other_ref), custom_call_target="tpu_custom_call" | custom-call | tf_op jit(solution)/shard_map/pallas_call | solution.py:169
  110.7 14.0 %all_to_all.11.returned_ref = bf16[8,4,3584]{2,1,0:T(4,128)(2,1)S(1)} all-to-all(bf16[8,4,3584]{2,1,0:T(4,128)(2,1)S(1)} %shard_map.65), channel_id=1, replica_groups={{0,2,4,6,8,10,12,14},{1,3,5,7,9,11,13,15},{16,18,20,22,24,26,28,30},{17..., dimensions={0} | all-to-all | bytes 458752 | tf_op jit(solution)/shard_map/all_to_all | solution.py:222
  124.7 0.7 shard_map.66
  (10 shorter events, 0.3 us)
Async XLA Ops:
  0.6 1.8 %copy-start = (bf16[1,96,4,3584]{3,2,1,0:T(4,128)(2,1)S(1)}, bf16[1,96,4,3584]{3,2,1,0:T(4,128)(2,1)}, u32[]{:S(2)}) copy-start(bf16[1,96,4,3584]{3,2,1,0:T(4,128)(2,1)} %param.3) | copy-start | bytes 8257540
  2.4 19.4 %collective-permute-start = (bf16[8,4,3584]{2,1,0:T(4,128)(2,1)S(1)}, bf16[8,4,3584]{2,1,0:T(4,128)(2,1)S(1)}, u32[]{:S(2)}, u32[]{:S(2)}) collective-permute-start(bf16[8,4,3584]{2,1,0:T(4,128)(2,1)S(1)} %get-tuple-element.11), channel_id=1, source_target_pairs={{0,704},{64,0},{128,64},{192,128},{256,192},{320,256},{384,320},{4... | collective-permute-start | bytes 688136 | tf_op jit(solution)/shard_map/ppermute | solution.py:188
  17.6 9.6 %collective-permute-start.6 = (bf16[8,4,3584]{2,1,0:T(4,128)(2,1)S(1)}, bf16[8,4,3584]{2,1,0:T(4,128)(2,1)S(1)}, u32[]{:S(2)}, u32[]{:S(2)}) collective-permute-start(bf16[8,4,3584]{2,1,0:T(4,128)(2,1)S(1)} %get-tuple-element.12), channel_id=1, source_target_pairs={{0,64},{64,128},{128,192},{192,256},{256,320},{320,384},{384,448},... | collective-permute-start | bytes 688136 | tf_op jit(solution)/shard_map/ppermute | solution.py:188
  21.9 8.7 %collective-permute-start.1 = (bf16[8,4,3584]{2,1,0:T(4,128)(2,1)S(1)}, bf16[8,4,3584]{2,1,0:T(4,128)(2,1)S(1)}, u32[]{:S(2)}, u32[]{:S(2)}) collective-permute-start(bf16[8,4,3584]{2,1,0:T(4,128)(2,1)S(1)} %shard_map.51), channel_id=1, source_target_pairs={{0,704},{64,0},{128,64},{192,128},{256,192},{320,256},{384,320},{4... | collective-permute-start | bytes 688136 | tf_op jit(solution)/shard_map/ppermute | solution.py:188
  27.3 8.6 %collective-permute-start.7 = (bf16[8,4,3584]{2,1,0:T(4,128)(2,1)S(1)}, bf16[8,4,3584]{2,1,0:T(4,128)(2,1)S(1)}, u32[]{:S(2)}, u32[]{:S(2)}) collective-permute-start(bf16[8,4,3584]{2,1,0:T(4,128)(2,1)S(1)} %shard_map.56), channel_id=1, source_target_pairs={{0,64},{64,128},{128,192},{192,256},{256,320},{320,384},{384,448},... | collective-permute-start | bytes 688136 | tf_op jit(solution)/shard_map/ppermute | solution.py:188
  30.6 8.3 %collective-permute-start.2 = (bf16[8,4,3584]{2,1,0:T(4,128)(2,1)S(1)}, bf16[8,4,3584]{2,1,0:T(4,128)(2,1)S(1)}, u32[]{:S(2)}, u32[]{:S(2)}) collective-permute-start(bf16[8,4,3584]{2,1,0:T(4,128)(2,1)S(1)} %shard_map.52), channel_id=1, source_target_pairs={{0,704},{64,0},{128,64},{192,128},{256,192},{320,256},{384,320},{4... | collective-permute-start | bytes 688136 | tf_op jit(solution)/shard_map/ppermute | solution.py:188
  35.9 8.0 %collective-permute-start.8 = (bf16[8,4,3584]{2,1,0:T(4,128)(2,1)S(1)}, bf16[8,4,3584]{2,1,0:T(4,128)(2,1)S(1)}, u32[]{:S(2)}, u32[]{:S(2)}) collective-permute-start(bf16[8,4,3584]{2,1,0:T(4,128)(2,1)S(1)} %shard_map.57), channel_id=1, source_target_pairs={{0,64},{64,128},{128,192},{192,256},{256,320},{320,384},{384,448},... | collective-permute-start | bytes 688136 | tf_op jit(solution)/shard_map/ppermute | solution.py:188
  38.9 8.0 %collective-permute-start.3 = (bf16[8,4,3584]{2,1,0:T(4,128)(2,1)S(1)}, bf16[8,4,3584]{2,1,0:T(4,128)(2,1)S(1)}, u32[]{:S(2)}, u32[]{:S(2)}) collective-permute-start(bf16[8,4,3584]{2,1,0:T(4,128)(2,1)S(1)} %shard_map.53), channel_id=1, source_target_pairs={{0,704},{64,0},{128,64},{192,128},{256,192},{320,256},{384,320},{4... | collective-permute-start | bytes 688136 | tf_op jit(solution)/shard_map/ppermute | solution.py:188
  43.9 8.2 %collective-permute-start.9 = (bf16[8,4,3584]{2,1,0:T(4,128)(2,1)S(1)}, bf16[8,4,3584]{2,1,0:T(4,128)(2,1)S(1)}, u32[]{:S(2)}, u32[]{:S(2)}) collective-permute-start(bf16[8,4,3584]{2,1,0:T(4,128)(2,1)S(1)} %shard_map.58), channel_id=1, source_target_pairs={{0,64},{64,128},{128,192},{192,256},{256,320},{320,384},{384,448},... | collective-permute-start | bytes 688136 | tf_op jit(solution)/shard_map/ppermute | solution.py:188
  46.9 13.3 %copy-start.3 = (s32[8,4,896]{2,1,0:T(4,128)S(1)}, s32[8,4,896]{2,1,0:T(4,128)}, u32[]{:S(2)}) copy-start(s32[8,4,896]{2,1,0:T(4,128)} %codes_ref) | copy-start | bytes 344068
  46.9 16.3 %copy-start.1 = (bf16[1,96,4,3584]{3,2,1,0:T(4,128)(2,1)S(1)}, bf16[1,96,4,3584]{3,2,1,0:T(4,128)(2,1)}, u32[]{:S(2)}) copy-start(bf16[1,96,4,3584]{3,2,1,0:T(4,128)(2,1)} %param.3) | copy-start | bytes 8257540
  46.9 16.3 %copy-start.2 = (f32[8,4,3584]{2,1,0:T(4,128)S(1)}, f32[8,4,3584]{2,1,0:T(4,128)}, u32[]{:S(2)}) copy-start(f32[8,4,3584]{2,1,0:T(4,128)} %momentum_ref.3) | copy-start | bytes 1376260
  46.9 8.2 %collective-permute-start.4 = (bf16[8,4,3584]{2,1,0:T(4,128)(2,1)S(1)}, bf16[8,4,3584]{2,1,0:T(4,128)(2,1)S(1)}, u32[]{:S(2)}, u32[]{:S(2)}) collective-permute-start(bf16[8,4,3584]{2,1,0:T(4,128)(2,1)S(1)} %shard_map.54), channel_id=1, source_target_pairs={{0,704},{64,0},{128,64},{192,128},{256,192},{320,256},{384,320},{4... | collective-permute-start | bytes 688136 | tf_op jit(solution)/shard_map/ppermute | solution.py:188
  52.3 8.3 %collective-permute-start.10 = (bf16[8,4,3584]{2,1,0:T(4,128)(2,1)S(1)}, bf16[8,4,3584]{2,1,0:T(4,128)(2,1)S(1)}, u32[]{:S(2)}, u32[]{:S(2)}) collective-permute-start(bf16[8,4,3584]{2,1,0:T(4,128)(2,1)S(1)} %shard_map.59), channel_id=1, source_target_pairs={{0,64},{64,128},{128,192},{192,256},{256,320},{320,384},{384,448},... | collective-permute-start | bytes 688136 | tf_op jit(solution)/shard_map/ppermute | solution.py:188
  55.2 8.0 %collective-permute-start.5 = (bf16[8,4,3584]{2,1,0:T(4,128)(2,1)S(1)}, bf16[8,4,3584]{2,1,0:T(4,128)(2,1)S(1)}, u32[]{:S(2)}, u32[]{:S(2)}) collective-permute-start(bf16[8,4,3584]{2,1,0:T(4,128)(2,1)S(1)} %shard_map.55), channel_id=1, source_target_pairs={{0,704},{64,0},{128,64},{192,128},{256,192},{320,256},{384,320},{4... | collective-permute-start | bytes 688136 | tf_op jit(solution)/shard_map/ppermute | solution.py:188
  90.3 14.8 %collective-permute-start.11 = (bf16[128,3584]{1,0:T(8,128)(2,1)S(1)}, bf16[128,3584]{1,0:T(8,128)(2,1)S(1)}, u32[]{:S(2)}, u32[]{:S(2)}) collective-permute-start(bf16[128,3584]{1,0:T(8,128)(2,1)S(1)} %all_gather.3.mine_ref), channel_id=1, source_target_pairs={{0,1},{1,0},{2,3},{3,2},{4,5},{5,4},{6,7},{7,6},{8,9},{9,8},{10,11... | collective-permute-start | bytes 2752520 | tf_op jit(solution)/shard_map/ppermute | solution.py:210

commit v8 on v6

--- a/solution.py
+++ b/solution.py
@@ -119,11 +119,12 @@
 def orthogonal_kernel(own_ref, mine_ref, other_ref, out_ref, square_ref):
     mine = mine_ref[...]
     other = other_ref[...]
-    cross = gram_block(mine, other)
+    beside = gram_block(jnp.concatenate([mine, other], axis=0), other)
+    cross = beside[:HALF]
     gram = jnp.concatenate(
         [
             jnp.concatenate([own_ref[...], cross], axis=1),
-            jnp.concatenate([cross.T, gram_block(other, other)], axis=1),
+            jnp.concatenate([cross.T, beside[HALF:]], axis=1),
         ],
         axis=0,
     )

time: 126 us -> 126 us (level)
  no operation moved by 1% of the time
where the time goes in v8:
time: 126 us; the launch traced here: 125 us
  starting transfers between devices  63.4 us (50%)
  blocking collectives  40.9 us (32%)
  waiting for transfers between devices  9.97 us (8%)
  Pallas kernels  8.47 us (7%)
  local copies, waits for them, and re-layouts  1.86 us (1%)
    ppermute x11, starting transfers between devices, send(): lax.ppermute(value, 'rep', [(i, (i + step) % REPS) for i in range(REPS)])  50.7 us
    all_to_all x1, blocking collectives, local(): lax.all_to_all(outgoing, 'shard', split_axis=0, concat_axis=0, tiled=True...  15.6 us
    all_to_all x1, blocking collectives, local(): lax.all_to_all(orthogonal.reshape(CHUNK), 'shard', split_axis=0, concat_a...  14 us
    ppermute x1, starting transfers between devices, local(): other = lax.ppermute(mine, 'shard', OTHER_CORE)  12.7 us
    all_gather x1, blocking collectives, local(): lax.all_gather(pieces, 'shard', axis=0, tiled=True, axis_index_groups=GRO...  11.3 us
    ppermute x11, waiting for transfers between devices, send(): lax.ppermute(value, 'rep', [(i, (i + step) % REPS) for i in range(REPS)])  9.18 us
    pallas_call x17, Pallas kernels, call(): pl.pallas_call(kernel, out_shape=outs, in_specs=[vmem() for _ in args], o...  8.47 us
  transfers between devices with their start and end apart: 12, of which 7 were waited for; matrix products, arithmetic and copies ran while one was open for 0% of the time, Pallas kernels for 1%

profile of v8, /device:TPU:1, one launch (start us, length us, event | category | flops | bytes accessed | tf_op | source)
XLA Modules:
  0.0 125.5 jit_solution(2109130517980189115)
XLA Ops:
  0.6 0.0 copy-start
  0.6 1.8 %copy-done = bf16[1,96,4,3584]{3,2,1,0:T(4,128)(2,1)S(1)} copy-done((bf16[1,96,4,3584]{3,2,1,0:T(4,128)(2,1)S(1)}, bf16[1,96,4,3584]{3,2,1,0:T(4,128)(2,1)}, u32[]{:S(2)}) %copy-start) | copy-done | bytes 2752536
  2.4 15.1 %collective-permute-start = (bf16[8,4,3584]{2,1,0:T(4,128)(2,1)S(1)}, bf16[8,4,3584]{2,1,0:T(4,128)(2,1)S(1)}, u32[]{:S(2)}, u32[]{:S(2)}) collective-permute-start(bf16[8,4,3584]{2,1,0:T(4,128)(2,1)S(1)} %get-tuple-element.11), channel_id=1, source_target_pairs={{0,704},{64,0},{128,64},{192,128},{256,192},{320,256},{384,320},{4... | collective-permute-start | bytes 688136 | tf_op jit(solution)/shard_map/ppermute | solution.py:187
  17.6 1.9 %collective-permute-start.6 = (bf16[8,4,3584]{2,1,0:T(4,128)(2,1)S(1)}, bf16[8,4,3584]{2,1,0:T(4,128)(2,1)S(1)}, u32[]{:S(2)}, u32[]{:S(2)}) collective-permute-start(bf16[8,4,3584]{2,1,0:T(4,128)(2,1)S(1)} %get-tuple-element.12), channel_id=1, source_target_pairs={{0,64},{64,128},{128,192},{192,256},{256,320},{320,384},{384,448},... | collective-permute-start | bytes 688136 | tf_op jit(solution)/shard_map/ppermute | solution.py:187
  19.5 2.3 %collective-permute-done.received_ref = bf16[8,4,3584]{2,1,0:T(4,128)(2,1)S(1)} collective-permute-done((bf16[8,4,3584]{2,1,0:T(4,128)(2,1)S(1)}, bf16[8,4,3584]{2,1,0:T(4,128)(2,1)S(1)}, u32[]{:S(2)}, u32[]{:S(2)}) %collective-permute-start) | collective-permute-done | bytes 229408 | tf_op jit(solution)/shard_map/ppermute | solution.py:187
  21.9 5.3 %collective-permute-start.1 = (bf16[8,4,3584]{2,1,0:T(4,128)(2,1)S(1)}, bf16[8,4,3584]{2,1,0:T(4,128)(2,1)S(1)}, u32[]{:S(2)}, u32[]{:S(2)}) collective-permute-start(bf16[8,4,3584]{2,1,0:T(4,128)(2,1)S(1)} %shard_map.51), channel_id=1, source_target_pairs={{0,704},{64,0},{128,64},{192,128},{256,192},{320,256},{384,320},{4... | collective-permute-start | bytes 688136 | tf_op jit(solution)/shard_map/ppermute | solution.py:187
  27.2 0.0 collective-permute-done.6.received_ref
  27.3 1.9 %collective-permute-start.7 = (bf16[8,4,3584]{2,1,0:T(4,128)(2,1)S(1)}, bf16[8,4,3584]{2,1,0:T(4,128)(2,1)S(1)}, u32[]{:S(2)}, u32[]{:S(2)}) collective-permute-start(bf16[8,4,3584]{2,1,0:T(4,128)(2,1)S(1)} %shard_map.56), channel_id=1, source_target_pairs={{0,64},{64,128},{128,192},{192,256},{256,320},{320,384},{384,448},... | collective-permute-start | bytes 688136 | tf_op jit(solution)/shard_map/ppermute | solution.py:187
  29.2 1.3 %collective-permute-done.1.received_ref = bf16[8,4,3584]{2,1,0:T(4,128)(2,1)S(1)} collective-permute-done((bf16[8,4,3584]{2,1,0:T(4,128)(2,1)S(1)}, bf16[8,4,3584]{2,1,0:T(4,128)(2,1)S(1)}, u32[]{:S(2)}, u32[]{:S(2)}) %collective-permute-start.1) | collective-permute-done | bytes 229408 | tf_op jit(solution)/shard_map/ppermute | solution.py:187
  30.6 5.3 %collective-permute-start.2 = (bf16[8,4,3584]{2,1,0:T(4,128)(2,1)S(1)}, bf16[8,4,3584]{2,1,0:T(4,128)(2,1)S(1)}, u32[]{:S(2)}, u32[]{:S(2)}) collective-permute-start(bf16[8,4,3584]{2,1,0:T(4,128)(2,1)S(1)} %shard_map.52), channel_id=1, source_target_pairs={{0,704},{64,0},{128,64},{192,128},{256,192},{320,256},{384,320},{4... | collective-permute-start | bytes 688136 | tf_op jit(solution)/shard_map/ppermute | solution.py:187
  35.9 0.0 collective-permute-done.7.received_ref
  35.9 1.9 %collective-permute-start.8 = (bf16[8,4,3584]{2,1,0:T(4,128)(2,1)S(1)}, bf16[8,4,3584]{2,1,0:T(4,128)(2,1)S(1)}, u32[]{:S(2)}, u32[]{:S(2)}) collective-permute-start(bf16[8,4,3584]{2,1,0:T(4,128)(2,1)S(1)} %shard_map.57), channel_id=1, source_target_pairs={{0,64},{64,128},{128,192},{192,256},{256,320},{320,384},{384,448},... | collective-permute-start | bytes 688136 | tf_op jit(solution)/shard_map/ppermute | solution.py:187
  37.9 1.0 collective-permute-done.2.received_ref
  38.9 5.0 %collective-permute-start.3 = (bf16[8,4,3584]{2,1,0:T(4,128)(2,1)S(1)}, bf16[8,4,3584]{2,1,0:T(4,128)(2,1)S(1)}, u32[]{:S(2)}, u32[]{:S(2)}) collective-permute-start(bf16[8,4,3584]{2,1,0:T(4,128)(2,1)S(1)} %shard_map.53), channel_id=1, source_target_pairs={{0,704},{64,0},{128,64},{192,128},{256,192},{320,256},{384,320},{4... | collective-permute-start | bytes 688136 | tf_op jit(solution)/shard_map/ppermute | solution.py:187
  43.9 0.0 collective-permute-done.8.received_ref
  43.9 1.9 %collective-permute-start.9 = (bf16[8,4,3584]{2,1,0:T(4,128)(2,1)S(1)}, bf16[8,4,3584]{2,1,0:T(4,128)(2,1)S(1)}, u32[]{:S(2)}, u32[]{:S(2)}) collective-permute-start(bf16[8,4,3584]{2,1,0:T(4,128)(2,1)S(1)} %shard_map.58), channel_id=1, source_target_pairs={{0,64},{64,128},{128,192},{192,256},{256,320},{320,384},{384,448},... | collective-permute-start | bytes 688136 | tf_op jit(solution)/shard_map/ppermute | solution.py:187
  45.9 1.0 collective-permute-done.3.received_ref
  46.9 0.0 copy-start.3
  46.9 0.0 copy-start.1
  46.9 0.0 copy-start.2
  46.9 5.3 %collective-permute-start.4 = (bf16[8,4,3584]{2,1,0:T(4,128)(2,1)S(1)}, bf16[8,4,3584]{2,1,0:T(4,128)(2,1)S(1)}, u32[]{:S(2)}, u32[]{:S(2)}) collective-permute-start(bf16[8,4,3584]{2,1,0:T(4,128)(2,1)S(1)} %shard_map.54), channel_id=1, source_target_pairs={{0,704},{64,0},{128,64},{192,128},{256,192},{320,256},{384,320},{4... | collective-permute-start | bytes 688136 | tf_op jit(solution)/shard_map/ppermute | solution.py:187
  52.2 0.0 collective-permute-done.9.received_ref
  52.3 1.9 %collective-permute-start.10 = (bf16[8,4,3584]{2,1,0:T(4,128)(2,1)S(1)}, bf16[8,4,3584]{2,1,0:T(4,128)(2,1)S(1)}, u32[]{:S(2)}, u32[]{:S(2)}) collective-permute-start(bf16[8,4,3584]{2,1,0:T(4,128)(2,1)S(1)} %shard_map.59), channel_id=1, source_target_pairs={{0,64},{64,128},{128,192},{192,256},{256,320},{320,384},{384,448},... | collective-permute-start | bytes 688136 | tf_op jit(solution)/shard_map/ppermute | solution.py:187
  54.2 1.0 collective-permute-done.4.received_ref
  55.2 5.0 %collective-permute-start.5 = (bf16[8,4,3584]{2,1,0:T(4,128)(2,1)S(1)}, bf16[8,4,3584]{2,1,0:T(4,128)(2,1)S(1)}, u32[]{:S(2)}, u32[]{:S(2)}) collective-permute-start(bf16[8,4,3584]{2,1,0:T(4,128)(2,1)S(1)} %shard_map.55), channel_id=1, source_target_pairs={{0,704},{64,0},{128,64},{192,128},{256,192},{320,256},{384,320},{4... | collective-permute-start | bytes 688136 | tf_op jit(solution)/shard_map/ppermute | solution.py:187
  60.2 0.0 copy-done.3
  60.2 0.3 shard_map.60.mask_ref
  60.5 0.0 collective-permute-done.10.up_ref
  60.5 2.6 %collective-permute-done.5.down_ref = bf16[8,4,3584]{2,1,0:T(4,128)(2,1)S(1)} collective-permute-done((bf16[8,4,3584]{2,1,0:T(4,128)(2,1)S(1)}, bf16[8,4,3584]{2,1,0:T(4,128)(2,1)S(1)}, u32[]{:S(2)}, u32[]{:S(2)}) %collective-permute-start.5) | collective-permute-done | bytes 229408 | tf_op jit(solution)/shard_map/ppermute | solution.py:187
  63.1 0.0 copy-done.1
  63.1 0.0 copy-done.2
  63.1 0.2 shard_map.61
  63.3 15.6 %all_to_all.10.pieces_ref = bf16[8,4,3584]{2,1,0:T(4,128)(2,1)S(1)} all-to-all(bf16[8,4,3584]{2,1,0:T(4,128)(2,1)S(1)} %shard_map.61), channel_id=1, replica_groups={{0,2,4,6,8,10,12,14},{1,3,5,7,9,11,13,15},{16,18,20,22,24,26,28,30},{17..., dimensions={0} | all-to-all | bytes 458752 | tf_op jit(solution)/shard_map/all_to_all | solution.py:206
  78.9 0.1 shard_map.62
  79.0 11.3 %all_gather.3.mine_ref = bf16[128,3584]{1,0:T(8,128)(2,1)S(1)} all-gather(bf16[32,3584]{1,0:T(8,128)(2,1)S(1)} %shard_map.62), channel_id=1, replica_groups={{0,16,32,48},{1,17,33,49},{2,18,34,50},{3,19,35,51},{4,20,36,52},{5,21,..., dimensions={0}, use_global_device_ids=true | all-gather | bytes 1146880 | tf_op jit(solution)/shard_map/all_gather | solution.py:208
  90.3 12.7 %collective-permute-start.11 = (bf16[128,3584]{1,0:T(8,128)(2,1)S(1)}, bf16[128,3584]{1,0:T(8,128)(2,1)S(1)}, u32[]{:S(2)}, u32[]{:S(2)}) collective-permute-start(bf16[128,3584]{1,0:T(8,128)(2,1)S(1)} %all_gather.3.mine_ref), channel_id=1, source_target_pairs={{0,1},{1,0},{2,3},{3,2},{4,5},{5,4},{6,7},{7,6},{8,9},{9,8},{10,11... | collective-permute-start | bytes 2752520 | tf_op jit(solution)/shard_map/ppermute | solution.py:209
  103.0 0.4 shard_map.63.refs_0_.own_ref
  103.4 0.9 shard_map.64
  104.3 0.8 collective-permute-done.11.other_ref
  105.1 5.6 %shard_map.65 = bf16[32,3584]{1,0:T(8,128)(2,1)S(1)} custom-call(f32[128,128]{1,0:T(8,128)S(1)} %shard_map.63.refs_0_.own_ref, bf16[128,3584]{1,0:T(8,128)(2,1)S(1)} %all_gather.3.mine_ref, bf16[128,3584]{1,0:T(8,128)(2,1)S(1)} %collective-permute-done.11.other_ref), custom_call_target="tpu_custom_call" | custom-call | tf_op jit(solution)/shard_map/pallas_call | solution.py:168
  110.7 0.1 reshape.7
  110.8 14.0 %all_to_all.11.returned_ref = bf16[8,4,3584]{2,1,0:T(4,128)(2,1)S(1)} all-to-all(bf16[8,4,3584]{2,1,0:T(4,128)(2,1)S(1)} %reshape.7), channel_id=1, replica_groups={{0,2,4,6,8,10,12,14},{1,3,5,7,9,11,13,15},{16,18,20,22,24,26,28,30},{17..., dimensions={0} | all-to-all | bytes 458752 | tf_op jit(solution)/shard_map/all_to_all | solution.py:221
  124.8 0.7 shard_map.66
  (10 shorter events, 0.3 us)
Async XLA Ops:
  0.6 1.8 %copy-start = (bf16[1,96,4,3584]{3,2,1,0:T(4,128)(2,1)S(1)}, bf16[1,96,4,3584]{3,2,1,0:T(4,128)(2,1)}, u32[]{:S(2)}) copy-start(bf16[1,96,4,3584]{3,2,1,0:T(4,128)(2,1)} %param.3) | copy-start | bytes 8257540
  2.4 19.4 %collective-permute-start = (bf16[8,4,3584]{2,1,0:T(4,128)(2,1)S(1)}, bf16[8,4,3584]{2,1,0:T(4,128)(2,1)S(1)}, u32[]{:S(2)}, u32[]{:S(2)}) collective-permute-start(bf16[8,4,3584]{2,1,0:T(4,128)(2,1)S(1)} %get-tuple-element.11), channel_id=1, source_target_pairs={{0,704},{64,0},{128,64},{192,128},{256,192},{320,256},{384,320},{4... | collective-permute-start | bytes 688136 | tf_op jit(solution)/shard_map/ppermute | solution.py:187
  17.6 9.6 %collective-permute-start.6 = (bf16[8,4,3584]{2,1,0:T(4,128)(2,1)S(1)}, bf16[8,4,3584]{2,1,0:T(4,128)(2,1)S(1)}, u32[]{:S(2)}, u32[]{:S(2)}) collective-permute-start(bf16[8,4,3584]{2,1,0:T(4,128)(2,1)S(1)} %get-tuple-element.12), channel_id=1, source_target_pairs={{0,64},{64,128},{128,192},{192,256},{256,320},{320,384},{384,448},... | collective-permute-start | bytes 688136 | tf_op jit(solution)/shard_map/ppermute | solution.py:187
  21.9 8.7 %collective-permute-start.1 = (bf16[8,4,3584]{2,1,0:T(4,128)(2,1)S(1)}, bf16[8,4,3584]{2,1,0:T(4,128)(2,1)S(1)}, u32[]{:S(2)}, u32[]{:S(2)}) collective-permute-start(bf16[8,4,3584]{2,1,0:T(4,128)(2,1)S(1)} %shard_map.51), channel_id=1, source_target_pairs={{0,704},{64,0},{128,64},{192,128},{256,192},{320,256},{384,320},{4... | collective-permute-start | bytes 688136 | tf_op jit(solution)/shard_map/ppermute | solution.py:187
  27.3 8.6 %collective-permute-start.7 = (bf16[8,4,3584]{2,1,0:T(4,128)(2,1)S(1)}, bf16[8,4,3584]{2,1,0:T(4,128)(2,1)S(1)}, u32[]{:S(2)}, u32[]{:S(2)}) collective-permute-start(bf16[8,4,3584]{2,1,0:T(4,128)(2,1)S(1)} %shard_map.56), channel_id=1, source_target_pairs={{0,64},{64,128},{128,192},{192,256},{256,320},{320,384},{384,448},... | collective-permute-start | bytes 688136 | tf_op jit(solution)/shard_map/ppermute | solution.py:187
  30.6 8.3 %collective-permute-start.2 = (bf16[8,4,3584]{2,1,0:T(4,128)(2,1)S(1)}, bf16[8,4,3584]{2,1,0:T(4,128)(2,1)S(1)}, u32[]{:S(2)}, u32[]{:S(2)}) collective-permute-start(bf16[8,4,3584]{2,1,0:T(4,128)(2,1)S(1)} %shard_map.52), channel_id=1, source_target_pairs={{0,704},{64,0},{128,64},{192,128},{256,192},{320,256},{384,320},{4... | collective-permute-start | bytes 688136 | tf_op jit(solution)/shard_map/ppermute | solution.py:187
  35.9 8.0 %collective-permute-start.8 = (bf16[8,4,3584]{2,1,0:T(4,128)(2,1)S(1)}, bf16[8,4,3584]{2,1,0:T(4,128)(2,1)S(1)}, u32[]{:S(2)}, u32[]{:S(2)}) collective-permute-start(bf16[8,4,3584]{2,1,0:T(4,128)(2,1)S(1)} %shard_map.57), channel_id=1, source_target_pairs={{0,64},{64,128},{128,192},{192,256},{256,320},{320,384},{384,448},... | collective-permute-start | bytes 688136 | tf_op jit(solution)/shard_map/ppermute | solution.py:187
  38.9 8.0 %collective-permute-start.3 = (bf16[8,4,3584]{2,1,0:T(4,128)(2,1)S(1)}, bf16[8,4,3584]{2,1,0:T(4,128)(2,1)S(1)}, u32[]{:S(2)}, u32[]{:S(2)}) collective-permute-start(bf16[8,4,3584]{2,1,0:T(4,128)(2,1)S(1)} %shard_map.53), channel_id=1, source_target_pairs={{0,704},{64,0},{128,64},{192,128},{256,192},{320,256},{384,320},{4... | collective-permute-start | bytes 688136 | tf_op jit(solution)/shard_map/ppermute | solution.py:187
  43.9 8.2 %collective-permute-start.9 = (bf16[8,4,3584]{2,1,0:T(4,128)(2,1)S(1)}, bf16[8,4,3584]{2,1,0:T(4,128)(2,1)S(1)}, u32[]{:S(2)}, u32[]{:S(2)}) collective-permute-start(bf16[8,4,3584]{2,1,0:T(4,128)(2,1)S(1)} %shard_map.58), channel_id=1, source_target_pairs={{0,64},{64,128},{128,192},{192,256},{256,320},{320,384},{384,448},... | collective-permute-start | bytes 688136 | tf_op jit(solution)/shard_map/ppermute | solution.py:187
  46.9 13.3 %copy-start.3 = (s32[8,4,896]{2,1,0:T(4,128)S(1)}, s32[8,4,896]{2,1,0:T(4,128)}, u32[]{:S(2)}) copy-start(s32[8,4,896]{2,1,0:T(4,128)} %codes_ref) | copy-start | bytes 344068
  46.9 16.3 %copy-start.1 = (bf16[1,96,4,3584]{3,2,1,0:T(4,128)(2,1)S(1)}, bf16[1,96,4,3584]{3,2,1,0:T(4,128)(2,1)}, u32[]{:S(2)}) copy-start(bf16[1,96,4,3584]{3,2,1,0:T(4,128)(2,1)} %param.3) | copy-start | bytes 8257540
  46.9 16.3 %copy-start.2 = (f32[8,4,3584]{2,1,0:T(4,128)S(1)}, f32[8,4,3584]{2,1,0:T(4,128)}, u32[]{:S(2)}) copy-start(f32[8,4,3584]{2,1,0:T(4,128)} %momentum_ref.3) | copy-start | bytes 1376260
  46.9 8.2 %collective-permute-start.4 = (bf16[8,4,3584]{2,1,0:T(4,128)(2,1)S(1)}, bf16[8,4,3584]{2,1,0:T(4,128)(2,1)S(1)}, u32[]{:S(2)}, u32[]{:S(2)}) collective-permute-start(bf16[8,4,3584]{2,1,0:T(4,128)(2,1)S(1)} %shard_map.54), channel_id=1, source_target_pairs={{0,704},{64,0},{128,64},{192,128},{256,192},{320,256},{384,320},{4... | collective-permute-start | bytes 688136 | tf_op jit(solution)/shard_map/ppermute | solution.py:187
  52.3 8.3 %collective-permute-start.10 = (bf16[8,4,3584]{2,1,0:T(4,128)(2,1)S(1)}, bf16[8,4,3584]{2,1,0:T(4,128)(2,1)S(1)}, u32[]{:S(2)}, u32[]{:S(2)}) collective-permute-start(bf16[8,4,3584]{2,1,0:T(4,128)(2,1)S(1)} %shard_map.59), channel_id=1, source_target_pairs={{0,64},{64,128},{128,192},{192,256},{256,320},{320,384},{384,448},... | collective-permute-start | bytes 688136 | tf_op jit(solution)/shard_map/ppermute | solution.py:187
  55.2 8.0 %collective-permute-start.5 = (bf16[8,4,3584]{2,1,0:T(4,128)(2,1)S(1)}, bf16[8,4,3584]{2,1,0:T(4,128)(2,1)S(1)}, u32[]{:S(2)}, u32[]{:S(2)}) collective-permute-start(bf16[8,4,3584]{2,1,0:T(4,128)(2,1)S(1)} %shard_map.55), channel_id=1, source_target_pairs={{0,704},{64,0},{128,64},{192,128},{256,192},{320,256},{384,320},{4... | collective-permute-start | bytes 688136 | tf_op jit(solution)/shard_map/ppermute | solution.py:187
  90.3 14.8 %collective-permute-start.11 = (bf16[128,3584]{1,0:T(8,128)(2,1)S(1)}, bf16[128,3584]{1,0:T(8,128)(2,1)S(1)}, u32[]{:S(2)}, u32[]{:S(2)}) collective-permute-start(bf16[128,3584]{1,0:T(8,128)(2,1)S(1)} %all_gather.3.mine_ref), channel_id=1, source_target_pairs={{0,1},{1,0},{2,3},{3,2},{4,5},{5,4},{6,7},{7,6},{8,9},{9,8},{10,11... | collective-permute-start | bytes 2752520 | tf_op jit(solution)/shard_map/ppermute | solution.py:209
